TPU v7x, 32 devices: a whole 2x2x4 slice. The times are simulated.
32 devices in a mesh: fsdp: 16 (over z, y, core), tp: 2 (over x).
Axes of the slice: x: 2, y: 2, z: 4, core: 2. Of those that a mesh axis runs over, the one named last changes fastest.
Arguments:
- tokens: bfloat16 [2, 16, 1024, 768], P(None, 'fsdp', 'tp'), may hold values from -6 to 6
- cotangent: bfloat16 [2, 16, 1024, 768], P(None, 'fsdp', 'tp'), may hold values from -6 to 6
- routes: int32 [2, 16, 1024, 1], P(None, 'fsdp'), may hold values from 0 to 1; in each aligned block of 1024 rows (0 to 1023, 1024 to 2047, ..., all dimensions but the last counted through in order) at most 640 rows name the same one
- prefix: int32 [2, 16], P(None, 'fsdp'), may hold values from 0 to 1024
- attn_gain: float32 [768], P(('fsdp', 'tp')), may hold values from 0.25 to 1.75
- query_weight: bfloat16 [768, 768], P('fsdp', 'tp'), may hold values from -0.21875 to 0.21875
- key_weight: bfloat16 [768, 768], P('fsdp', 'tp'), may hold values from -0.21875 to 0.21875
- value_weight: bfloat16 [768, 768], P('fsdp', 'tp'), may hold values from -0.21875 to 0.21875
- out_weight_t: bfloat16 [768, 768], P('fsdp', 'tp'), may hold values from -1.75 to 1.75
- bias_table: float32 [12, 32], P('tp'), may hold values from -4 to 4
- ffn_gain: float32 [768], P(('fsdp', 'tp')), may hold values from 0.25 to 1.75
- router: float32 [768, 2], P(('fsdp', 'tp')), may hold values from -0.15625 to 0.15625
- inner_weight: bfloat16 [768, 2, 3072], P('fsdp', None, 'tp'), may hold values from -0.21875 to 0.21875
- down_weight_t: bfloat16 [768, 2, 3072], P('fsdp', None, 'tp'), may hold values from -0.625 to 0.625
Outputs:
- layer_out: bfloat16 [2, 16, 1024, 768], P(None, 'fsdp', 'tp')
- tokens_grad: float32 [2, 16, 1024, 768], P(None, 'fsdp', 'tp')
- attn_gain_grad: float32 [768], P(('fsdp', 'tp'))
- query_grad: float32 [768, 768], P('fsdp', 'tp')
- key_grad: float32 [768, 768], P('fsdp', 'tp')
- value_grad: float32 [768, 768], P('fsdp', 'tp')
- out_grad: float32 [768, 768], P('fsdp', 'tp')
- bias_table_grad: float32 [12, 32], P('tp')
- ffn_gain_grad: float32 [768], P(('fsdp', 'tp'))
- router_grad: float32 [768, 2], P(('fsdp', 'tp'))
- inner_grad: float32 [768, 2, 3072], P('fsdp', None, 'tp')
- down_grad: float32 [768, 2, 3072], P('fsdp', None, 'tp')
Inputs may be any that keep to these rules, and one draw needn't show every extreme that they name: `routes`: within each sequence no expert is named by more than 640 tokens, and in some sequences one expert is named by exactly 640.
All inputs are finite; a program needn't handle non-finite values.
Results may differ from a plain program's by a relative error of at most 0.017.
Values may be sent and summed in bfloat16 or wider, within the bound.
A program may use at most 320 MiB of HBM per device.

v0:
```python
import jax
import jax.numpy as jnp
from jax import lax
from jax.sharding import PartitionSpec as P

epsilon = 1e-06
masked_score = -1e30
highest = lax.Precision.HIGHEST
bucket_edges = (12, 16, 23, 32, 46, 64, 91)


def rms_scale(values, gain_vector):
    return (
        values
        * lax.rsqrt(jnp.mean(values * values, axis=-1, keepdims=True) + epsilon)
        * gain_vector
    )


def gelu_exact(values):
    return jax.nn.gelu(values, approximate=False)


def bucket_of(offset):
    distance = jnp.abs(offset)
    far_bucket = jnp.full_like(distance, 8)
    for edge_value in bucket_edges:
        far_bucket = far_bucket + (distance >= edge_value).astype(jnp.int32)
    near_bucket = jnp.where(distance < 8, distance, far_bucket)
    return near_bucket + 16 * (offset > 0).astype(jnp.int32)


def contract_rows(left_side, right_side):
    return lax.dot_general(
        left_side, right_side, (((0,), (0,)), ((), ())), preferred_element_type=jnp.float32
    )


def contract_cols(left_side, right_side):
    return lax.dot_general(
        left_side, right_side, (((1,), (1,)), ((), ())), preferred_element_type=jnp.float32
    )


def block_scores(query_block, keys_all, reduced_bias_table, first_row, prefix_len):
    block_len = query_block.shape[0]
    key_len = keys_all.shape[0]
    head_dim = keys_all.shape[2]
    query_pos = first_row + jnp.arange(block_len, dtype=jnp.int32)
    key_pos = jnp.arange(key_len, dtype=jnp.int32)
    offset = key_pos[None, :] - query_pos[:, None]
    bucket_ids = jnp.arange(reduced_bias_table.shape[1], dtype=jnp.int32)
    expert_picker = (bucket_of(offset)[None] == bucket_ids[:, None, None]).astype(jnp.bfloat16)
    raw_scores = jnp.einsum(
        "qhd,khd->hqk", query_block, keys_all, preferred_element_type=jnp.float32
    ) * head_dim ** (-0.5)
    scores = raw_scores + jnp.einsum(
        "cf,flg->clg", reduced_bias_table, expert_picker, preferred_element_type=jnp.float32
    )
    visible = (key_pos[None, :] < prefix_len) | (offset <= 0)
    return (jnp.where(visible[None], scores, masked_score), expert_picker)


def body(
    tokens,
    cotangent,
    routes,
    prefix,
    attn_gain,
    query_weight,
    key_weight,
    value_weight,
    out_weight_t,
    bias_table,
    ffn_gain,
    router,
    inner_weight,
    down_weight_t,
):
    micro_count = tokens.shape[0]
    seq_len = routes.shape[2]
    heads_here = bias_table.shape[0]
    head_dim = query_weight.shape[1] // heads_here
    expert_count = router.shape[1]
    capacity = seq_len * 5 // (4 * expert_count)
    block_rows = min(512, seq_len)
    block_count = seq_len // block_rows
    head_scale = head_dim ** (-0.5)
    reduced_bias_table = bias_table.astype(jnp.bfloat16)
    block_starts = jnp.arange(block_count, dtype=jnp.int32) * block_rows
    expert_ids = jnp.arange(expert_count, dtype=jnp.int32)
    weight_acc = None
    small_acc = None
    table_acc = jnp.zeros(bias_table.shape, jnp.float32)
    layer_outs = []
    input_grads = []
    for micro_idx in range(micro_count):
        matrices = (
            lax.all_gather(query_weight, "fsdp", axis=0, tiled=True),
            lax.all_gather(key_weight, "fsdp", axis=0, tiled=True),
            lax.all_gather(value_weight, "fsdp", axis=0, tiled=True),
            lax.all_gather(out_weight_t, "fsdp", axis=0, tiled=True),
            lax.all_gather(inner_weight, "fsdp", axis=0, tiled=True),
            lax.all_gather(down_weight_t, "fsdp", axis=0, tiled=True),
        )
        vectors = (
            lax.all_gather(attn_gain, ("fsdp", "tp"), axis=0, tiled=True),
            lax.all_gather(ffn_gain, ("fsdp", "tp"), axis=0, tiled=True),
            lax.all_gather(router, ("fsdp", "tp"), axis=0, tiled=True),
        )
        fetched = (matrices, vectors)
        matrices, vectors = fetched
        query_all, key_all, value_rows_gathered, out_all, inner_all, down_all = matrices
        gain_one, gain_two, router_all = vectors
        prefix_len = prefix[micro_idx, 0]
        route_ids = routes[micro_idx, 0, :, 0]
        tokens_now = tokens[micro_idx, 0].astype(jnp.float32)
        cotangent_now = cotangent[micro_idx, 0]
        normed_one = rms_scale(tokens_now, gain_one).astype(jnp.bfloat16)
        normed_all = lax.all_gather(normed_one, "tp", axis=0, tiled=True)
        queries = jnp.dot(normed_all, query_all, preferred_element_type=jnp.float32).astype(
            jnp.bfloat16
        )
        queries = queries.reshape(seq_len, heads_here, head_dim)
        keys_all = jnp.dot(normed_all, key_all, preferred_element_type=jnp.float32).astype(
            jnp.bfloat16
        )
        keys_all = keys_all.reshape(seq_len, heads_here, head_dim)
        values_all = jnp.dot(
            normed_all, value_rows_gathered, preferred_element_type=jnp.float32
        ).astype(jnp.bfloat16)
        values_all = values_all.reshape(seq_len, heads_here, head_dim)

        def forward_block(first_row):
            query_block = lax.dynamic_slice_in_dim(queries, first_row, block_rows, 0)
            masked = block_scores(query_block, keys_all, reduced_bias_table, first_row, prefix_len)[
                0
            ]
            top_score = jnp.max(masked, axis=-1, keepdims=True)
            exponent = jnp.exp(masked - top_score)
            row_total = jnp.sum(exponent, axis=-1, keepdims=True)
            weights_low = (exponent / row_total).astype(jnp.bfloat16)
            mixed_block = jnp.einsum(
                "hqk,khd->qhd", weights_low, values_all, preferred_element_type=jnp.float32
            )
            return (mixed_block.astype(jnp.bfloat16), (top_score + jnp.log(row_total))[..., 0])

        mixed_blocks, log_totals = lax.map(forward_block, block_starts)
        mixed_heads = mixed_blocks.reshape(seq_len, heads_here * head_dim)
        attended = lax.psum_scatter(
            contract_cols(mixed_heads, out_all), "tp", scatter_dimension=0, tiled=True
        )
        residual = tokens_now + attended
        normed_two = rms_scale(residual, gain_two).astype(jnp.bfloat16)
        normed_two_all = lax.all_gather(normed_two, "tp", axis=0, tiled=True)
        chosen = route_ids[:, None] == expert_ids[None, :]
        chosen_int = chosen.astype(jnp.int32)
        rank_in = jnp.sum((jnp.cumsum(chosen_int, axis=0) - 1) * chosen_int, axis=1)
        slot_ids = route_ids * capacity + rank_in
        normed_wide = normed_two_all.astype(jnp.float32)
        router_prob = jax.nn.softmax(
            jnp.dot(normed_wide, router_all, precision=highest, preferred_element_type=jnp.float32),
            axis=-1,
        )
        gate_value = jnp.sum(jnp.where(chosen, router_prob, 0.0), axis=1)
        buffer_in = jnp.zeros((expert_count * capacity, normed_two_all.shape[1]), jnp.bfloat16)
        buffer_in = buffer_in.at[slot_ids].set(normed_two_all).reshape(expert_count, capacity, -1)
        inner_act = jnp.einsum(
            "ecd,def->ecf", buffer_in, inner_all, preferred_element_type=jnp.float32
        )
        activated = gelu_exact(inner_act).astype(jnp.bfloat16)
        expert_out = jnp.einsum(
            "ecf,def->ecd", activated, down_all, preferred_element_type=jnp.float32
        )
        token_out = jnp.take(expert_out.reshape(expert_count * capacity, -1), slot_ids, axis=0)
        branch_sum = lax.psum_scatter(
            (gate_value[:, None] * token_out).astype(jnp.bfloat16),
            "tp",
            scatter_dimension=0,
            tiled=True,
        ).astype(jnp.float32)
        layer_outs.append((residual + branch_sum).astype(jnp.bfloat16))
        grad_rows_all = lax.all_gather(cotangent_now, "tp", axis=0, tiled=True)
        grad_rows_wide = grad_rows_all.astype(jnp.float32)
        grad_gate = jnp.sum(grad_rows_wide * token_out, axis=1)
        grad_token = (gate_value[:, None] * grad_rows_wide).astype(jnp.bfloat16)
        grad_slots = jnp.zeros((expert_count * capacity, grad_token.shape[1]), jnp.bfloat16)
        grad_slots = grad_slots.at[slot_ids].set(grad_token).reshape(expert_count, capacity, -1)
        down_grad = jnp.einsum(
            "ecd,ecf->def", grad_slots, activated, preferred_element_type=jnp.float32
        )
        grad_hidden = jnp.einsum(
            "ecd,def->ecf", grad_slots, down_all, preferred_element_type=jnp.float32
        )
        grad_inner = jax.vjp(gelu_exact, inner_act)[1](grad_hidden)[0].astype(jnp.bfloat16)
        inner_grad = jnp.einsum(
            "ecd,ecf->def", buffer_in, grad_inner, preferred_element_type=jnp.float32
        )
        grad_buffer = jnp.einsum(
            "ecf,def->ecd", grad_inner, inner_all, preferred_element_type=jnp.float32
        )
        grad_logit = (
            router_prob * (chosen.astype(jnp.float32) - gate_value[:, None]) * grad_gate[:, None]
        )
        router_part = lax.dot_general(
            normed_wide,
            grad_logit,
            (((0,), (0,)), ((), ())),
            precision=highest,
            preferred_element_type=jnp.float32,
        )
        grad_two_part = jnp.take(grad_buffer.reshape(expert_count * capacity, -1), slot_ids, axis=0)
        grad_two_part = grad_two_part + lax.dot_general(
            grad_logit,
            router_all,
            (((1,), (1,)), ((), ())),
            precision=highest,
            preferred_element_type=jnp.float32,
        )
        grad_two = lax.psum_scatter(grad_two_part, "tp", scatter_dimension=0, tiled=True)
        second_pull = jax.vjp(rms_scale, residual, gain_two)[1]
        grad_resid_norm, gain_two_part = second_pull(grad_two)
        grad_residual = cotangent_now.astype(jnp.float32) + grad_resid_norm
        grad_attended = grad_residual.astype(jnp.bfloat16)
        grad_attn_all = lax.all_gather(grad_attended, "tp", axis=0, tiled=True)
        out_part = contract_rows(grad_attn_all, mixed_heads)
        grad_mixed = jnp.dot(grad_attn_all, out_all, preferred_element_type=jnp.float32).astype(
            jnp.bfloat16
        )
        grad_mixed = grad_mixed.reshape(block_count, block_rows, heads_here, head_dim)

        def backward_block(carried, inputs):
            key_acc, value_acc, table_part = carried
            first_row, log_block, grad_block = inputs
            query_block = lax.dynamic_slice_in_dim(queries, first_row, block_rows, 0)
            masked, expert_picker = block_scores(
                query_block, keys_all, reduced_bias_table, first_row, prefix_len
            )
            probs_block = jnp.exp(masked - log_block[..., None])
            value_acc = value_acc + jnp.einsum(
                "hqk,qhd->khd",
                probs_block.astype(jnp.bfloat16),
                grad_block,
                preferred_element_type=jnp.float32,
            )
            grad_probs = jnp.einsum(
                "qhd,khd->hqk", grad_block, values_all, preferred_element_type=jnp.float32
            )
            score_gradients = probs_block * (
                grad_probs - jnp.sum(probs_block * grad_probs, axis=-1, keepdims=True)
            )
            score_gradients = score_gradients.astype(jnp.bfloat16)
            table_part = table_part + jnp.einsum(
                "toi,roi->tr", score_gradients, expert_picker, preferred_element_type=jnp.float32
            )
            grad_qblock = (
                jnp.einsum(
                    "hqk,khd->qhd", score_gradients, keys_all, preferred_element_type=jnp.float32
                )
                * head_scale
            )
            key_acc = (
                key_acc
                + jnp.einsum(
                    "hqk,qhd->khd", score_gradients, query_block, preferred_element_type=jnp.float32
                )
                * head_scale
            )
            return ((key_acc, value_acc, table_part), grad_qblock.astype(jnp.bfloat16))

        start_carry = (
            jnp.zeros((seq_len, heads_here, head_dim), jnp.float32),
            jnp.zeros((seq_len, heads_here, head_dim), jnp.float32),
            jnp.zeros(bias_table.shape, jnp.float32),
        )
        (key_sum, value_sum, table_part_sum), query_block_gradients = lax.scan(
            backward_block, start_carry, (block_starts, log_totals, grad_mixed)
        )
        grad_query = query_block_gradients.reshape(seq_len, heads_here * head_dim)
        grad_key = key_sum.astype(jnp.bfloat16).reshape(seq_len, heads_here * head_dim)
        grad_value = value_sum.astype(jnp.bfloat16).reshape(seq_len, heads_here * head_dim)
        query_part = contract_rows(normed_all, grad_query)
        key_part = contract_rows(normed_all, grad_key)
        value_part = contract_rows(normed_all, grad_value)
        term_sum = contract_cols(grad_query, query_all)
        term_sum = term_sum + contract_cols(grad_key, key_all)
        grad_normed = lax.psum_scatter(
            (term_sum + contract_cols(grad_value, value_rows_gathered)).astype(jnp.bfloat16),
            "tp",
            scatter_dimension=0,
            tiled=True,
        ).astype(jnp.float32)
        first_pull = jax.vjp(rms_scale, tokens_now, gain_one)[1]
        grad_tokens_norm, gain_one_part = first_pull(grad_normed)
        input_grads.append(grad_residual + grad_tokens_norm)
        new_weights = (query_part, key_part, value_part, out_part, inner_grad, down_grad)
        weight_acc = (
            new_weights if weight_acc is None else jax.tree.map(jnp.add, weight_acc, new_weights)
        )
        new_small = (gain_one_part, gain_two_part, router_part)
        small_acc = new_small if small_acc is None else jax.tree.map(jnp.add, small_acc, new_small)
        table_acc = table_acc + table_part_sum
    weight_acc = lax.psum_scatter(weight_acc, "fsdp", scatter_dimension=0, tiled=True)
    small_sums = lax.psum_scatter(small_acc, ("fsdp", "tp"), scatter_dimension=0, tiled=True)
    table_total = lax.psum(table_acc, "fsdp")
    layer_out = jnp.stack(layer_outs)[:, None]
    tokens_grad = jnp.stack(input_grads)[:, None]
    return (
        layer_out,
        tokens_grad,
        small_sums[0],
        weight_acc[0],
        weight_acc[1],
        weight_acc[2],
        weight_acc[3],
        table_total,
        small_sums[1],
        small_sums[2],
        weight_acc[4],
        weight_acc[5],
    )


def solution(mesh):
    in_specs = (
        P(None, "fsdp", "tp", None),
        P(None, "fsdp", "tp", None),
        P(None, "fsdp", None, None),
        P(None, "fsdp"),
        P(("fsdp", "tp")),
        P("fsdp", "tp"),
        P("fsdp", "tp"),
        P("fsdp", "tp"),
        P("fsdp", "tp"),
        P("tp", None),
        P(("fsdp", "tp")),
        P(("fsdp", "tp"), None),
        P("fsdp", None, "tp"),
        P("fsdp", None, "tp"),
    )
    out_specs = (
        P(None, "fsdp", "tp", None),
        P(None, "fsdp", "tp", None),
        P(("fsdp", "tp")),
        P("fsdp", "tp"),
        P("fsdp", "tp"),
        P("fsdp", "tp"),
        P("fsdp", "tp"),
        P("tp", None),
        P(("fsdp", "tp")),
        P(("fsdp", "tp"), None),
        P("fsdp", None, "tp"),
        P("fsdp", None, "tp"),
    )
    return jax.shard_map(body, mesh=mesh, in_specs=in_specs, out_specs=out_specs, check_vma=False)
```

profile of v0, /device:TPU:0, one launch (start us, length us, event | category | flops | bytes accessed | tf_op | source)
XLA Modules:
  0.0 1740.5 jit_solution(12325525859442130922)
XLA Ops:
  10.8 42.1 %all-reduce.8 = (f32[768]{0:T(1024)S(1)}, f32[768]{0:T(1024)}) all-reduce(f32[768]{0:T(1024)S(1)} %dynamic-update-slice, f32[768]{0:T(1024)S(1)} %dynamic-update-slice.1), channel_id=1, replica_groups=mesh['fsdp'=16,'tp'=2] {'fsdp','tp'}, use_global_device_ids=true, to_apply=%add | all-reduce | flops 1536 | bytes 12288
  56.7 23.0 %all_gather.62 = bf16[768,384]{1,0:T(8,128)(2,1)S(1)} all-gather(bf16[48,384]{1,0:T(8,128)(2,1)S(1)} %copy-done.111), channel_id=1, replica_groups=mesh['fsdp'=16,'tp'=2] {'fsdp'}, dimensions={0}, use_global_device_ids=true | all-gather | bytes 626688 | tf_op jit(solution)/shard_map/all_gather | solution.py:99
  79.8 19.0 %all_gather.63 = bf16[768,384]{1,0:T(8,128)(2,1)S(1)} all-gather(bf16[48,384]{1,0:T(8,128)(2,1)S(1)} %copy-done.112), channel_id=1, replica_groups=mesh['fsdp'=16,'tp'=2] {'fsdp'}, dimensions={0}, use_global_device_ids=true | all-gather | bytes 626688 | tf_op jit(solution)/shard_map/all_gather | solution.py:100
  98.8 20.4 %all_gather.64 = bf16[768,384]{1,0:T(8,128)(2,1)S(1)} all-gather(bf16[48,384]{1,0:T(8,128)(2,1)S(1)} %copy-done.113), channel_id=1, replica_groups=mesh['fsdp'=16,'tp'=2] {'fsdp'}, dimensions={0}, use_global_device_ids=true | all-gather | bytes 626688 | tf_op jit(solution)/shard_map/all_gather | solution.py:101
  119.9 20.5 %all_gather.65 = bf16[768,384]{1,0:T(8,128)(2,1)} all-gather(bf16[48,384]{1,0:T(8,128)(2,1)S(1)} %copy-done.114), channel_id=1, replica_groups=mesh['fsdp'=16,'tp'=2] {'fsdp'}, dimensions={0}, use_global_device_ids=true | all-gather | bytes 626688 | tf_op jit(solution)/shard_map/all_gather | solution.py:102
  146.0 96.3 %while.59 = (s32[]{:T(128)}, bf16[2,512,6,64]{1,3,2,0:T(8,128)(2,1)}, f32[2,6,512]{2,1,0:T(8,128)}, s32[]{:T(128)}, s32[2]{0:T(128)S(1)}, /*index=5*/bf16[1024,6...) while((s32[]{:T(128)}, ...), condition=%wide.region_19.21_spmd, body=%wide.region_16.20_spmd.sunk | while | flops 1068169728 | bytes 70628904 | solution.py:148
  151.7 12.6 fusion.385
  165.4 15.4 fusion.387
  193.6 12.6 fusion.385
  207.3 15.4 fusion.387
  253.0 81.9 %while.58 = (s32[]{:T(128)}, bf16[2,512,6,64]{1,3,2,0:T(8,128)(2,1)S(1)}, f32[2,6,512]{2,1,0:T(8,128)S(1)}, s32[]{:T(128)}, s32[2]{0:T(128)S(1)}, /*index=5*/bf1...) while((s32[]{:T(128)}, ...), condition=%wide.region_4.5_spmd, body=%wide.region_1.4_spmd.sunk | while | flops 1068169728 | bytes 70644280 | solution.py:148
  258.4 12.7 fusion.376
  272.2 15.4 fusion.378
  299.2 12.7 fusion.376
  313.0 15.3 fusion.378
  339.7 41.0 %reduce-scatter.14.cloned.1.call-done = f32[512,768]{1,0:T(8,128)} async-done(((f32[1024,768]{1,0:T(8,128)}), f32[512,768]{1,0:T(8,128)}) %reduce-scatter.14.cloned.1.call-update) | async-done | bytes 1572880 | tf_op jit(solution)/shard_map/reduce_scatter | solution.py:150
  390.1 67.1 %all-gather.2 = f32[32,24,2]{1,2,0:T(2,128)S(1)} all-gather(f32[1,24,2]{1,2,0:T(2,128)S(1)} %bitcast.508), channel_id=1, replica_groups=mesh['fsdp'=16,'tp'=2] {'fsdp','tp'}, dimensions={0}, use_global_device_ids=true | all-gather | bytes 6336 | tf_op jit(solution)/shard_map/all_gather | solution.py:109
  479.8 18.3 %all-gather.18.cloned.1.call-done = bf16[768,2,1536]{2,0,1:T(8,128)(2,1)} async-done(((bf16[48,2,1536]{2,0,1:T(8,128)(2,1)}), bf16[768,2,1536]{2,0,1:T(8,128)(2,1)}) %all-gather.18.cloned.1.call-update) | async-done | bytes 4718608 | tf_op jit(solution)/shard_map/all_gather | solution.py:103
  498.2 11.2 fusion.144
  509.3 43.1 %all-gather.20.cloned.1.call-done = bf16[768,2,1536]{2,0,1:T(8,128)(2,1)} async-done(((bf16[48,2,1536]{2,0,1:T(8,128)(2,1)}), bf16[768,2,1536]{2,0,1:T(8,128)(2,1)}) %all-gather.20.cloned.1.call-update) | async-done | bytes 4718608 | tf_op jit(solution)/shard_map/all_gather | solution.py:104
  552.4 25.6 %add_convert_fusion.1 = (bf16[2,640,1536]{2,1,0:T(8,128)(2,1)}, f32[2,640,1536]{2,1,0:T(8,128)}) fusion(f32[2,640,1536]{2,1,0:T(8,128)} %get-tuple-element.614, u8[640,1536]{1,0:T(8,128)(4,1)} %get-tuple-element.460, u8[640,1536]{1,0:T(8,128)(4,1)} %get-tuple-element.459, bf16[2,640,768]{2,1,0:T(8,128)(2,1)} %bitcast.484, ...), kind=kOutput, calls=%fused_computation.188 | convolution fusion | flops 3171287040 | bytes 28311552 | tf_op jit(solution)/shard_map/ecd,def->ecf/dot_general | solution.py:192
  585.5 8.9 fusion.209
  602.6 8.7 fusion.212
  628.3 41.4 %reduce-scatter.22.cloned.1.call-done = f32[512,768]{1,0:T(8,128)} async-done(((f32[1024,768]{1,0:T(8,128)}), f32[512,768]{1,0:T(8,128)}) %reduce-scatter.22.cloned.1.call-update) | async-done | bytes 1572880 | tf_op jit(solution)/shard_map/reduce_scatter | solution.py:220
  674.0 26.6 %all-gather.24.cloned.1.call-done = bf16[1024,768]{1,0:T(8,128)(2,1)} async-done(((bf16[512,768]{1,0:T(8,128)(2,1)}), bf16[1024,768]{1,0:T(8,128)(2,1)}) %all-gather.24.cloned.1.call-update) | async-done | bytes 1572880 | tf_op jit(solution)/shard_map/all_gather | solution.py:155
  711.2 12.5 fusion.145
  737.2 25.6 %add_convert_fusion = (bf16[2,640,1536]{2,1,0:T(8,128)(2,1)}, f32[2,640,1536]{2,1,0:T(8,128)}) fusion(f32[2,640,1536]{2,1,0:T(8,128)} %get-tuple-element.617, u8[640,1536]{1,0:T(8,128)(4,1)} %get-tuple-element.462, u8[640,1536]{1,0:T(8,128)(4,1)} %get-tuple-element.461, bf16[2,640,768]{2,1,0:T(8,128)(2,1)} %bitcast.460, ...), kind=kOutput, calls=%fused_computation.187 | convolution fusion | flops 3171287040 | bytes 28311552 | tf_op jit(solution)/shard_map/ecd,def->ecf/dot_general | solution.py:192
  770.2 8.9 fusion.211
  787.1 8.7 fusion.215
  813.7 42.7 %reduce-scatter.26.cloned.1.call-done = f32[512,768]{1,0:T(8,128)} async-done(((f32[1024,768]{1,0:T(8,128)}), f32[512,768]{1,0:T(8,128)}) %reduce-scatter.26.cloned.1.call-update) | async-done | bytes 1572880 | tf_op jit(solution)/shard_map/reduce_scatter | solution.py:220
  858.8 25.9 %reduce-scatter.20.cloned.1.call-done = bf16[512,768]{1,0:T(8,128)(2,1)} async-done(((bf16[1024,768]{1,0:T(8,128)(2,1)}), bf16[512,768]{1,0:T(8,128)(2,1)}) %reduce-scatter.20.cloned.1.call-update) | async-done | bytes 786448 | tf_op jit(solution)/shard_map/reduce_scatter | solution.py:176
  888.9 10.4 fusion.223
  905.8 12.1 add_bitcast_fusion
  917.9 15.3 copy.101
  933.2 12.2 add_bitcast_fusion.1
  945.4 14.9 copy.98
  972.3 222.8 %while.61 = (s32[]{:T(128)}, f32[1024,6,64]{0,2,1:T(8,128)}, f32[1024,6,64]{0,2,1:T(8,128)}, f32[6,32]{1,0:T(8,128)S(1)}, bf16[2,512,6,64]{1,3,2,0:T(8,128)(2,1)...) while((s32[]{:T(128)}, f32[1024,6,64]{0,2,1:T(8,128)}, ...), condition=%wide.region_45.47_spmd.clone, body=%wide.region_43.46_spmd.clone.sunk | while | flops 2499542016 | bytes 329456640 | solution.py:276
  981.2 12.6 fusion.420
  993.8 15.7 copy.130
  1019.8 12.7 multiply_reduce_fusion.11
  1045.5 12.4 copy.131
  1057.9 16.1 fusion.422
  1092.0 12.6 fusion.420
  1104.6 15.7 copy.130
  1130.6 12.5 multiply_reduce_fusion.11
  1156.0 12.2 copy.131
  1168.2 16.7 fusion.422
  1203.9 220.2 %while.60 = (s32[]{:T(128)}, f32[1024,6,64]{0,2,1:T(8,128)}, f32[1024,6,64]{0,2,1:T(8,128)}, f32[6,32]{1,0:T(8,128)S(1)}, bf16[2,512,6,64]{1,3,2,0:T(8,128)(2,1)...) while((s32[]{:T(128)}, f32[1024,6,64]{0,2,1:T(8,128)}, ...), condition=%wide.region_36.38_spmd.clone, body=%wide.region_34.37_spmd.clone.sunk | while | flops 2499542016 | bytes 329456640 | solution.py:276
  1216.3 12.7 fusion.403
  1229.0 15.9 copy.127
  1254.2 11.7 multiply_reduce_fusion.10
  1270.5 8.4 multiply_convert_fusion.10
  1278.9 12.2 copy.128
  1291.1 16.1 fusion.405
  1323.9 12.7 fusion.403
  1336.6 15.6 copy.127
  1361.5 11.4 multiply_reduce_fusion.10
  1385.8 12.2 copy.128
  1398.0 16.1 fusion.405
  1452.7 33.7 %psum.7 = f32[6,32]{1,0:T(8,128)} all-reduce(f32[6,32]{1,0:T(8,128)S(1)} %add.565), channel_id=1, replica_groups=mesh['fsdp'=16,'tp'=2] {'fsdp'}, use_global_device_ids=true, to_apply=%region_55.57 | all-reduce | flops 192 | bytes 1536 | tf_op jit(solution)/shard_map/psum | solution.py:305
  1496.5 37.2 %all-reduce.7 = (f32[768]{0:T(1024)S(1)}, f32[768]{0:T(1024)S(1)}, f32[768,2]{0,1:T(2,128)S(1)}) all-reduce(f32[768]{0:T(1024)S(1)} %add.560, f32[768]{0:T(1024)S(1)} %add.566, f32[768,2]{0,1:T(2,128)S(1)} %convolution_add_fusion.4), channel_id=12, replica_groups=mesh['fsdp'=16,'tp'=2] {'fsdp','tp'}, use_global_device_ids=true, to_apply=%region_50.52.clone | all-reduce | flops 3072 | bytes 24576
  1548.6 61.8 %reduce-scatter.34.cloned.1.call-done = f32[48,384]{1,0:T(8,128)} async-done(((f32[768,384]{1,0:T(8,128)}), f32[48,384]{1,0:T(8,128)}) %reduce-scatter.34.cloned.1.call-update) | async-done | bytes 73744 | tf_op jit(solution)/shard_map/reduce_scatter | solution.py:303
  1610.4 61.8 %reduce-scatter.32.cloned.1.call-done = f32[48,384]{1,0:T(8,128)} async-done(((f32[768,384]{1,0:T(8,128)}), f32[48,384]{1,0:T(8,128)}) %reduce-scatter.32.cloned.1.call-update) | async-done | bytes 73744 | tf_op jit(solution)/shard_map/reduce_scatter | solution.py:303
  1672.1 61.7 %reduce-scatter.30.cloned.1.call-done = f32[48,384]{1,0:T(8,128)} async-done(((f32[768,384]{1,0:T(8,128)}), f32[48,384]{1,0:T(8,128)}) %reduce-scatter.30.cloned.1.call-update) | async-done | bytes 73744 | tf_op jit(solution)/shard_map/reduce_scatter | solution.py:303
  (656 shorter events, 431.1 us)
Async XLA Ops:
  7.2 133.2 %all-gather.22.cloned.1.call-start = ((), (), s32[]{:S(2)}) async-start(), calls=%async_computation.18 | async-start | bytes 2359296 | tf_op jit(solution)/shard_map/all_gather | solution.py:120
  7.2 49.5 %copy-start.111 = (bf16[48,384]{1,0:T(8,128)(2,1)S(1)}, bf16[48,384]{1,0:T(8,128)(2,1)}, u32[]{:S(2)}) copy-start(bf16[48,384]{1,0:T(8,128)(2,1)} %param.29) | copy-start | bytes 110596
  7.2 72.5 %copy-start.112 = (bf16[48,384]{1,0:T(8,128)(2,1)S(1)}, bf16[48,384]{1,0:T(8,128)(2,1)}, u32[]{:S(2)}) copy-start(bf16[48,384]{1,0:T(8,128)(2,1)} %param.30) | copy-start | bytes 110596
  9.0 47.7 %copy-start.130 = (f32[512]{0:T(512)}, f32[512]{0:T(512)S(1)}, u32[]{:S(2)}) copy-start(f32[512]{0:T(512)S(1)} %get-tuple-element.473) | copy-start | bytes 6148
  9.0 47.7 %copy-start.132 = (f32[512]{0:T(512)}, f32[512]{0:T(512)S(1)}, u32[]{:S(2)}) copy-start(f32[512]{0:T(512)S(1)} %get-tuple-element.474) | copy-start | bytes 6148
  9.0 89.8 %copy-start.113 = (bf16[48,384]{1,0:T(8,128)(2,1)S(1)}, bf16[48,384]{1,0:T(8,128)(2,1)}, u32[]{:S(2)}) copy-start(bf16[48,384]{1,0:T(8,128)(2,1)} %param.31) | copy-start | bytes 110596
  9.1 47.6 %copy-start.123 = (f32[512]{0:T(512)}, f32[512]{0:T(512)S(1)}, u32[]{:S(2)}) copy-start(f32[512]{0:T(512)S(1)} %fusion.190) | copy-start | bytes 6148
  9.1 47.6 %copy-start.120 = (f32[512]{0:T(512)}, f32[512]{0:T(512)S(1)}, u32[]{:S(2)}) copy-start(f32[512]{0:T(512)S(1)} %fusion.192) | copy-start | bytes 6148
  52.9 66.3 %copy-start.142 = (f32[6,32]{1,0:T(8,128)S(1)}, f32[6,32]{1,0:T(8,128)}, u32[]{:S(2)}) copy-start(f32[6,32]{1,0:T(8,128)} %param.33) | copy-start | bytes 2308
  52.9 66.3 %copy-start.143 = (s32[2,1]{0,1:T(1,128)S(1)}, s32[2,1]{0,1:T(1,128)}, u32[]{:S(2)}) copy-start(s32[2,1]{0,1:T(1,128)} %param.27) | copy-start | bytes 28
  52.9 67.1 %copy-start.114 = (bf16[48,384]{1,0:T(8,128)(2,1)S(1)}, bf16[48,384]{1,0:T(8,128)(2,1)}, u32[]{:S(2)}) copy-start(bf16[48,384]{1,0:T(8,128)(2,1)} %param.32) | copy-start | bytes 110596
  55.9 192.9 %all-gather.14.cloned.1.call-start = ((), (), s32[]{:S(2)}) async-start(), calls=%async_computation.12 | async-start | bytes 2359296 | tf_op jit(solution)/shard_map/all_gather | solution.py:120
  56.6 283.1 %reduce-scatter.18.cloned.1.call-start = ((), (), s32[]{:S(2)}) async-start(), calls=%async_computation.19 | async-start | bytes 4718592 | tf_op jit(solution)/shard_map/reduce_scatter | solution.py:150
  79.8 60.7 %copy-start.57 = (bf16[768,384]{1,0:T(8,128)(2,1)}, bf16[768,384]{1,0:T(8,128)(2,1)S(1)}, u32[]{:S(2)}) copy-start(bf16[768,384]{1,0:T(8,128)(2,1)S(1)} %all_gather.62) | copy-start | bytes 1769476
  98.8 44.0 %copy-start.53 = (bf16[768,384]{1,0:T(8,128)(2,1)}, bf16[768,384]{1,0:T(8,128)(2,1)S(1)}, u32[]{:S(2)}) copy-start(bf16[768,384]{1,0:T(8,128)(2,1)S(1)} %all_gather.63) | copy-start | bytes 1769476
  119.2 24.4 %copy-start.49 = (bf16[768,384]{1,0:T(8,128)(2,1)}, bf16[768,384]{1,0:T(8,128)(2,1)S(1)}, u32[]{:S(2)}) copy-start(bf16[768,384]{1,0:T(8,128)(2,1)S(1)} %all_gather.64) | copy-start | bytes 1769476
  248.7 132.0 %reduce-scatter.14.cloned.1.call-start = ((), (), s32[]{:S(2)}) async-start(), calls=%async_computation.13 | async-start | bytes 4718592 | tf_op jit(solution)/shard_map/reduce_scatter | solution.py:150
  336.9 43.9 %copy-start.16 = (bf16[2,1,512,768]{3,2,1,0:T(8,128)(2,1)S(1)}, bf16[2,1,512,768]{3,2,1,0:T(8,128)(2,1)}, u32[]{:S(2)}) copy-start(bf16[2,1,512,768]{3,2,1,0:T(8,128)(2,1)} %param.24) | copy-start | bytes 4718596
  339.6 45.2 %copy-start.91 = (f32[768]{0:T(1024)S(1)}, f32[768]{0:T(1024)}, u32[]{:S(2)}) copy-start(f32[768]{0:T(1024)} %get-tuple-element.567) | copy-start | bytes 9220
  339.6 121.7 %all-gather.16.cloned.1.call-start = ((), (), s32[]{:S(2)}) async-start(), calls=%async_computation.14 | async-start | bytes 2359296 | tf_op jit(solution)/shard_map/all_gather | solution.py:155
  383.7 501.0 %copy-start.18 = (f32[512,768]{1,0:T(8,128)}, f32[512,768]{1,0:T(8,128)S(1)}, u32[]{:S(2)}) copy-start(f32[512,768]{1,0:T(8,128)S(1)} %get-tuple-element.604) | copy-start | bytes 4718596
  385.9 71.4 %copy-start.122 = (s32[2,1,1024,1]{2,3,1,0:T(1,128)S(1)}, s32[2,1,1024,1]{2,3,1,0:T(1,128)}, u32[]{:S(2)}) copy-start(s32[2,1,1024,1]{2,3,1,0:T(1,128)} %param.26) | copy-start | bytes 24580
  385.9 86.5 %all-gather.30.cloned.1.call-start = ((), (), s32[]{:S(2)}) async-start(), calls=%async_computation.32 | async-start | bytes 2359296 | tf_op jit(solution)/shard_map/all_gather | solution.py:183
  387.5 110.7 %all-gather.18.cloned.1.call-start = ((), (), s32[]{:S(2)}) async-start(), calls=%async_computation.15 | async-start | bytes 5013504 | tf_op jit(solution)/shard_map/all_gather | solution.py:103
  388.3 164.1 %all-gather.20.cloned.1.call-start = ((), (), s32[]{:S(2)}) async-start(), calls=%async_computation.16 | async-start | bytes 5013504 | tf_op jit(solution)/shard_map/all_gather | solution.py:104
  390.1 279.7 %reduce-scatter.22.cloned.1.call-start = ((), (), s32[]{:S(2)}) async-start(), calls=%async_computation.22 | async-start | bytes 4718592 | tf_op jit(solution)/shard_map/reduce_scatter | solution.py:220
  457.3 165.5 %copy-start.89 = (s32[1,1,1024,1]{2,3,1,0:T(1,128)}, s32[1,1,1024,1]{2,3,1,0:T(1,128)S(1)}, u32[]{:S(2)}) copy-start(s32[1,1,1024,1]{2,3,1,0:T(1,128)S(1)} %get-tuple-element.607) | copy-start | bytes 12292
  457.3 350.6 %copy-start.87 = (s32[1,1,1024,1]{2,3,1,0:T(1,128)}, s32[1,1,1024,1]{2,3,1,0:T(1,128)S(1)}, u32[]{:S(2)}) copy-start(s32[1,1,1024,1]{2,3,1,0:T(1,128)S(1)} %get-tuple-element.608) | copy-start | bytes 12292
  467.7 41.7 %copy-start.79 = (bf16[1280,768]{1,0:T(8,128)(2,1)}, bf16[1280,768]{1,0:T(8,128)(2,1)S(1)}, u32[]{:S(2)}) copy-start(bf16[1280,768]{1,0:T(8,128)(2,1)S(1)} %scatter_custom_fusion) | copy-start | bytes 5898244
  627.7 42.1 %copy-start.21 = (f32[512,768]{1,0:T(8,128)S(1)}, f32[512,768]{1,0:T(8,128)}, u32[]{:S(2)}) copy-start(f32[512,768]{1,0:T(8,128)} %copy-done.20) | copy-start | bytes 4718596
  627.7 42.1 %copy-start.92 = (f32[768]{0:T(1024)S(1)}, f32[768]{0:T(1024)}, u32[]{:S(2)}) copy-start(f32[768]{0:T(1024)} %get-tuple-element.567) | copy-start | bytes 9220
  627.7 42.1 %copy-start.109 = (f32[512]{0:T(512)S(1)}, f32[512]{0:T(512)}, u32[]{:S(2)}) copy-start(f32[512]{0:T(512)} %copy-done.108) | copy-start | bytes 6148
  627.7 72.8 %all-gather.24.cloned.1.call-start = ((), (), s32[]{:S(2)}) async-start(), calls=%async_computation.20 | async-start | bytes 2359296 | tf_op jit(solution)/shard_map/all_gather | solution.py:155
  628.3 256.4 %copy-start.106 = (f32[512]{0:T(512)}, f32[512]{0:T(512)S(1)}, u32[]{:S(2)}) copy-start(f32[512]{0:T(512)S(1)} %fusion.193) | copy-start | bytes 6148
  673.2 56.3 %all-gather.32.cloned.1.call-start = ((), (), s32[]{:S(2)}) async-start(), calls=%async_computation.33 | async-start | bytes 2359296 | tf_op jit(solution)/shard_map/all_gather | solution.py:183
  673.9 182.4 %reduce-scatter.26.cloned.1.call-start = ((), (), s32[]{:S(2)}) async-start(), calls=%async_computation.25 | async-start | bytes 4718592 | tf_op jit(solution)/shard_map/reduce_scatter | solution.py:220
  711.2 96.8 %copy-start.96 = (f32[1024]{0:T(1024)}, f32[1024]{0:T(1024)S(1)}, u32[]{:S(2)}) copy-start(f32[1024]{0:T(1024)S(1)} %get-tuple-element.578) | copy-start | bytes 12292
  711.2 96.8 %copy-start.100 = (f32[1024,2]{0,1:T(2,128)}, f32[1024,2]{0,1:T(2,128)S(1)}, u32[]{:S(2)}) copy-start(f32[1024,2]{0,1:T(2,128)S(1)} %get-tuple-element.579) | copy-start | bytes 24580
  812.8 71.9 %reduce-scatter.20.cloned.1.call-start = ((), (), s32[]{:S(2)}) async-start(), calls=%async_computation.21 | async-start | bytes 2359296 | tf_op jit(solution)/shard_map/reduce_scatter | solution.py:176
  813.6 146.8 %all-gather.28.cloned.1.call-start = ((), (), s32[]{:S(2)}) async-start(), calls=%async_computation.26 | async-start | bytes 2359296 | tf_op jit(solution)/shard_map/all_gather | solution.py:225
  813.7 75.1 %copy-start.134 = (f32[512]{0:T(512)}, f32[512]{0:T(512)S(1)}, u32[]{:S(2)}) copy-start(f32[512]{0:T(512)S(1)} %multiply_multiply_fusion.15) | copy-start | bytes 6148
  858.8 30.0 %copy-start.125 = (f32[512]{0:T(512)}, f32[512]{0:T(512)S(1)}, u32[]{:S(2)}) copy-start(f32[512]{0:T(512)S(1)} %multiply_multiply_fusion.13) | copy-start | bytes 6148
  888.8 78.2 %all-gather.26.cloned.1.call-start = ((), (), s32[]{:S(2)}) async-start(), calls=%async_computation.23 | async-start | bytes 2359296 | tf_op jit(solution)/shard_map/all_gather | solution.py:225
  905.7 585.4 %all-reduce.12.cloned.1.call-start = ((), (), s32[]{:S(2)}) async-start(), calls=%async_computation.34 | async-start | bytes 37748736
  960.3 533.2 %reduce-scatter.28.cloned.1.call-start = ((), (), s32[]{:S(2)}) async-start(), calls=%async_computation.27 | async-start | bytes 2359296 | tf_op jit(solution)/shard_map/reduce_scatter | solution.py:287
  972.5 39.0 %copy-start.24 = (bf16[2,512,6,64]{1,3,2,0:T(8,128)(2,1)}, bf16[2,512,6,64]{1,3,2,0:T(8,128)(2,1)S(1)}, u32[]{:S(2)}) copy-start(bf16[2,512,6,64]{1,3,2,0:T(8,128)(2,1)S(1)} %get-tuple-element.1069) | copy-start | bytes 2359300 | tf_op jit(solution)/shard_map/while
  1045.5 28.5 %slice-start.6 = ((s8[6291456]{0:T(1024)(128)(4,1)}), s8[2097152]{0:T(1024)(128)(4,1)S(1)}, s32[]{:S(2)}) async-start(s8[6291456]{0:T(1024)(128)(4,1)} %bitcast.444), calls=%async_computation.41 | async-start | bytes 4194304 | tf_op jit(solution)/shard_map/while
  1083.3 38.9 %copy-start.24 = (bf16[2,512,6,64]{1,3,2,0:T(8,128)(2,1)}, bf16[2,512,6,64]{1,3,2,0:T(8,128)(2,1)S(1)}, u32[]{:S(2)}) copy-start(bf16[2,512,6,64]{1,3,2,0:T(8,128)(2,1)S(1)} %get-tuple-element.1069) | copy-start | bytes 2359300 | tf_op jit(solution)/shard_map/while
  1156.0 28.9 %slice-start.6 = ((s8[6291456]{0:T(1024)(128)(4,1)}), s8[2097152]{0:T(1024)(128)(4,1)S(1)}, s32[]{:S(2)}) async-start(s8[6291456]{0:T(1024)(128)(4,1)} %bitcast.444), calls=%async_computation.41 | async-start | bytes 4194304 | tf_op jit(solution)/shard_map/while
  1202.9 290.6 %reduce-scatter.24.cloned.1.call-start = ((), (), s32[]{:S(2)}) async-start(), calls=%async_computation.24 | async-start | bytes 2359296 | tf_op jit(solution)/shard_map/reduce_scatter | solution.py:287
  1278.9 28.3 %slice-start.8 = ((s8[6291456]{0:T(1024)(128)(4,1)}), s8[2097152]{0:T(1024)(128)(4,1)S(1)}, s32[]{:S(2)}) async-start(s8[6291456]{0:T(1024)(128)(4,1)} %bitcast.446), calls=%async_computation.43 | async-start | bytes 4194304 | tf_op jit(solution)/shard_map/while
  1385.8 28.3 %slice-start.8 = ((s8[6291456]{0:T(1024)(128)(4,1)}), s8[2097152]{0:T(1024)(128)(4,1)S(1)}, s32[]{:S(2)}) async-start(s8[6291456]{0:T(1024)(128)(4,1)} %bitcast.446), calls=%async_computation.43 | async-start | bytes 4194304 | tf_op jit(solution)/shard_map/while
  1431.5 104.1 %reduce-scatter.16.cloned.1.call-start = ((), (), s32[]{:S(2)}) async-start(), calls=%async_computation.17 | async-start | bytes 2359296 | tf_op jit(solution)/shard_map/reduce_scatter | solution.py:176
  1432.2 116.3 %reduce-scatter.36.cloned.1.call-start = ((), (), s32[]{:S(2)}) async-start(), calls=%async_computation.31 | async-start | bytes 1253376 | tf_op jit(solution)/shard_map/reduce_scatter | solution.py:303
  1437.3 173.1 %reduce-scatter.34.cloned.1.call-start = ((), (), s32[]{:S(2)}) async-start(), calls=%async_computation.30 | async-start | bytes 1253376 | tf_op jit(solution)/shard_map/reduce_scatter | solution.py:303
  1442.2 230.0 %reduce-scatter.32.cloned.1.call-start = ((), (), s32[]{:S(2)}) async-start(), calls=%async_computation.29 | async-start | bytes 1253376 | tf_op jit(solution)/shard_map/reduce_scatter | solution.py:303
  1446.9 39.5 %copy-start.76 = (bf16[48,8,2,512]{3,1,2,0:T(8,128)(2,1)S(1)}, bf16[48,8,2,512]{3,1,2,0:T(8,128)(2,1)}, u32[]{:S(2)}) copy-start(bf16[48,8,2,512]{3,1,2,0:T(8,128)(2,1)} %copy-done.75) | copy-start | bytes 2359300
  1447.0 286.8 %reduce-scatter.30.cloned.1.call-start = ((), (), s32[]{:S(2)}) async-start(), calls=%async_computation.28 | async-start | bytes 1253376 | tf_op jit(solution)/shard_map/reduce_scatter | solution.py:303
  1491.0 44.5 %copy-start.131 = (f32[512]{0:T(512)S(1)}, f32[512]{0:T(512)}, u32[]{:S(2)}) copy-start(f32[512]{0:T(512)} %copy-done.130) | copy-start | bytes 6148
  1491.0 44.5 %copy-start.133 = (f32[512]{0:T(512)S(1)}, f32[512]{0:T(512)}, u32[]{:S(2)}) copy-start(f32[512]{0:T(512)} %copy-done.132) | copy-start | bytes 6148
  1491.0 44.5 %copy-start.22 = (f32[512,768]{1,0:T(8,128)S(1)}, f32[512,768]{1,0:T(8,128)}, u32[]{:S(2)}) copy-start(f32[512,768]{1,0:T(8,128)} %copy-done.20) | copy-start | bytes 4718596
  1491.0 44.5 %copy-start.93 = (f32[768]{0:T(1024)S(1)}, f32[768]{0:T(1024)}, u32[]{:S(2)}) copy-start(f32[768]{0:T(1024)} %get-tuple-element.567) | copy-start | bytes 9220
  1491.0 44.5 %copy-start.110 = (f32[512]{0:T(512)S(1)}, f32[512]{0:T(512)}, u32[]{:S(2)}) copy-start(f32[512]{0:T(512)} %copy-done.108) | copy-start | bytes 6148
  1491.0 44.5 %copy-start.135 = (f32[512]{0:T(512)S(1)}, f32[512]{0:T(512)}, u32[]{:S(2)}) copy-start(f32[512]{0:T(512)} %copy-done.134) | copy-start | bytes 6148
  (147 other events, 814.3 us)
Sparse Core Ops, SparseCore 0:
  56.0 27.2 all-gather.21
  85.4 27.1 all-gather.13
  248.9 40.9 reduce-scatter.17
  339.7 40.9 reduce-scatter.13
  386.0 27.4 all-gather.15
  414.9 27.4 all-gather.29
  444.6 53.4 all-gather.17
  500.4 51.9 all-gather.19
  627.8 41.8 reduce-scatter.21
  673.3 27.2 all-gather.23
  702.2 27.1 all-gather.31
  812.9 43.3 reduce-scatter.25
  858.6 26.0 reduce-scatter.19
  888.9 27.2 all-gather.27
  918.2 27.2 all-gather.25
  960.5 330.0 all-reduce.11
  1292.7 26.1 reduce-scatter.27
  1431.6 26.0 reduce-scatter.23
  1459.9 26.0 reduce-scatter.15
  1490.5 58.0 reduce-scatter.35
  1553.2 57.0 reduce-scatter.33
  1615.0 57.0 reduce-scatter.31
  1676.8 57.0 reduce-scatter.29
where the time goes:
time: 1750 us; the launch traced here: 1740 us
  matrix products  570 us (33%)
  waiting for transfers between devices  438 us (25%)
  blocking collectives  263 us (15%)
  local copies, waits for them, and re-layouts  257 us (15%)
  other arithmetic  161 us (9%)
  loops' own time  34.2 us (2%)
    reduce_scatter x4, waiting for transfers between devices, body(): lax.psum_scatter(weight_acc, 'fsdp', scatter_dimension=0, tiled=True)  190 us
    dot_general x8, matrix products, block_scores(): jnp.einsum('qhd,khd->hqk', query_block, keys_all, preferred_element_type=...  110 us
    dot_general x8, matrix products, block_scores(): jnp.einsum('cf,flg->clg', reduced_bias_table, expert_picker, preferred_el...  101 us
    reduce_scatter x2, waiting for transfers between devices, body(): lax.psum_scatter(grad_two_part, 'tp', scatter_dimension=0, tiled=True)  84.1 us
    unnamed x2, blocking collectives  79.2 us
    all_gather x1, blocking collectives, body(): lax.all_gather(router, ('fsdp', 'tp'), axis=0, tiled=True)  67.1 us
    dot_general x4, matrix products, backward_block(): jnp.einsum('toi,roi->tr', score_gradients, expert_picker, preferred_eleme...  64.9 us
    dot_general x4, local copies, waits for them, and re-layouts, block_scores(): jnp.einsum('cf,flg->clg', reduced_bias_table, expert_picker, preferred_el...  63 us
  transfers between devices with their start and end apart: 23, of which 12 were waited for; matrix products, arithmetic and copies ran while one was open for 45% of the time, Pallas kernels for 0%

commit v1 on v0

v1 whole, which is shorter than its diff:
```python
import functools

import jax
import jax.numpy as jnp
from jax import lax
from jax.experimental import pallas as pl
from jax.experimental.pallas import tpu as pltpu
from jax.sharding import PartitionSpec as P

epsilon = 1e-06
masked = -1e30
bucket_edges = (12, 16, 23, 32, 46, 64, 91)
TILE = 128
f32, bf16 = jnp.float32, jnp.bfloat16
highest = lax.Precision.HIGHEST
VMEM = pl.BlockSpec(memory_space=pltpu.VMEM)
SMEM = pl.BlockSpec(memory_space=pltpu.SMEM)


def params(**more):
    return pltpu.CompilerParams(vmem_limit_bytes=60 * 2**20, **more)


def mm(a, b):
    return lax.dot_general(a, b, (((1,), (0,)), ((), ())), preferred_element_type=f32)


def mm_nt(a, b):
    return lax.dot_general(a, b, (((1,), (1,)), ((), ())), preferred_element_type=f32)


def bucket_of(offset):
    distance = jnp.abs(offset)
    far_bucket = jnp.full_like(distance, 8)
    for edge_value in bucket_edges:
        far_bucket = far_bucket + (distance >= edge_value).astype(jnp.int32)
    near_bucket = jnp.where(distance < 8, distance, far_bucket)
    return near_bucket + 16 * (offset > 0).astype(jnp.int32)


def project_kernel(x_ref, gain_ref, w_ref, nrm_ref, q_ref, k_ref, v_ref, *, cols):
    length = x_ref.shape[0]
    depth = x_ref.shape[1]
    block = 256

    def rows_body(i, _):
        rows = pl.ds(pl.multiple_of(i * block, block), block)
        x = x_ref[rows, :].astype(f32)
        r = lax.rsqrt(jnp.mean(x * x, axis=-1, keepdims=True) + epsilon)
        n = (x * r * gain_ref[...]).astype(bf16)
        nrm_ref[rows, :] = n
        for t in range(2):
            w = w_ref[:, t].reshape(depth, 4 * cols)
            at = slice(t * cols, (t + 1) * cols)
            q = mm(n, w[:, :cols]).astype(bf16)
            q_ref[rows, at] = q * 0.125
            k_ref[rows, at] = mm(n, w[:, cols : 2 * cols]).astype(bf16)
            v_ref[rows, at] = mm(n, w[:, 2 * cols : 3 * cols]).astype(bf16)
        return 0

    lax.fori_loop(0, length // block, rows_body, 0)


def project(x, gain, w):
    length, depth = x.shape
    cols = w.shape[3] // 4
    shape = jax.ShapeDtypeStruct((length, depth), bf16)
    return pl.pallas_call(
        functools.partial(project_kernel, cols=cols),
        out_shape=[shape] * 4,
        in_specs=[VMEM] * 3,
        out_specs=[VMEM] * 4,
        compiler_params=params(),
        name="project",
    )(x, gain, w)


def attend_kernel(prefix_ref, far_ref, q_ref, k_ref, v_ref, band_ref, mixed_ref, rl_ref, p_ref, vext):
    h = pl.program_id(0)
    length = q_ref.shape[0]
    tiles = length // TILE
    half = lax.rem(h, 2)
    lane = lax.broadcasted_iota(jnp.int32, (1, TILE), 1)
    mine = (lane // 64) == half
    prefix = prefix_ref[0]
    far = far_ref[h]

    @pl.when(h == 0)
    def _():
        vext[:, TILE:] = jnp.ones((length, TILE), bf16)

    @pl.when(half == 0)
    def _():
        vext[:, :TILE] = v_ref[...]

    key = lax.broadcasted_iota(jnp.int32, (1, length), 1)
    hidden = jnp.where(key < prefix, 0.0, masked)
    beyond = hidden + far
    tri = jnp.where(
        lax.broadcasted_iota(jnp.int32, (TILE, TILE), 1)
        <= lax.broadcasted_iota(jnp.int32, (TILE, TILE), 0),
        0.0,
        masked,
    )
    keys = k_ref[...]
    for block in range(tiles // 2):
        q = jnp.where(mine, q_ref[block * 256 : block * 256 + 256, :], jnp.zeros((), bf16))
        s = mm_nt(q, keys)
        for part in range(2):
            i = block * 2 + part
            rows = slice(i * TILE, (i + 1) * TILE)
            pieces = []
            for j in range(tiles):
                at = slice(j * TILE, (j + 1) * TILE)
                piece = s[part * TILE : (part + 1) * TILE, at]
                if j == i - 1:
                    piece = piece + band_ref[0, :, :TILE]
                elif j == i:
                    piece = piece + (
                        band_ref[0, :, TILE : 2 * TILE] + jnp.maximum(tri, hidden[:, at])
                    )
                elif j == i + 1:
                    piece = piece + (band_ref[0, :, 2 * TILE :] + hidden[:, at])
                elif j > i:
                    piece = piece + beyond[:, at]
                pieces.append(piece)
            top = functools.reduce(jnp.maximum, pieces)
            top = jnp.max(top, axis=-1, keepdims=True)
            for j in range(tiles):
                at = slice(j * TILE, (j + 1) * TILE)
                p_ref[0, rows, at] = jnp.exp(pieces[j] - top).astype(bf16)
        rows = slice(block * 256, block * 256 + 256)
        o = mm(p_ref[0, rows, :], vext[...])
        rl = 1.0 / o[:, TILE:]
        out = (o[:, :TILE] * rl).astype(bf16)
        mixed_ref[rows, :] = jnp.where(mine, out, mixed_ref[rows, :])
        rl_ref[rows, :] = jnp.where(lane == h, rl, rl_ref[rows, :])


def attend(prefix, far, q, k, v, band):
    length, width = q.shape
    heads = band.shape[0]
    pair = pl.BlockSpec((length, TILE), lambda h: (0, h // 2))
    return pl.pallas_call(
        attend_kernel,
        grid=(heads,),
        in_specs=[
            SMEM,
            SMEM,
            pair,
            pair,
            pair,
            pl.BlockSpec((1, TILE, 3 * TILE), lambda h: (h, 0, 0)),
        ],
        out_specs=[
            pair,
            pl.BlockSpec((length, TILE), lambda h: (0, 0)),
            pl.BlockSpec((1, length, length), lambda h: (h, 0, 0)),
        ],
        out_shape=[
            jax.ShapeDtypeStruct((length, width), bf16),
            jax.ShapeDtypeStruct((length, TILE), f32),
            jax.ShapeDtypeStruct((heads, length, length), bf16),
        ],
        scratch_shapes=[pltpu.VMEM((length, 2 * TILE), bf16)],
        compiler_params=params(),
        name="attend",
    )(prefix, far, q, k, v, band)


def dispatch_kernel(
    x_ref, c_ref, mixed_ref, w_ref, gain_ref, router_ref, route_ref, slot_ref,
    res_ref, nt_ref, prob_ref, xs_ref, gs_ref, low_ref, *, cols,
):
    length, depth = x_ref.shape
    block = 256

    def rows_body(i, _):
        rows = pl.ds(pl.multiple_of(i * block, block), block)
        attended = jnp.zeros((block, depth), f32)
        for t in range(2):
            w = w_ref[:, t].reshape(depth, cols)
            attended = attended + mm_nt(mixed_ref[rows, t * cols : (t + 1) * cols], w)
        res = x_ref[rows, :].astype(f32) + attended
        res_ref[rows, :] = res
        r = lax.rsqrt(jnp.mean(res * res, axis=-1, keepdims=True) + epsilon)
        nt = (res * r * gain_ref[...]).astype(bf16)
        nt_ref[rows, :] = nt
        logits = lax.dot_general(
            nt.astype(f32), router_ref[...], (((1,), (0,)), ((), ())),
            precision=highest, preferred_element_type=f32,
        )
        first, second = logits[:, 0:1], logits[:, 1:2]
        top = jnp.maximum(first, second)
        a, b = jnp.exp(first - top), jnp.exp(second - top)
        total = a + b
        p0, p1 = a / total, b / total
        lane = lax.broadcasted_iota(jnp.int32, (1, TILE), 1)
        gate = jnp.where(route_ref[rows, :] == 0, p0, p1)
        prob_ref[rows, :] = jnp.where(lane == 0, p0, jnp.where(lane == 1, p1, gate))
        low_ref[rows, :] = (gate * c_ref[rows, :].astype(f32)).astype(bf16)
        return 0

    lax.fori_loop(0, length // block, rows_body, 0)
    slots = xs_ref.shape[0]
    step = 320

    def slots_body(i, _):
        at = pl.multiple_of(i * step, 64)
        place = lax.broadcasted_iota(jnp.int32, (step, 1), 0) + at
        pick = (slot_ref[...] == place).astype(bf16)
        xs_ref[pl.ds(at, step), :] = mm(pick, nt_ref[...]).astype(bf16)
        gs_ref[pl.ds(at, step), :] = mm(pick, low_ref[...]).astype(bf16)
        return 0

    lax.fori_loop(0, slots // step, slots_body, 0)


def dispatch(x, c, mixed, w, gain, router, route, slot_row, slots):
    length, depth = x.shape
    cols = w.shape[3]
    return pl.pallas_call(
        functools.partial(dispatch_kernel, cols=cols),
        out_shape=[
            jax.ShapeDtypeStruct((length, depth), f32),
            jax.ShapeDtypeStruct((length, depth), bf16),
            jax.ShapeDtypeStruct((length, TILE), f32),
            jax.ShapeDtypeStruct((slots, depth), bf16),
            jax.ShapeDtypeStruct((slots, depth), bf16),
        ],
        in_specs=[VMEM] * 8,
        out_specs=[VMEM] * 5,
        scratch_shapes=[pltpu.VMEM((length, depth), bf16)],
        compiler_params=params(),
        name="dispatch",
    )(x, c, mixed, w, gain, router, route, slot_row)


def experts_kernel(
    x_ref, g_ref, w1_ref, w2_ref, y_ref, gb_ref, d1_ref, d2_ref, xt, gt, y_acc, gb_acc
):
    step = pl.program_id(1)
    last = pl.num_programs(1) - 1
    group, _, rows, chunk = w1_ref.shape
    depth = group * rows

    @pl.when(step == 0)
    def _():
        xt[...] = x_ref[...].T
        gt[...] = g_ref[...].T
        y_acc[...] = jnp.zeros_like(y_acc)
        gb_acc[...] = jnp.zeros_like(gb_acc)

    w1 = w1_ref[:, 0].reshape(depth, chunk)
    w2 = w2_ref[:, 0].reshape(depth, chunk)
    inner = mm(x_ref[...], w1)
    hidden = mm(g_ref[...], w2)
    phi = 0.5 + 0.5 * lax.erf(inner * 0.7071067811865476)
    act = (inner * phi).astype(bf16)
    slope = phi + inner * (jnp.exp(inner * inner * -0.5) * 0.3989422804014327)
    grad = (hidden * slope).astype(bf16)
    y_acc[...] += mm_nt(act, w2)
    gb_acc[...] += mm_nt(grad, w1)
    d2_ref[:, 0] = mm(gt[...], act).astype(bf16).reshape(group, rows, chunk)
    d1_ref[:, 0] = mm(xt[...], grad).astype(bf16).reshape(group, rows, chunk)

    @pl.when(step == last)
    def _():
        y_ref[...] = y_acc[...].astype(bf16)
        gb_ref[...] = gb_acc[...].astype(bf16)


def experts(xs, gs, w1, w2, expert_count):
    slots, depth = xs.shape
    capacity = slots // expert_count
    group, halves, rows, width = w1.shape
    hidden = width // expert_count
    chunk = 512
    per = hidden // chunk
    row_block = pl.BlockSpec((capacity, depth), lambda e, s: (e, 0))
    weight_block = pl.BlockSpec(
        (group, 1, rows, chunk), lambda e, s: (0, s // per, 0, e * per + lax.rem(s, per))
    )
    return pl.pallas_call(
        experts_kernel,
        grid=(expert_count, halves * per),
        in_specs=[row_block, row_block, weight_block, weight_block],
        out_specs=[row_block, row_block, weight_block, weight_block],
        out_shape=[
            jax.ShapeDtypeStruct((slots, depth), bf16),
            jax.ShapeDtypeStruct((slots, depth), bf16),
            jax.ShapeDtypeStruct(w1.shape, bf16),
            jax.ShapeDtypeStruct(w2.shape, bf16),
        ],
        scratch_shapes=[
            pltpu.VMEM((depth, capacity), bf16),
            pltpu.VMEM((depth, capacity), bf16),
            pltpu.VMEM((capacity, depth), f32),
            pltpu.VMEM((capacity, depth), f32),
        ],
        compiler_params=params(),
        name="experts",
    )(xs, gs, w1, w2)


def combine_kernel(
    res_ref, c_ref, nt_ref, prob_ref, route_ref, slot_ref, y_ref, gb_ref, mixed_ref, w_ref, gain_ref,
    router_ref, out_ref, gres_ref, gmix_ref, dwo_ref, gain_part_ref, router_part_ref, gat, *, cols,
):
    length, depth = res_ref.shape
    slots = y_ref.shape[0]
    block = 256
    gain_part_ref[...] = jnp.zeros_like(gain_part_ref)
    router_part_ref[...] = jnp.zeros_like(router_part_ref)

    def rows_body(i, _):
        rows = pl.ds(pl.multiple_of(i * block, block), block)
        lane = lax.broadcasted_iota(jnp.int32, (1, slots), 1)
        pick = (slot_ref[rows, :] == lane).astype(bf16)
        y = mm(pick, y_ref[...])
        gn = mm(pick, gb_ref[...])
        res = res_ref[rows, :]
        c = c_ref[rows, :].astype(f32)
        prob = prob_ref[rows, :]
        p0, p1, gate = prob[:, 0:1], prob[:, 1:2], prob[:, 2:3]
        out_ref[rows, :] = (res + gate * y).astype(bf16)
        grad_gate = jnp.sum(c * y, axis=-1, keepdims=True)
        route = route_ref[rows, :]
        gl0 = p0 * (jnp.where(route == 0, 1.0, 0.0) - gate) * grad_gate
        gl1 = p1 * (jnp.where(route == 1, 1.0, 0.0) - gate) * grad_gate
        gn = gn + gl0 * router_ref[0:1, :] + gl1 * router_ref[1:2, :]
        nt = nt_ref[rows, :].astype(f32)
        router_part_ref[0:1, :] += jnp.sum(nt * gl0, axis=0, keepdims=True)
        router_part_ref[1:2, :] += jnp.sum(nt * gl1, axis=0, keepdims=True)
        r = lax.rsqrt(jnp.mean(res * res, axis=-1, keepdims=True) + epsilon)
        n2 = res * r
        gain_part_ref[0:1, :] += jnp.sum(gn * n2, axis=0, keepdims=True)
        g2 = gn * gain_ref[...]
        gres = c + r * (g2 - n2 * jnp.mean(g2 * n2, axis=-1, keepdims=True))
        gres_ref[rows, :] = gres
        ga = gres.astype(bf16)
        gat[:, rows] = ga.T
        for t in range(2):
            w = w_ref[:, t].reshape(depth, cols)
            gmix_ref[rows, t * cols : (t + 1) * cols] = mm(ga, w).astype(bf16)
        return 0

    lax.fori_loop(0, length // block, rows_body, 0)
    group = dwo_ref.shape[0]
    rows = dwo_ref.shape[2]
    for t in range(2):
        d = mm(gat[...], mixed_ref[:, t * cols : (t + 1) * cols])
        dwo_ref[:, t] = d.astype(bf16).reshape(group, rows, cols)


def combine(res, c, nt, prob, route, slot_col, y, gb, mixed, w, gain, router_rows):
    length, depth = res.shape
    cols = w.shape[3]
    return pl.pallas_call(
        functools.partial(combine_kernel, cols=cols),
        out_shape=[
            jax.ShapeDtypeStruct((length, depth), bf16),
            jax.ShapeDtypeStruct((length, depth), f32),
            jax.ShapeDtypeStruct((length, depth), bf16),
            jax.ShapeDtypeStruct(w.shape, bf16),
            jax.ShapeDtypeStruct((8, depth), f32),
            jax.ShapeDtypeStruct((8, depth), f32),
        ],
        in_specs=[VMEM] * 12,
        out_specs=[VMEM] * 6,
        scratch_shapes=[pltpu.VMEM((depth, length), bf16)],
        compiler_params=params(),
        name="combine",
    )(res, c, nt, prob, route, slot_col, y, gb, mixed, w, gain, router_rows)


def attend_back_kernel(
    q_ref, k_ref, v_ref, mixed_ref, g_ref, rl_ref, p_ref,
    dq_ref, dk_ref, dv_ref, band_ref, far_ref, kext, qt, dot_, dkt, dvt, delta,
):
    h = pl.program_id(0)
    length = q_ref.shape[0]
    tiles = length // TILE
    half = lax.rem(h, 2)
    lane = lax.broadcasted_iota(jnp.int32, (1, TILE), 1)
    mine = (lane // 64) == half
    block = 256

    @pl.when(h == 0)
    def _():
        row = lax.broadcasted_iota(jnp.int32, (length, TILE), 0)
        col = lax.broadcasted_iota(jnp.int32, (length, TILE), 1)
        kext[:, TILE:] = (row // TILE == col).astype(bf16)

    @pl.when(half == 0)
    def _():
        kext[:, :TILE] = k_ref[...]
        qt[...] = q_ref[...].T

    band_ref[...] = jnp.zeros_like(band_ref)
    left = jnp.zeros((1, TILE), f32)
    right = jnp.zeros((1, TILE), f32)
    for b in range(length // block):
        rows = slice(b * block, (b + 1) * block)
        rl = jnp.sum(jnp.where(lane == h, rl_ref[rows, :], 0.0), axis=-1, keepdims=True)
        g = jnp.where(mine, g_ref[rows, :].astype(f32) * rl, 0.0)
        delta = jnp.sum(g * mixed_ref[rows, :].astype(f32), axis=-1, keepdims=True)
        g = g.astype(bf16)
        gp = mm_nt(g, v_ref[...])
        p = p_ref[0, rows, :]
        ds = p.astype(f32) * (gp - delta)
        low = ds.astype(bf16)
        dq = mm(low, kext[...])
        dq_ref[rows, :] = jnp.where(mine, (dq[:, :TILE] * 0.125).astype(bf16), dq_ref[rows, :])
        gv = mm(g.T, p)
        gk = mm(qt[:, rows], low)
        if b == 0:
            dvt[...] = gv
            dkt[...] = gk
        else:
            dvt[...] += gv
            dkt[...] += gk
        for part in range(block // TILE):
            i = b * (block // TILE) + part
            sums = dq[part * TILE : (part + 1) * TILE, TILE:]
            sums = jnp.sum(sums, axis=0, keepdims=True)
            left = left + jnp.where(lane <= i - 2, sums, 0.0)
            right = right + jnp.where(lane >= i + 2, sums, 0.0)
            for side in (-1, 0, 1):
                j = i + side
                if 0 <= j < tiles:
                    band_ref[0, :, (side + 1) * TILE : (side + 2) * TILE] += ds[
                        part * TILE : (part + 1) * TILE, j * TILE : (j + 1) * TILE
                    ]
    row = lax.broadcasted_iota(jnp.int32, (8, TILE), 0)
    far_ref[0] = jnp.where(row == 0, left, jnp.where(row == 1, right, 0.0))
    dk_ref[...] = jnp.where(mine, dkt[...].T.astype(bf16), dk_ref[...])
    dv_ref[...] = jnp.where(mine, dvt[...].T.astype(bf16), dv_ref[...])


def attend_back(q, k, v, mixed, g, rl, p):
    length, width = q.shape
    heads = p.shape[0]
    pair = pl.BlockSpec((length, TILE), lambda h: (0, h // 2))
    shape = jax.ShapeDtypeStruct((length, width), bf16)
    return pl.pallas_call(
        attend_back_kernel,
        grid=(heads,),
        in_specs=[
            pair, pair, pair, pair, pair,
            pl.BlockSpec((length, TILE), lambda h: (0, 0)),
            pl.BlockSpec((1, length, length), lambda h: (h, 0, 0)),
        ],
        out_specs=[
            pair, pair, pair,
            pl.BlockSpec((1, TILE, 3 * TILE), lambda h: (h, 0, 0)),
            pl.BlockSpec((1, 8, TILE), lambda h: (h, 0, 0)),
        ],
        out_shape=[
            shape, shape, shape,
            jax.ShapeDtypeStruct((heads, TILE, 3 * TILE), f32),
            jax.ShapeDtypeStruct((heads, 8, TILE), f32),
        ],
        scratch_shapes=[
            pltpu.VMEM((length, 2 * TILE), bf16),
            pltpu.VMEM((TILE, length), bf16),
            pltpu.VMEM((TILE, length), bf16),
            pltpu.VMEM((TILE, length), f32),
            pltpu.VMEM((TILE, length), f32),
            pltpu.VMEM((length, TILE), f32),
        ],
        compiler_params=params(),
        name="attend_back",
    )(q, k, v, mixed, g, rl, p)


def finish_kernel(
    x_ref, gain_ref, nrm_ref, dq_ref, dk_ref, dv_ref, w_ref, gres_ref,
    gx_ref, dw_ref, gain_part_ref, nt, *, cols,
):
    length, depth = x_ref.shape
    group, _, rows_per, _ = dw_ref.shape
    block = 256
    gain_part_ref[...] = jnp.zeros_like(gain_part_ref)
    nt[...] = nrm_ref[...].T
    for t in range(2):
        at = slice(t * cols, (t + 1) * cols)
        for n, ref in enumerate((dq_ref, dk_ref, dv_ref)):
            d = mm(nt[...], ref[:, at]).astype(bf16)
            dw_ref[:, t, :, n * cols : (n + 1) * cols] = d.reshape(group, rows_per, cols)

    def rows_body(i, _):
        rows = pl.ds(pl.multiple_of(i * block, block), block)
        gn = jnp.zeros((block, depth), f32)
        for t in range(2):
            w = w_ref[:, t].reshape(depth, 4 * cols)
            at = slice(t * cols, (t + 1) * cols)
            for n, ref in enumerate((dq_ref, dk_ref, dv_ref)):
                gn = gn + mm_nt(ref[rows, at], w[:, n * cols : (n + 1) * cols])
        x = x_ref[rows, :].astype(f32)
        r = lax.rsqrt(jnp.mean(x * x, axis=-1, keepdims=True) + epsilon)
        n1 = x * r
        gain_part_ref[0:1, :] += jnp.sum(gn * n1, axis=0, keepdims=True)
        g1 = gn * gain_ref[...]
        gx_ref[rows, :] = gres_ref[rows, :] + r * (
            g1 - n1 * jnp.mean(g1 * n1, axis=-1, keepdims=True)
        )
        return 0

    lax.fori_loop(0, length // block, rows_body, 0)


def finish(x, gain, nrm, dq, dk, dv, w, gres):
    length, depth = x.shape
    cols = w.shape[3] // 4
    return pl.pallas_call(
        functools.partial(finish_kernel, cols=cols),
        out_shape=[
            jax.ShapeDtypeStruct((length, depth), f32),
            jax.ShapeDtypeStruct(w.shape[:3] + (3 * cols,), bf16),
            jax.ShapeDtypeStruct((8, depth), f32),
        ],
        in_specs=[VMEM] * 8,
        out_specs=[VMEM] * 3,
        scratch_shapes=[pltpu.VMEM((depth, length), bf16)],
        compiler_params=params(),
        name="finish",
    )(x, gain, nrm, dq, dk, dv, w, gres)


def body(
    tokens, cotangent, routes, prefix, attn_gain, query_weight, key_weight, value_weight,
    out_weight_t, bias_table, ffn_gain, router, inner_weight, down_weight_t,
):
    fsdp, tp = lax.axis_size("fsdp"), lax.axis_size("tp")
    half_len, depth = tokens.shape[2], tokens.shape[3]
    length = half_len * tp
    heads_here, buckets = bias_table.shape
    heads = heads_here * tp
    expert_count = router.shape[1]
    capacity = length * 5 // (4 * expert_count)
    slots = capacity * expert_count
    rows, cols = query_weight.shape
    small = attn_gain.shape[0]
    me = lax.axis_index("tp")
    swap = [(0, 1), (1, 0)]

    def exchange(array):
        keep = lax.dynamic_index_in_dim(array, me, 0, keepdims=False)
        give = lax.dynamic_index_in_dim(array, 1 - me, 0, keepdims=False)
        take = lax.ppermute(give, "tp", swap)
        return keep, take

    def whole_sequence(array):
        keep, take = exchange(array[:, 0])
        return jnp.where(me == 0, jnp.concatenate([keep, take]), jnp.concatenate([take, keep]))

    attn_shard = jnp.concatenate([query_weight, key_weight, value_weight, out_weight_t], axis=1)
    ffn_shape = (rows, expert_count * inner_weight.shape[2])
    attn_w = lax.all_gather(attn_shard, ("fsdp", "tp")).reshape(fsdp, tp, rows, 4 * cols)
    vectors = jnp.concatenate(
        [attn_gain, ffn_gain, router.T.reshape(-1), bias_table.reshape(-1)]
    )
    vectors = lax.all_gather(vectors, ("fsdp", "tp"))
    w1 = lax.all_gather(inner_weight.reshape(ffn_shape), ("fsdp", "tp"))
    w2 = lax.all_gather(down_weight_t.reshape(ffn_shape), ("fsdp", "tp"))
    w1 = w1.reshape(fsdp, tp, *ffn_shape)
    w2 = w2.reshape(fsdp, tp, *ffn_shape)
    x = whole_sequence(tokens)
    c = whole_sequence(cotangent)
    gain_one = vectors[:, :small].reshape(1, depth)
    gain_two = vectors[:, small : 2 * small].reshape(1, depth)
    router_rows = jnp.stack(
        [vectors[:, (2 + e) * small : (3 + e) * small].reshape(depth) for e in range(expert_count)]
    )
    table = vectors[:tp, (2 + expert_count) * small :].reshape(heads, buckets)
    router_cols = jnp.pad(router_rows.T, ((0, 0), (0, TILE - expert_count)))
    router_rows = jnp.pad(router_rows, ((0, 8 - expert_count), (0, 0)))

    route = lax.dynamic_index_in_dim(routes, me, 0, keepdims=False)[0]
    prefix_len = lax.dynamic_index_in_dim(prefix, me, 0, keepdims=False)
    chosen = (route == jnp.arange(expert_count)[None, :]).astype(bf16)
    before = jnp.tril(jnp.ones((length, length), bf16), -1)
    rank = jnp.dot(before, chosen, preferred_element_type=f32).astype(jnp.int32)
    slot_ids = route[:, 0] * capacity + jnp.where(route[:, 0] == 0, rank[:, 0], rank[:, 1])

    low_table = table.astype(bf16).astype(f32)
    offset = jnp.arange(3 * TILE)[None, :] - TILE - jnp.arange(TILE)[:, None]
    bucket = bucket_of(offset)
    near = jnp.take(low_table, bucket.reshape(-1), axis=1).reshape(heads, TILE, 3 * TILE)
    farthest = buckets // 2 - 1
    base = low_table[:, farthest]
    band = near - base[:, None, None]
    far = low_table[:, buckets - 1] - base

    nrm, q, k, v = project(x, gain_one, attn_w)
    mixed, rl, p = attend(prefix_len, far, q, k, v, band)
    out_w = attn_w[..., 3 * cols :]
    res, nt, prob, xs, gs = dispatch(
        x, c, mixed, out_w, gain_two, router_cols, route, slot_ids[None, :], slots
    )
    y, gb, d1, d2 = experts(xs, gs, w1, w2, expert_count)
    d1 = lax.psum_scatter(d1.reshape(fsdp * tp, *ffn_shape), ("fsdp", "tp"))
    d2 = lax.psum_scatter(d2.reshape(fsdp * tp, *ffn_shape), ("fsdp", "tp"))
    out, gres, gmix, dwo, gain_two_part, router_part = combine(
        res, c, nt, prob, route, slot_ids[:, None], y, gb, mixed, out_w, gain_two, router_rows
    )
    dq, dk, dv, band_grad, far_grad = attend_back(q, k, v, mixed, gmix, rl, p)
    gx, dw, gain_one_part = finish(x, gain_one, nrm, dq, dk, dv, attn_w, gres)
    dw = lax.psum_scatter(
        jnp.concatenate([dw, dwo], axis=-1).reshape(fsdp * tp, rows, 4 * cols), ("fsdp", "tp")
    ).astype(f32)

    picker = (bucket.reshape(-1)[:, None] == jnp.arange(buckets)[None, :]).astype(f32)
    table_grad = jnp.dot(
        band_grad.reshape(heads, -1), picker, precision=highest, preferred_element_type=f32
    )
    table_grad = table_grad.at[:, farthest].add(jnp.sum(far_grad[:, 0, :], axis=-1))
    table_grad = table_grad.at[:, buckets - 1].add(jnp.sum(far_grad[:, 1, :], axis=-1))
    sums = jnp.concatenate(
        [gain_one_part[0], gain_two_part[0]]
        + [router_part[e] for e in range(expert_count)]
        + [table_grad.reshape(-1)]
    )
    sums = lax.psum(sums, ("fsdp", "tp"))
    start = (lax.axis_index("fsdp") * tp + me) * small
    own = [
        lax.dynamic_slice_in_dim(sums, n * depth + start, small) for n in range(2 + expert_count)
    ]
    table_own = lax.dynamic_slice_in_dim(
        sums[(2 + expert_count) * depth :].reshape(heads, buckets), me * heads_here, heads_here
    )

    def halves(array, kind):
        array = array.reshape(tp, half_len, depth)
        keep, take = exchange(array.astype(bf16))
        keep = lax.dynamic_index_in_dim(array, me, 0, keepdims=False).astype(kind)
        take = take.astype(kind)
        both = jnp.where(me == 0, jnp.stack([keep, take]), jnp.stack([take, keep]))
        return both[:, None]

    ffn_out = inner_weight.shape
    return (
        halves(out, bf16),
        halves(gx, f32),
        own[0],
        dw[:, :cols],
        dw[:, cols : 2 * cols],
        dw[:, 2 * cols : 3 * cols],
        dw[:, 3 * cols :],
        table_own,
        own[1],
        jnp.stack(own[2:], axis=1),
        d1.astype(f32).reshape(ffn_out),
        d2.astype(f32).reshape(ffn_out),
    )


def solution(mesh):
    tokens = P(None, "fsdp", "tp", None)
    every = P(("fsdp", "tp"))
    square = P("fsdp", "tp")
    expert = P("fsdp", None, "tp")
    in_specs = (
        tokens, tokens, P(None, "fsdp", None, None), P(None, "fsdp"), every, square, square, square,
        square, P("tp", None), every, P(("fsdp", "tp"), None), expert, expert,
    )
    out_specs = (
        tokens, tokens, every, square, square, square, square, P("tp", None), every,
        P(("fsdp", "tp"), None), expert, expert,
    )
    return jax.shard_map(body, mesh=mesh, in_specs=in_specs, out_specs=out_specs, check_vma=False)
```

time: 1750 us -> 874 us (0.50)
  matrix products: 570 us -> 4.16 us
  Pallas kernels: 0 us -> 173 us
  other arithmetic: 161 us -> 26 us
  waiting for transfers between devices: 438 us -> 304 us
  blocking collectives: 263 us -> 131 us
  local copies, waits for them, and re-layouts: 257 us -> 207 us
  loops' own time: 34.2 us -> 0 us
    dot_general x82 -> x2, matrix products: 570 us -> 4.16 us  [the longest x1 3.34 us: body(): jnp.dot(band_grad.reshape(heads, -1), picker, precision=highest, preferre...]
    pallas_call x0 -> x7, Pallas kernels: none -> 173 us  [the longest x1 48.6 us: experts(): pl.pallas_call(experts_kernel, grid=(expert_count, halves * per), in_spec...]
    all_gather x5 -> x0, blocking collectives: 150 us -> none  [the longest x1 67.1 us: body(): lax.all_gather(router, ('fsdp', 'tp'), axis=0, tiled=True)]
    gather x4 -> x2, local copies, waits for them, and re-layouts: 32.1 us -> 178 us  [body(): jnp.take(low_table, bucket.reshape(-1), axis=1)]
    all_gather x10 -> x3, waiting for transfers between devices: 93.8 us -> 0.01 us  [the longest x1 0.01 us: body(): lax.all_gather(attn_shard, ('fsdp', 'tp')).reshape(fsdp, tp, rows, 4 * cols)]
    dot_general x4 -> x0, local copies, waits for them, and re-layouts: 63 us -> none  [block_scores(): jnp.einsum('cf,flg->clg', reduced_bias_table, expert_picker, preferred_el...]
    convert_element_type x16 -> x2, other arithmetic: 60.1 us -> 1.01 us  [the longest x1 0.93 us: body(): dw = lax.psum_scatter(jnp.concatenate([dw, dwo], axis=-1).reshape(fsdp *...]
    convert_element_type x6 -> x4, local copies, waits for them, and re-layouts: 49.7 us -> 4.88 us  [the longest x1 2.36 us: body(): d2.astype(f32).reshape(ffn_out)]
  transfers between devices with their start and end apart: 23 -> 10, of which waited for: 12 -> 3; matrix products, arithmetic and copies ran while one was open for 45% -> 26% of each run, Pallas kernels for 0% -> 7%
where the time goes in v1:
time: 874 us; the launch traced here: 865 us
  waiting for transfers between devices  304 us (35%)
  local copies, waits for them, and re-layouts  207 us (24%)
  Pallas kernels  173 us (20%)
  blocking collectives  131 us (15%)
  other arithmetic  26 us (3%)
  between operations  14.9 us (2%)
    gather x2, local copies, waits for them, and re-layouts, body(): jnp.take(low_table, bucket.reshape(-1), axis=1)  178 us
    reduce_scatter x1, waiting for transfers between devices, body(): d2 = lax.psum_scatter(d2.reshape(fsdp * tp, *ffn_shape), ('fsdp', 'tp'))  140 us
    reduce_scatter x1, waiting for transfers between devices, body(): d1 = lax.psum_scatter(d1.reshape(fsdp * tp, *ffn_shape), ('fsdp', 'tp'))  138 us
    unnamed x1, blocking collectives  73.6 us
    psum x1, blocking collectives, body(): sums = lax.psum(sums, ('fsdp', 'tp'))  57 us
    pallas_call x1, Pallas kernels, experts(): pl.pallas_call(experts_kernel, grid=(expert_count, halves * per), in_spec...  48.6 us
    pallas_call x1, Pallas kernels, attend_back(): pl.pallas_call(attend_back_kernel, grid=(heads,), in_specs=[pair, pair, p...  29.7 us
    pallas_call x1, Pallas kernels, attend(): pl.pallas_call(attend_kernel, grid=(heads,), in_specs=[SMEM, SMEM, pair,...  26.8 us
  transfers between devices with their start and end apart: 10, of which 3 were waited for; matrix products, arithmetic and copies ran while one was open for 26% of the time, Pallas kernels for 7%

profile of v1, /device:TPU:0, one launch (start us, length us, event | category | flops | bytes accessed | tf_op | source)
XLA Modules:
  0.0 865.0 jit_solution(10652589765664818174)
XLA Ops:
  7.3 1.6 pad_maximum_fusion.1
  8.9 2.0 all_gather_reshape.6
  11.0 1.9 all_gather_reshape.7
  13.0 1.3 dynamic-slice_bitcast_fusion.6
  14.3 3.0 collective-permute-start
  17.4 1.2 dynamic-slice_bitcast_fusion.4
  18.8 0.2 maximum_dynamic-update-slice_fusion
  19.0 73.6 %all-reduce.2 = f32[9216]{0:T(1024)S(1)} all-reduce(f32[9216]{0:T(1024)S(1)} %maximum_dynamic-update-slice_fusion), channel_id=2, replica_groups=mesh['fsdp'=16,'tp'=2] {'fsdp','tp'}, use_global_device_ids=true, to_apply=%add.2 | all-reduce | flops 9216 | bytes 73728
  93.2 0.2 copy.75.route_ref
  93.5 0.2 copy.85
  93.7 0.2 copy.86
  94.0 0.8 fusion.6
  94.8 1.2 slice_reduce_fusion
  96.0 0.6 fusion.35.slot_ref
  96.6 1.4 compare_select_fusion
  98.3 0.6 constant_dynamic-slice_fusion.2
  98.9 0.7 reshape.488.gain_ref
  99.5 0.7 reshape.486.gain_ref
  100.2 0.6 pad.13.router_ref
  101.0 0.8 pad.12.clone.router_ref
  101.8 163.0 %gather_fusion = f32[49152,12]{1,0:T(8,128)} fusion(f32[12,32]{0,1:T(8,128)S(1)} %copy.71, s32[49152]{0:T(1024)S(1)} %broadcast_clamp_fusion), kind=kCustom, calls=%fused_computation | custom fusion | bytes 4915200 | tf_op jit(solution)/shard_map/jit(_take)/gather | solution.py:590
  264.8 14.9 %copy.83 = f32[12,128,384]{2,1,0:T(8,128)S(1)} copy(f32[12,128,384]{0,2,1:T(8,128)} %bitcast.70) | data formatting | bytes 4718592 | tf_op jit(solution)/shard_map/jit(_take)/gather | solution.py:590
  279.7 0.5 sub.67.far_ref
  280.2 0.3 compare_and_fusion
  280.5 1.7 select_subtract_fusion.band_ref
  282.2 3.2 maximum_select_fusion.1.x_ref
  285.4 1.8 maximum_select_fusion.2.c_ref
  287.2 2.4 slice.135.w_ref
  289.6 10.7 %project.1 = (bf16[1024,768]{1,0:T(8,128)(2,1)}, bf16[1024,768]{1,0:T(8,128)(2,1)}, bf16[1024,768]{1,0:T(8,128)(2,1)}, bf16[1024,768]{1,0:T(8,128)(2,1)}) custom-call(bf16[1024,768]{1,0:T(8,128)(2,1)} %maximum_select_fusion.1.x_ref, f32[1,768]{1,0:T(1,128)} %reshape.486.gain_ref, bf16[16,2,48,1536]{3,2,1,0:T(8,128)(2,1)} %bitcast.72), custom_call_target="tpu_custom_call" | custom-call | tf_op jit(solution)/shard_map/project/pallas_call | solution.py:68
  300.3 26.8 %attend.1 = (bf16[1024,768]{1,0:T(8,128)(2,1)}, f32[1024,128]{1,0:T(8,128)}, bf16[12,1024,1024]{2,1,0:T(8,128)(2,1)}) custom-call(s32[1]{0:T(128)} %bitcast.4.prefix_ref, f32[12]{0:T(128)} %sub.67.far_ref, bf16[1024,768]{1,0:T(8,128)(2,1)} %get-tuple-element.66.q_ref, bf16[1024,768]{1,0:T(8,128)(2,1)} %get-tuple-element.67.k_ref, ...), custom_call_target="tpu_custom_call" | custom-call | tf_op jit(solution)/shard_map/attend/pallas_call | solution.py:144
  327.1 20.9 %dispatch.1 = (f32[1024,768]{1,0:T(8,128)}, bf16[1024,768]{1,0:T(8,128)(2,1)}, f32[1024,128]{1,0:T(8,128)}, bf16[1280,768]{1,0:T(8,128)(2,1)}, bf16[1280,768]{1,0:T(8,128)(2,1)}) custom-call(bf16[1024,768]{1,0:T(8,128)(2,1)} %maximum_select_fusion.1.x_ref, bf16[1024,768]{1,0:T(8,128)(2,1)} %maximum_select_fusion.2.c_ref, ...), custom_call_target="tpu_custom_call" | custom-call | tf_op jit(solution)/shard_map/dispatch/pallas_call | solution.py:222
  348.0 48.6 %experts.1 = (bf16[1280,768]{1,0:T(8,128)(2,1)}, bf16[1280,768]{1,0:T(8,128)(2,1)}, bf16[16,2,48,3072]{3,2,1,0:T(8,128)(2,1)}, bf16[16,2,48,3072]{3,2,1,0:T(8,128)(2,1)}) custom-call(bf16[1280,768]{1,0:T(8,128)(2,1)} %get-tuple-element.73.x_ref, bf16[1280,768]{1,0:T(8,128)(2,1)} %get-tuple-element.74.g_ref, bf16[16,2,48,3072]{3,2,1,0:T(8,128)(2,1)} %bitcast.79, ...), custom_call_target="tpu_custom_call" | custom-call | tf_op jit(solution)/shard_map/experts/pallas_call | solution.py:284
  396.6 17.2 %combine.1 = (bf16[1024,768]{1,0:T(8,128)(2,1)}, f32[1024,768]{1,0:T(8,128)}, bf16[1024,768]{1,0:T(8,128)(2,1)}, bf16[16,2,48,384]{3,2,1,0:T(8,128)(2,1)}, f32[8,768]{1,0:T(8,128)}, /*index=5*/f32[8,768]{1,0:T(8,128)}) custom-call(f32[1024,768]{1,0:T(8,128)} %get-tuple-element.70.res_ref, bf16[1024,768]{1,0:T(8,128)(2,1)} %maximum_select_fusion.2.c_ref, ...), custom_call_target="tpu_custom_call" | custom-call | tf_op jit(solution)/shard_map/combine/pallas_call | solution.py:359
  413.9 29.7 %attend_back.1 = (bf16[1024,768]{1,0:T(8,128)(2,1)}, bf16[1024,768]{1,0:T(8,128)(2,1)}, bf16[1024,768]{1,0:T(8,128)(2,1)}, f32[12,128,384]{2,1,0:T(8,128)}, f32[12,8,128]{2,1,0:T(8,128)}) custom-call(bf16[1024,768]{1,0:T(8,128)(2,1)} %get-tuple-element.66.q_ref, bf16[1024,768]{1,0:T(8,128)(2,1)} %get-tuple-element.67.k_ref, ...), custom_call_target="tpu_custom_call" | custom-call | tf_op jit(solution)/shard_map/attend_back/pallas_call | solution.py:446
  443.5 18.8 %finish.1 = (f32[1024,768]{1,0:T(8,128)}, bf16[16,2,48,1152]{3,2,1,0:T(8,128)(2,1)}, f32[8,768]{1,0:T(8,128)}) custom-call(bf16[1024,768]{1,0:T(8,128)(2,1)} %maximum_select_fusion.1.x_ref, f32[1,768]{1,0:T(1,128)} %reshape.486.gain_ref, bf16[1024,768]{1,0:T(8,128)(2,1)} %get-tuple-element.78.nrm_ref, bf16[1024,768]{1,0:T(8,128)(2,1)} %get-tuple-element.82.dq_ref, ...), custom_call_target="tpu_custom_call" | custom-call | tf_op jit(solution)/shard_map/finish/pallas_call | solution.py:516
  462.4 4.8 pad_maximum_fusion
  467.2 0.5 reduce-scatter.8.cloned.1.call-update
  467.8 0.5 reduce-scatter.6.cloned.1.call-update
  468.4 0.6 compare_reduce_fusion
  469.2 1.0 slice_reduce_fusion.4
  470.4 1.7 fusion.11
  472.1 2.3 collective-permute-start.3
  474.4 1.0 dynamic-slice_bitcast_fusion.2
  475.4 0.3 pad.45
  475.7 1.8 copy.87
  477.6 3.3 fusion
  480.9 0.7 add_select_fusion
  481.7 0.8 slice_reduce_fusion.9
  482.5 0.8 slice_reduce_fusion.6
  483.7 57.0 %psum.7 = f32[3456]{0:T(1024)S(1)} all-reduce(f32[3456]{0:T(1024)S(1)} %constant_dynamic-update-slice_fusion), channel_id=1, replica_groups=mesh['fsdp'=16,'tp'=2] {'fsdp','tp'}, use_global_device_ids=true, to_apply=%region_3.4 | all-reduce | flops 3456 | bytes 27648 | tf_op jit(solution)/shard_map/psum | solution.py:625
  540.7 0.6 dynamic-slice_bitcast_fusion.8
  541.3 0.6 pad_maximum_fusion.3
  541.9 0.6 constant_dynamic-slice_fusion
  542.5 1.5 dynamic-slice_bitcast_fusion
  544.0 1.4 maximum_select_fusion.3
  545.4 1.2 bitcast_convert_fusion
  546.7 1.9 maximum_select_fusion
  548.5 25.0 %reduce-scatter.4.cloned.1.call-done = bf16[1,48,1536]{2,1,0:T(8,128)(2,1)} async-done(((bf16[32,48,1536]{2,1,0:T(8,128)(2,1)}), bf16[1,48,1536]{2,1,0:T(8,128)(2,1)}) %reduce-scatter.4.cloned.1.call-update) | async-done | bytes 147472 | tf_op jit(solution)/shard_map/reduce_scatter | solution.py:610
  573.5 0.9 bitcast_convert_fusion.1
  574.4 0.7 fusion.40
  575.1 139.7 %reduce-scatter.8.cloned.1.call-done = bf16[1,48,3072]{2,1,0:T(8,128)(2,1)} async-done(((bf16[32,48,3072]{2,1,0:T(8,128)(2,1)}), bf16[1,48,3072]{2,1,0:T(8,128)(2,1)}) %reduce-scatter.8.cloned.1.call-update) | async-done | bytes 294928 | tf_op jit(solution)/shard_map/reduce_scatter | solution.py:604
  714.9 2.4 reshape.505
  717.2 138.1 %reduce-scatter.6.cloned.1.call-done = bf16[1,48,3072]{2,1,0:T(8,128)(2,1)} async-done(((bf16[32,48,3072]{2,1,0:T(8,128)(2,1)}), bf16[1,48,3072]{2,1,0:T(8,128)(2,1)}) %reduce-scatter.6.cloned.1.call-update) | async-done | bytes 294928 | tf_op jit(solution)/shard_map/reduce_scatter | solution.py:603
  855.3 2.4 reshape.504
  (85 shorter events, 2.6 us)
Async XLA Ops:
  7.2 91.1 %copy-start = (s32[2,1]{0,1:T(1,128)S(1)}, s32[2,1]{0,1:T(1,128)}, u32[]{:S(2)}) copy-start(s32[2,1]{0,1:T(1,128)} %param.21) | copy-start | bytes 28
  7.2 5.8 copy-start.6
  7.2 280.0 %all-gather.10.cloned.1.call-start = ((), (), s32[]{:S(2)}) async-start(), calls=%async_computation.8 | async-start | bytes 4866048 | tf_op jit(solution)/shard_map/all_gather | solution.py:560
  8.9 8.5 copy-start.7
  8.9 339.1 %all-gather.6.cloned.1.call-start = ((), (), s32[]{:S(2)}) async-start(), calls=%async_computation.3 | async-start | bytes 9732096 | tf_op jit(solution)/shard_map/all_gather | solution.py:565
  11.0 337.0 %all-gather.8.cloned.1.call-start = ((), (), s32[]{:S(2)}) async-start(), calls=%async_computation.4 | async-start | bytes 9732096 | tf_op jit(solution)/shard_map/all_gather | solution.py:566
  12.9 560.6 %reduce-scatter.4.cloned.1.call-start = ((), (), s32[]{:S(2)}) async-start(), calls=%async_computation.5 | async-start | bytes 4866048 | tf_op jit(solution)/shard_map/reduce_scatter | solution.py:610
  14.3 4.3 copy-start.14
  14.3 4.4 copy-start.11
  14.3 4.5 copy-start.12
  14.3 4.5 copy-start.13
  14.3 78.8 %copy-start.10 = (s32[2,1,1024,1]{2,3,1,0:T(1,128)S(1)}, s32[2,1,1024,1]{2,3,1,0:T(1,128)}, u32[]{:S(2)}) copy-start(s32[2,1,1024,1]{2,3,1,0:T(1,128)} %param.20) | copy-start | bytes 24580
  14.3 267.8 %collective-permute-start = (bf16[512,768]{1,0:T(8,128)(2,1)}, bf16[512,768]{1,0:T(8,128)(2,1)}, u32[]{:S(2)}, u32[]{:S(2)}) collective-permute-start(bf16[512,768]{1,0:T(8,128)(2,1)} %get-tuple-element.109), channel_id=1, source_target_pairs={{0,1},{1,0},{2,3},{3,2},{4,5},{5,4},{6,7},{7,6},{8,9},{9,8},{10,11... | collective-permute-start | bytes 2359304 | tf_op jit(solution)/shard_map/ppermute | solution.py:551
  18.6 266.8 %collective-permute-start.1 = (bf16[512,768]{1,0:T(8,128)(2,1)}, bf16[512,768]{1,0:T(8,128)(2,1)S(1)}, u32[]{:S(2)}, u32[]{:S(2)}) collective-permute-start(bf16[512,768]{1,0:T(8,128)(2,1)} %get-tuple-element.107), channel_id=1, source_target_pairs={{0,1},{1,0},{2,3},{3,2},{4,5},{5,4},{6,7},{7,6},{8,9},{9,8},{10,11... | collective-permute-start | bytes 2359304 | tf_op jit(solution)/shard_map/ppermute | solution.py:551
  93.4 1.4 copy-start.2
  280.5 1.7 copy-start.4
  282.2 3.2 copy-start.3
  443.5 18.8 %copy-start.9 = (bf16[16,2,48,384]{3,2,1,0:T(8,128)(2,1)S(1)}, bf16[16,2,48,384]{3,2,1,0:T(8,128)(2,1)}, u32[]{:S(2)}) copy-start(bf16[16,2,48,384]{3,2,1,0:T(8,128)(2,1)} %get-tuple-element.93) | copy-start | bytes 3538948
  467.1 247.7 %reduce-scatter.8.cloned.1.call-start = ((), (), s32[]{:S(2)}) async-start(), calls=%async_computation.7 | async-start | bytes 9732096 | tf_op jit(solution)/shard_map/reduce_scatter | solution.py:604
  467.7 387.6 %reduce-scatter.6.cloned.1.call-start = ((), (), s32[]{:S(2)}) async-start(), calls=%async_computation.6 | async-start | bytes 9732096 | tf_op jit(solution)/shard_map/reduce_scatter | solution.py:603
  468.3 6.1 copy-start.8
  470.4 5.0 copy-start.5
  472.1 73.3 %collective-permute-start.3 = (bf16[512,768]{1,0:T(8,128)(2,1)S(1)}, bf16[512,768]{1,0:T(8,128)(2,1)}, u32[]{:S(2)}, u32[]{:S(2)}) collective-permute-start(bf16[512,768]{1,0:T(8,128)(2,1)S(1)} %fusion.11), channel_id=1, source_target_pairs={{0,1},{1,0},{2,3},{3,2},{4,5},{5,4},{6,7},{7,6},{8,9},{9,8},{10,11... | collective-permute-start | bytes 2359304 | tf_op jit(solution)/shard_map/ppermute | solution.py:551
  475.4 68.6 %collective-permute-start.2 = (bf16[512,768]{1,0:T(8,128)(2,1)}, bf16[512,768]{1,0:T(8,128)(2,1)S(1)}, u32[]{:S(2)}, u32[]{:S(2)}) collective-permute-start(bf16[512,768]{1,0:T(8,128)(2,1)} %get-tuple-element.105), channel_id=1, source_target_pairs={{0,1},{1,0},{2,3},{3,2},{4,5},{5,4},{6,7},{7,6},{8,9},{9,8},{10,11... | collective-permute-start | bytes 2359304 | tf_op jit(solution)/shard_map/ppermute | solution.py:551
  546.7 311.0 %copy-start.1 = (s32[2,1]{0,1:T(1,128)S(1)}, s32[2,1]{0,1:T(1,128)}, u32[]{:S(2)}) copy-start(s32[2,1]{0,1:T(1,128)} %param.21) | copy-start | bytes 28
Sparse Core Ops, SparseCore 0:
  11.5 69.7 all-gather.9
  84.2 80.5 all-gather.5
  167.7 80.6 all-gather.7
  467.3 106.1 reduce-scatter.3
  580.2 134.5 reduce-scatter.7
  720.6 134.6 reduce-scatter.5

commit v2 on v1

--- a/solution.py
+++ b/solution.py
@@ -75,8 +75,11 @@
     )(x, gain, w)
 
 
-def attend_kernel(prefix_ref, far_ref, q_ref, k_ref, v_ref, band_ref, mixed_ref, rl_ref, p_ref, vext):
+def attend_kernel(prefix_ref, far_ref, q_ref, k_ref, v_ref, bias_ref, mixed_ref, rl_ref, p_ref, vext):
     h = pl.program_id(0)
+    band = pltpu.roll(
+        jnp.broadcast_to(bias_ref[0, 0:1, :], (TILE, 4 * TILE)), 0, 1, stride=1, stride_axis=0
+    )
     length = q_ref.shape[0]
     tiles = length // TILE
     half = lax.rem(h, 2)
@@ -114,13 +117,13 @@
                 at = slice(j * TILE, (j + 1) * TILE)
                 piece = s[part * TILE : (part + 1) * TILE, at]
                 if j == i - 1:
-                    piece = piece + band_ref[0, :, :TILE]
+                    piece = piece + band[:, :TILE]
                 elif j == i:
                     piece = piece + (
-                        band_ref[0, :, TILE : 2 * TILE] + jnp.maximum(tri, hidden[:, at])
+                        band[:, TILE : 2 * TILE] + jnp.maximum(tri, hidden[:, at])
                     )
                 elif j == i + 1:
-                    piece = piece + (band_ref[0, :, 2 * TILE :] + hidden[:, at])
+                    piece = piece + (band[:, 2 * TILE : 3 * TILE] + hidden[:, at])
                 elif j > i:
                     piece = piece + beyond[:, at]
                 pieces.append(piece)
@@ -137,9 +140,9 @@
         rl_ref[rows, :] = jnp.where(lane == h, rl, rl_ref[rows, :])
 
 
-def attend(prefix, far, q, k, v, band):
+def attend(prefix, far, q, k, v, bias):
     length, width = q.shape
-    heads = band.shape[0]
+    heads = bias.shape[0]
     pair = pl.BlockSpec((length, TILE), lambda h: (0, h // 2))
     return pl.pallas_call(
         attend_kernel,
@@ -150,7 +153,7 @@
             pair,
             pair,
             pair,
-            pl.BlockSpec((1, TILE, 3 * TILE), lambda h: (h, 0, 0)),
+            pl.BlockSpec((1, 8, 4 * TILE), lambda h: (h, 0, 0)),
         ],
         out_specs=[
             pair,
@@ -165,7 +168,7 @@
         scratch_shapes=[pltpu.VMEM((length, 2 * TILE), bf16)],
         compiler_params=params(),
         name="attend",
-    )(prefix, far, q, k, v, band)
+    )(prefix, far, q, k, v, bias)
 
 
 def dispatch_kernel(
@@ -376,7 +379,7 @@
 
 def attend_back_kernel(
     q_ref, k_ref, v_ref, mixed_ref, g_ref, rl_ref, p_ref,
-    dq_ref, dk_ref, dv_ref, band_ref, far_ref, kext, qt, dot_, dkt, dvt, delta,
+    dq_ref, dk_ref, dv_ref, diag_ref, kext, qt, dkt, dvt, band_ref,
 ):
     h = pl.program_id(0)
     length = q_ref.shape[0]
@@ -429,11 +432,19 @@
             for side in (-1, 0, 1):
                 j = i + side
                 if 0 <= j < tiles:
-                    band_ref[0, :, (side + 1) * TILE : (side + 2) * TILE] += ds[
+                    band_ref[:, (side + 1) * TILE : (side + 2) * TILE] += ds[
                         part * TILE : (part + 1) * TILE, j * TILE : (j + 1) * TILE
                     ]
-    row = lax.broadcasted_iota(jnp.int32, (8, TILE), 0)
-    far_ref[0] = jnp.where(row == 0, left, jnp.where(row == 1, right, 0.0))
+    turned = band_ref[0:8, :]
+    for g in range(1, TILE // 8):
+        turned = turned + pltpu.roll(band_ref[8 * g : 8 * g + 8, :], 4 * TILE - 8 * g, 1)
+    diag = turned[0:1, :]
+    for r in range(1, 8):
+        diag = diag + pltpu.roll(turned[r : r + 1, :], 4 * TILE - r, 1)
+    diag_ref[0] = jnp.zeros((8, 4 * TILE), f32)
+    diag_ref[0, 0:1, :] = diag
+    diag_ref[0, 1:2, :TILE] = left
+    diag_ref[0, 2:3, :TILE] = right
     dk_ref[...] = jnp.where(mine, dkt[...].T.astype(bf16), dk_ref[...])
     dv_ref[...] = jnp.where(mine, dvt[...].T.astype(bf16), dv_ref[...])
 
@@ -453,21 +464,18 @@
         ],
         out_specs=[
             pair, pair, pair,
-            pl.BlockSpec((1, TILE, 3 * TILE), lambda h: (h, 0, 0)),
-            pl.BlockSpec((1, 8, TILE), lambda h: (h, 0, 0)),
+            pl.BlockSpec((1, 8, 4 * TILE), lambda h: (h, 0, 0)),
         ],
         out_shape=[
             shape, shape, shape,
-            jax.ShapeDtypeStruct((heads, TILE, 3 * TILE), f32),
-            jax.ShapeDtypeStruct((heads, 8, TILE), f32),
+            jax.ShapeDtypeStruct((heads, 8, 4 * TILE), f32),
         ],
         scratch_shapes=[
             pltpu.VMEM((length, 2 * TILE), bf16),
             pltpu.VMEM((TILE, length), bf16),
-            pltpu.VMEM((TILE, length), bf16),
             pltpu.VMEM((TILE, length), f32),
             pltpu.VMEM((TILE, length), f32),
-            pltpu.VMEM((length, TILE), f32),
+            pltpu.VMEM((TILE, 4 * TILE), f32),
         ],
         compiler_params=params(),
         name="attend_back",
@@ -475,7 +483,7 @@
 
 
 def finish_kernel(
-    x_ref, gain_ref, nrm_ref, dq_ref, dk_ref, dv_ref, w_ref, gres_ref,
+    x_ref, gain_ref, nrm_ref, dq_ref, dk_ref, dv_ref, w_ref, gres_ref, dwo_ref,
     gx_ref, dw_ref, gain_part_ref, nt, *, cols,
 ):
     length, depth = x_ref.shape
@@ -483,6 +491,7 @@
     block = 256
     gain_part_ref[...] = jnp.zeros_like(gain_part_ref)
     nt[...] = nrm_ref[...].T
+    dw_ref[:, :, :, 3 * cols :] = dwo_ref[...]
     for t in range(2):
         at = slice(t * cols, (t + 1) * cols)
         for n, ref in enumerate((dq_ref, dk_ref, dv_ref)):
@@ -510,22 +519,573 @@
     lax.fori_loop(0, length // block, rows_body, 0)
 
 
-def finish(x, gain, nrm, dq, dk, dv, w, gres):
+def finish(x, gain, nrm, dq, dk, dv, w, gres, dwo):
     length, depth = x.shape
     cols = w.shape[3] // 4
     return pl.pallas_call(
         functools.partial(finish_kernel, cols=cols),
         out_shape=[
             jax.ShapeDtypeStruct((length, depth), f32),
-            jax.ShapeDtypeStruct(w.shape[:3] + (3 * cols,), bf16),
+            jax.ShapeDtypeStruct(w.shape, bf16),
             jax.ShapeDtypeStruct((8, depth), f32),
         ],
-        in_specs=[VMEM] * 8,
+        in_specs=[VMEM] * 9,
         out_specs=[VMEM] * 3,
         scratch_shapes=[pltpu.VMEM((depth, length), bf16)],
         compiler_params=params(),
         name="finish",
-    )(x, gain, nrm, dq, dk, dv, w, gres)
+    )(x, gain, nrm, dq, dk, dv, w, gres, dwo)
+
+
+def grid_sizes(fsdp):
+    ny = 2 if fsdp <= 16 else 4
+    return {"z": fsdp // (2 * ny), "y": ny, "c": 2, "x": 2}
+
+
+class Grid:
+    def __init__(self, fsdp):
+        self.size = grid_sizes(fsdp)
+        ny = self.size["y"]
+        i = lax.axis_index("fsdp")
+        self.at = {
+            "z": i // (2 * ny),
+            "y": lax.rem(i // 2, ny),
+            "c": lax.rem(i, 2),
+            "x": lax.axis_index("tp"),
+        }
+
+    def device(self, dim, to):
+        at = dict(self.at)
+        at[dim] = to
+        return ((at["z"] * self.size["y"] + at["y"]) * 2 + at["c"], at["x"])
+
+    def enter(self):
+        barrier = pltpu.get_barrier_semaphore()
+
+        def greet(device):
+            pl.semaphore_signal(barrier, inc=1, device_id=device, device_id_type=pl.DeviceIdType.MESH)
+
+        count = 0
+        for dim in "czyx":
+            n, me = self.size[dim], self.at[dim]
+            if n == 2:
+                greet(self.device(dim, 1 - me))
+                count = count + 1
+            elif n > 2:
+                run(me > 0, functools.partial(greet, self.device(dim, me - 1)))
+                run(me < n - 1, functools.partial(greet, self.device(dim, me + 1)))
+                count = count + (me > 0).astype(jnp.int32) + (me < n - 1).astype(jnp.int32)
+        pl.semaphore_wait(barrier, count)
+
+
+def run(when, act):
+    if when is None:
+        act()
+    else:
+        pl.when(when)(act)
+
+
+class Draft:
+    def __init__(self, fsdp):
+        self.size = grid_sizes(fsdp)
+        self.at = dict.fromkeys("zycx", 0)
+        self.used, self.shapes = 0, []
+
+    def pick(self):
+        self.used += 1
+
+    def buffer(self, shape, kind):
+        self.shapes.append(pltpu.VMEM(shape, kind))
+
+
+class Wire:
+    def __init__(self, grid, sends, receives, buffers=()):
+        self.grid, self.sends, self.receives = grid, sends, receives
+        self.size, self.at = grid.size, grid.at
+        self.used, self.sent, self.buffers = 0, [], list(buffers)
+
+    def pick(self):
+        self.used += 1
+        return self.used - 1
+
+    def buffer(self, shape, kind):
+        return self.buffers.pop(0)
+
+    def send(self, src, dst, dim, to, sem, when=None):
+        copy = pltpu.make_async_remote_copy(
+            src_ref=src, dst_ref=dst, send_sem=self.sends.at[sem], recv_sem=self.receives.at[sem],
+            device_id=self.grid.device(dim, to), device_id_type=pl.DeviceIdType.MESH,
+        )
+        run(when, copy.start)
+        self.sent.append((when, copy))
+
+    def wait(self, dst, sem, when=None):
+        copy = pltpu.make_async_remote_copy(
+            src_ref=dst, dst_ref=dst, send_sem=self.sends.at[sem], recv_sem=self.receives.at[sem],
+            device_id=self.grid.device("x", 1 - self.at["x"]), device_id_type=pl.DeviceIdType.MESH,
+        )
+        run(when, copy.wait_recv)
+
+    def close(self):
+        for when, copy in self.sent:
+            run(when, copy.wait_send)
+
+
+link_rate = {"z": 87e3, "y": 87e3, "x": 87e3, "c": 300e3}
+link_delay = 2.0
+
+
+def schedule(chains, room=3, ready=None):
+    here = [0] * len(chains)
+    begun = [False] * len(chains)
+    opens = list(ready) if ready is not None else [0.0] * len(chains)
+    free = dict.fromkeys(link_rate, 0.0)
+    busy = dict.fromkeys(link_rate, 0)
+    flying, acts, now = [], [], 0.0
+
+    def rest(n):
+        return sum(p[1] / link_rate[p[0]] + link_delay for p in chains[n][1][here[n] :])
+
+    while True:
+        for dim in link_rate:
+            while busy[dim] < room:
+                able = [
+                    n
+                    for n in range(len(chains))
+                    if not begun[n] and opens[n] <= now
+                    and here[n] < len(chains[n][1]) and chains[n][1][here[n]][0] == dim
+                ]
+                if not able:
+                    break
+                n = min(able, key=lambda n: (chains[n][0], -rest(n), n))
+                phase = chains[n][1][here[n]]
+                free[dim] = max(now, free[dim]) + phase[1] / link_rate[dim]
+                flying.append((free[dim] + link_delay, n))
+                acts.append((now, phase[2]))
+                busy[dim] += 1
+                begun[n] = True
+        later = [opens[n] for n in range(len(chains)) if opens[n] > now]
+        if not flying and not later:
+            return acts
+        flying.sort()
+        if later and (not flying or min(later) < flying[0][0]):
+            now = min(later)
+            continue
+        now, n = flying.pop(0)
+        phase = chains[n][1][here[n]]
+        acts.append((now, phase[3]))
+        busy[phase[0]] -= 1
+        begun[n] = False
+        here[n] += 1
+
+
+def spot(fixed, at, dim, slot):
+    return tuple(
+        slot if d == dim else at[d] if d in fixed else slice(None) for d in "zycx"
+    )
+
+
+def gather_chain(wire, full, columns, width, order):
+    phases = []
+    todo = [d for d in order + "c" if wire.size[d] > 1]
+    bytes_here = width * 2 * 2
+
+    def look(fixed, dim, slot):
+        return full.at[spot(fixed, wire.at, dim, slot) + (slice(None), columns)]
+
+    for n_dim, dim in enumerate(todo):
+        n, me = wire.size[dim], wire.at[dim]
+        view = functools.partial(look, todo[n_dim:], dim)
+        cost = bytes_here if dim != "c" else bytes_here // 2
+        if n == 2:
+            sem = wire.pick()
+
+            def start(view=view, dim=dim, me=me, sem=sem):
+                wire.send(view(me), view(me), dim, 1 - me, sem)
+
+            def finish(view=view, me=me, sem=sem):
+                wire.wait(view(1 - me), sem)
+
+            phases.append((dim, cost, start, finish))
+        else:
+            for hop in range(1, n):
+                up, down = wire.pick(), wire.pick()
+
+                def start(view=view, dim=dim, n=n, me=me, hop=hop, up=up, down=down):
+                    low, high = me - (hop - 1), me + (hop - 1)
+                    wire.send(view(low), view(low), dim, me + 1, up, (me + 1 < n) & (low >= 0))
+                    wire.send(view(high), view(high), dim, me - 1, down, (me > 0) & (high < n))
+
+                def finish(view=view, n=n, me=me, hop=hop, up=up, down=down):
+                    wire.wait(view(me - hop), up, me - hop >= 0)
+                    wire.wait(view(me + hop), down, me + hop < n)
+
+                phases.append((dim, cost, start, finish))
+        bytes_here *= n
+    return phases
+
+
+def swap_chain(wire, pairs, size):
+    phases = []
+    for src, dst, mine in pairs:
+        sem = wire.pick()
+
+        def start(src=src, dst=dst, sem=sem):
+            wire.send(src, dst, "x", 1 - wire.at["x"], sem)
+
+        def finish(mine=mine, sem=sem):
+            wire.wait(mine, sem)
+
+        phases.append(("x", size, start, finish))
+    return phases
+
+
+def parts_of(start, width):
+    tiles = width // TILE
+    small = max(tiles // 6, 1)
+    large = (tiles - small) // 2
+    edges = [start, start + large * TILE, start + (large + small) * TILE, start + width]
+    return [slice(a, b) for a, b in zip(edges, edges[1:])]
+
+
+ORDERS = ("zyx", "xyz", "xzy")
+
+
+def gather_group(wire, full, start, width, rows, rank):
+    return [
+        (rank, gather_chain(wire, full, at, rows * (at.stop - at.start), order))
+        for at, order in zip(parts_of(start, width), ORDERS)
+    ]
+
+
+def gather_plan(wire, refs, rows, cols, wide, expert_count, half, depth):
+    attn, w1, w2, vec, tokens, x_all, cotangent, c_all = refs
+    chains = gather_group(wire, attn, 0, 4 * cols, rows, 0)
+    chains.append((0, gather_chain(wire, vec, slice(None), 8 * TILE, "zyx")))
+    for rank, src, dst in ((0, tokens, x_all), (3, cotangent, c_all)):
+        pairs = [(None, None, None)] * 2
+        if src is not None:
+            x, piece = wire.at["x"], half // 2
+            pairs = []
+            for n in range(2):
+                own = pl.ds(pl.multiple_of(x * half + n * piece, piece), piece)
+                other = pl.ds(pl.multiple_of((1 - x) * half + n * piece, piece), piece)
+                pairs.append(
+                    (src.at[1 - x, 0, pl.ds(n * piece, piece)], dst.at[own], dst.at[other])
+                )
+        chains += [(rank, swap_chain(wire, [pair], 2 * half * depth)) for pair in pairs]
+    for e in range(expert_count):
+        for n, full in enumerate((w1, w2)):
+            chains += gather_group(wire, full, e * wide, wide, rows, 1 + 2 * e + n)
+    return chains
+
+
+def gather_kernel(
+    wq, wk, wv, wo, w1, w2, vec, tokens, cotangent,
+    attn_all, w1_all, w2_all, vec_all, x_all, c_all, sends, receives, local, *, fsdp, expert_count,
+):
+    grid = Grid(fsdp)
+    wire = Wire(grid, sends, receives)
+    here = tuple(grid.at[d] for d in "zycx")
+    rows, cols = wq.shape
+    half, depth = tokens.shape[2], tokens.shape[3]
+    x = grid.at["x"]
+    mine = [
+        (ref, attn_all.at[here + (slice(None), slice(n * cols, (n + 1) * cols))])
+        for n, ref in enumerate((wq, wk, wv, wo))
+    ]
+    own_rows = pl.ds(pl.multiple_of(x * half, half), half)
+    mine += [(vec, vec_all.at[here]), (w1, w1_all.at[here]), (w2, w2_all.at[here])]
+    mine += [(tokens.at[x, 0], x_all.at[own_rows]), (cotangent.at[x, 0], c_all.at[own_rows])]
+    copies = [pltpu.make_async_copy(a, b, local.at[n]) for n, (a, b) in enumerate(mine)]
+    for copy in copies:
+        copy.start()
+    grid.enter()
+    for copy in copies:
+        copy.wait()
+    chains = gather_plan(
+        wire, (attn_all, w1_all, w2_all, vec_all, tokens, x_all, cotangent, c_all),
+        rows, cols, w1.shape[1] // expert_count, expert_count, half, depth,
+    )
+    for _, act in schedule(chains):
+        act()
+    wire.close()
+
+
+ANY = pl.BlockSpec(memory_space=pl.ANY)
+
+
+def gather(wq, wk, wv, wo, w1, w2, vec, tokens, cotangent, fsdp, expert_count):
+    size = grid_sizes(fsdp)
+    shape = tuple(size[d] for d in "zycx")
+    rows, cols = wq.shape
+    half, depth = tokens.shape[2], tokens.shape[3]
+    draft = Draft(fsdp)
+    gather_plan(
+        draft, (None,) * 8, rows, cols, w1.shape[1] // expert_count, expert_count, half, depth
+    )
+    return pl.pallas_call(
+        functools.partial(gather_kernel, fsdp=fsdp, expert_count=expert_count),
+        out_shape=[
+            jax.ShapeDtypeStruct(shape + (rows, 4 * cols), bf16),
+            jax.ShapeDtypeStruct(shape + w1.shape, bf16),
+            jax.ShapeDtypeStruct(shape + w2.shape, bf16),
+            jax.ShapeDtypeStruct(shape + vec.shape, f32),
+            jax.ShapeDtypeStruct((2 * half, depth), bf16),
+            jax.ShapeDtypeStruct((2 * half, depth), bf16),
+        ],
+        in_specs=[ANY] * 9,
+        out_specs=[ANY] * 6,
+        scratch_shapes=[
+            pltpu.SemaphoreType.DMA((draft.used,)),
+            pltpu.SemaphoreType.DMA((draft.used,)),
+            pltpu.SemaphoreType.DMA((9,)),
+        ],
+        compiler_params=params(collective_id=0, has_side_effects=True),
+        name="gather",
+    )(wq, wk, wv, wo, w1, w2, vec, tokens, cotangent)
+
+
+def add_into(total, index, part):
+    lead = next((n for n, i in enumerate(index[:3]) if isinstance(i, slice)), None)
+    if lead is None:
+        total[index] = total[index] + part[...]
+        return
+
+    def body(n, _):
+        at = index[:lead] + (n,) + index[lead + 1 :]
+        total[at] = total[at] + part[n]
+        return 0
+
+    lax.fori_loop(0, total.shape[lead], body, 0)
+
+
+def reduce_chain(wire, grads, columns, total, offset, rows, loads, order):
+    width = columns.stop - columns.start
+    here = slice(columns.start - offset, columns.stop - offset)
+    size, at = wire.size, wire.at
+    shape = {d: size[d] for d in "zyx"}
+    phases = []
+    bytes_all = rows * width * 2 * size["z"] * size["y"] * size["x"]
+
+    def block(done, dim, slot):
+        lead = tuple(
+            slot if d == dim else at[d] if d in done else slice(None) for d in "zyx"
+        )
+        return lead + (slice(None), here)
+
+    def buffer(*lead):
+        return wire.buffer(tuple(lead) + (rows, width), bf16)
+
+    sem = wire.pick()
+    incoming = buffer(size["z"], size["y"], size["x"])
+    c = at["c"]
+
+    def start(incoming=incoming, sem=sem):
+        loads(columns, here)[0].start()
+        wire.send(
+            grads.at[:, :, 1 - c, :, :, columns], incoming, "c", 1 - c, sem
+        )
+
+    def finish(incoming=incoming, sem=sem):
+        loads(columns, here)[0].wait()
+        wire.wait(incoming, sem)
+        add_into(total, block("", None, None), incoming)
+
+    phases.append(("c", bytes_all, start, finish))
+    done = ""
+    cost = 2 * bytes_all
+    for dim in (d for d in order if size[d] > 1):
+        n, me = size[dim], at[dim]
+        look = functools.partial(block, done, dim)
+        lead = [size[d] for d in "zyx" if d != dim and d not in done]
+        cost //= n
+        if n == 2:
+            sem = wire.pick()
+            incoming = buffer(*lead)
+
+            def start(look=look, dim=dim, me=me, sem=sem, incoming=incoming):
+                wire.send(total.at[look(1 - me)], incoming, dim, 1 - me, sem)
+
+            def finish(look=look, me=me, sem=sem, incoming=incoming):
+                wire.wait(incoming, sem)
+                add_into(total, look(me), incoming)
+
+            phases.append((dim, cost, start, finish))
+        else:
+            incoming = buffer(2 * (n - 1), *lead)
+            for t in range(n - 1):
+                up, down = wire.pick(), wire.pick()
+
+                def start(look=look, dim=dim, n=n, me=me, t=t, up=up, down=down, incoming=incoming):
+                    wire.send(
+                        total.at[look(n - 1 - t + me)], incoming.at[t], dim, me + 1, up, me <= t
+                    )
+                    back = n - 1 - me
+                    wire.send(
+                        total.at[look(t - back)], incoming.at[n - 1 + t], dim, me - 1, down,
+                        back <= t,
+                    )
+
+                def finish(look=look, n=n, me=me, t=t, up=up, down=down, incoming=incoming):
+                    back = n - 1 - me
+
+                    def take_up():
+                        wire.wait(incoming.at[t], up)
+                        add_into(total, look(n - 2 - t + me), incoming.at[t])
+
+                    def take_down():
+                        wire.wait(incoming.at[n - 1 + t], down)
+                        add_into(total, look(t + 1 - back), incoming.at[n - 1 + t])
+
+                    run((me > 0) & (me - 1 <= t), take_up)
+                    run((back > 0) & (back - 1 <= t), take_down)
+
+                phases.append((dim, cost, start, finish))
+        done += dim
+    return phases
+
+
+def reduce_group(wire, grads, start, width, rows, rank, loads):
+    size = wire.size
+    total = wire.buffer((size["z"], size["y"], size["x"], rows, width), bf16)
+    chains = []
+    for n, (columns, order) in enumerate(zip(parts_of(start, width), ORDERS)):
+        chains.append(
+            (
+                rank,
+                reduce_chain(
+                    wire, grads, columns, total, start, rows,
+                    functools.partial(loads, grads, total, n), order[::-1],
+                ),
+            )
+        )
+    return chains, total
+
+
+def reduce_plan(wire, refs, local, rows, cols, wide, expert_count, half, depth):
+    dw, d1, d2, vec, out, out_end, low, low_in = refs
+    at = wire.at
+    groups = [(d, e * wide, wide) for e in range(expert_count) for d in (d1, d2)]
+    groups.append((dw, 0, 4 * cols))
+    chains, totals = [], []
+    for rank, (grads, start, width) in enumerate(groups):
+
+        def loads(grads, total, n, columns, here, rank=rank):
+            return [
+                pltpu.make_async_copy(
+                    grads.at[:, :, at["c"], :, :, columns],
+                    total.at[:, :, :, :, here],
+                    local.at[rank * 3 + n],
+                )
+            ]
+
+        more, total = reduce_group(wire, grads, start, width, rows, rank, loads)
+        chains += more
+        totals.append(total)
+    chains.append((0, gather_chain(wire, vec, slice(None), 16 * TILE, "zyx")))
+    pairs = [(None, None, None)] * 2
+    if out is not None:
+        x = at["x"]
+        other = pl.ds(pl.multiple_of((1 - x) * half, half), half)
+        pairs = [
+            (out.at[other], out_end.at[x, 0], out_end.at[1 - x, 0]),
+            (low, low_in, low_in),
+        ]
+    chains += [(rank, swap_chain(wire, [pair], 4 * half * depth)) for rank, pair in enumerate(pairs)]
+    return chains, totals
+
+
+def reduce_kernel(
+    dw, d1, d2, vec, out, gx, dw_own, d1_own, d2_own, vec_all, out_end, gx_end,
+    sends, receives, local, gx_block, low, low_in, dw_block, d_block, *buffers, fsdp, expert_count,
+):
+    grid = Grid(fsdp)
+    wire = Wire(grid, sends, receives, buffers)
+    at = grid.at
+    rows, wide = d1_own.shape
+    wide //= expert_count
+    half, depth = gx_end.shape[2], gx_end.shape[3]
+    x = at["x"]
+    here = tuple(at[d] for d in "zycx")
+    last = 3 * (2 * expert_count + 1)
+    own = pl.ds(pl.multiple_of(x * half, half), half)
+    other = pl.ds(pl.multiple_of((1 - x) * half, half), half)
+    fetch = pltpu.make_async_copy(gx.at[other], gx_block, local.at[last])
+    copies = [
+        pltpu.make_async_copy(vec, vec_all.at[here], local.at[last + 1]),
+        pltpu.make_async_copy(out.at[own], out_end.at[x, 0], local.at[last + 2]),
+        pltpu.make_async_copy(gx.at[own], gx_end.at[x, 0], local.at[last + 3]),
+    ]
+    fetch.start()
+    for copy in copies:
+        copy.start()
+    grid.enter()
+    fetch.wait()
+    low[...] = gx_block[...].astype(bf16)
+    for copy in copies:
+        copy.wait()
+    chains, totals = reduce_plan(
+        wire, (dw, d1, d2, vec_all, out, out_end, low, low_in), local, rows, dw_own.shape[1] // 4,
+        wide, expert_count, half, depth,
+    )
+    for _, act in schedule(chains):
+        act()
+    gx_block[...] = low_in[...].astype(f32)
+    place = (at["z"], at["y"], at["x"])
+    ends = [pltpu.make_async_copy(gx_block, gx_end.at[1 - x, 0], local.at[0])]
+    dw_block[...] = totals[-1][place].astype(f32)
+    ends.append(pltpu.make_async_copy(dw_block, dw_own, local.at[1]))
+    for e in range(expert_count):
+        for n, end in enumerate((d1_own, d2_own)):
+            d_block[2 * e + n] = totals[2 * e + n][place].astype(f32)
+            ends.append(
+                pltpu.make_async_copy(
+                    d_block.at[2 * e + n], end.at[:, e * wide : (e + 1) * wide],
+                    local.at[2 + 2 * e + n],
+                )
+            )
+    for copy in ends:
+        copy.start()
+    for copy in ends:
+        copy.wait()
+    wire.close()
+
+
+def reduce(dw, d1, d2, vec, out, gx, fsdp, expert_count):
+    size = grid_sizes(fsdp)
+    shape = tuple(size[d] for d in "zycx")
+    rows, wide = d1.shape[-2], d1.shape[-1] // expert_count
+    cols = dw.shape[-1] // 4
+    half, depth = gx.shape[0] // 2, gx.shape[1]
+    draft = Draft(fsdp)
+    reduce_plan(draft, (None,) * 8, None, rows, cols, wide, expert_count, half, depth)
+    return pl.pallas_call(
+        functools.partial(reduce_kernel, fsdp=fsdp, expert_count=expert_count),
+        out_shape=[
+            jax.ShapeDtypeStruct((rows, 4 * cols), f32),
+            jax.ShapeDtypeStruct((rows, expert_count * wide), f32),
+            jax.ShapeDtypeStruct((rows, expert_count * wide), f32),
+            jax.ShapeDtypeStruct(shape + vec.shape, f32),
+            jax.ShapeDtypeStruct((2, 1, half, depth), bf16),
+            jax.ShapeDtypeStruct((2, 1, half, depth), f32),
+        ],
+        in_specs=[ANY] * 6,
+        out_specs=[ANY] * 6,
+        scratch_shapes=[
+            pltpu.SemaphoreType.DMA((draft.used,)),
+            pltpu.SemaphoreType.DMA((draft.used,)),
+            pltpu.SemaphoreType.DMA((3 * (2 * expert_count + 1) + 4,)),
+            pltpu.VMEM((half, depth), f32),
+            pltpu.VMEM((half, depth), bf16),
+            pltpu.VMEM((half, depth), bf16),
+            pltpu.VMEM((rows, 4 * cols), f32),
+            pltpu.VMEM((2 * expert_count, rows, wide), f32),
+        ]
+        + draft.shapes,
+        compiler_params=params(collective_id=1, has_side_effects=True),
+        name="reduce",
+    )(dw, d1, d2, vec, out, gx)
 
 
 def body(
@@ -543,37 +1103,27 @@
     rows, cols = query_weight.shape
     small = attn_gain.shape[0]
     me = lax.axis_index("tp")
-    swap = [(0, 1), (1, 0)]
-
-    def exchange(array):
-        keep = lax.dynamic_index_in_dim(array, me, 0, keepdims=False)
-        give = lax.dynamic_index_in_dim(array, 1 - me, 0, keepdims=False)
-        take = lax.ppermute(give, "tp", swap)
-        return keep, take
-
-    def whole_sequence(array):
-        keep, take = exchange(array[:, 0])
-        return jnp.where(me == 0, jnp.concatenate([keep, take]), jnp.concatenate([take, keep]))
-
-    attn_shard = jnp.concatenate([query_weight, key_weight, value_weight, out_weight_t], axis=1)
     ffn_shape = (rows, expert_count * inner_weight.shape[2])
-    attn_w = lax.all_gather(attn_shard, ("fsdp", "tp")).reshape(fsdp, tp, rows, 4 * cols)
     vectors = jnp.concatenate(
         [attn_gain, ffn_gain, router.T.reshape(-1), bias_table.reshape(-1)]
     )
-    vectors = lax.all_gather(vectors, ("fsdp", "tp"))
-    w1 = lax.all_gather(inner_weight.reshape(ffn_shape), ("fsdp", "tp"))
-    w2 = lax.all_gather(down_weight_t.reshape(ffn_shape), ("fsdp", "tp"))
+    vector_len = vectors.shape[0]
+    padded = -(-vector_len // TILE) * TILE
+    vectors = jnp.broadcast_to(jnp.pad(vectors, (0, padded - vector_len))[None], (8, padded))
+    attn_w, w1, w2, vectors, x, c = gather(
+        query_weight, key_weight, value_weight, out_weight_t, inner_weight.reshape(ffn_shape),
+        down_weight_t.reshape(ffn_shape), vectors, tokens, cotangent, fsdp, expert_count,
+    )
+    attn_w = attn_w.reshape(fsdp, tp, rows, 4 * cols)
     w1 = w1.reshape(fsdp, tp, *ffn_shape)
     w2 = w2.reshape(fsdp, tp, *ffn_shape)
-    x = whole_sequence(tokens)
-    c = whole_sequence(cotangent)
+    vectors = vectors.reshape(fsdp * tp, 8, padded)[:, 0]
     gain_one = vectors[:, :small].reshape(1, depth)
     gain_two = vectors[:, small : 2 * small].reshape(1, depth)
     router_rows = jnp.stack(
         [vectors[:, (2 + e) * small : (3 + e) * small].reshape(depth) for e in range(expert_count)]
     )
-    table = vectors[:tp, (2 + expert_count) * small :].reshape(heads, buckets)
+    table = vectors[:tp, (2 + expert_count) * small : vector_len].reshape(heads, buckets)
     router_cols = jnp.pad(router_rows.T, ((0, 0), (0, TILE - expert_count)))
     router_rows = jnp.pad(router_rows, ((0, 8 - expert_count), (0, 0)))
 
@@ -585,64 +1135,58 @@
     slot_ids = route[:, 0] * capacity + jnp.where(route[:, 0] == 0, rank[:, 0], rank[:, 1])
 
     low_table = table.astype(bf16).astype(f32)
-    offset = jnp.arange(3 * TILE)[None, :] - TILE - jnp.arange(TILE)[:, None]
-    bucket = bucket_of(offset)
-    near = jnp.take(low_table, bucket.reshape(-1), axis=1).reshape(heads, TILE, 3 * TILE)
+    at = jnp.arange(4 * TILE)
+    bucket = bucket_of(jnp.where(at < 3 * TILE, at - TILE, at - 5 * TILE))
+    picker = (bucket[:, None] == jnp.arange(buckets)[None, :]).astype(f32)
     farthest = buckets // 2 - 1
     base = low_table[:, farthest]
-    band = near - base[:, None, None]
+    near = lax.dot_general(
+        low_table, picker, (((1,), (1,)), ((), ())), precision=highest, preferred_element_type=f32
+    )
+    bias = jnp.broadcast_to((near - base[:, None])[:, None, :], (heads, 8, 4 * TILE))
     far = low_table[:, buckets - 1] - base
 
     nrm, q, k, v = project(x, gain_one, attn_w)
-    mixed, rl, p = attend(prefix_len, far, q, k, v, band)
+    mixed, rl, p = attend(prefix_len, far, q, k, v, bias)
     out_w = attn_w[..., 3 * cols :]
     res, nt, prob, xs, gs = dispatch(
         x, c, mixed, out_w, gain_two, router_cols, route, slot_ids[None, :], slots
     )
     y, gb, d1, d2 = experts(xs, gs, w1, w2, expert_count)
-    d1 = lax.psum_scatter(d1.reshape(fsdp * tp, *ffn_shape), ("fsdp", "tp"))
-    d2 = lax.psum_scatter(d2.reshape(fsdp * tp, *ffn_shape), ("fsdp", "tp"))
     out, gres, gmix, dwo, gain_two_part, router_part = combine(
         res, c, nt, prob, route, slot_ids[:, None], y, gb, mixed, out_w, gain_two, router_rows
     )
-    dq, dk, dv, band_grad, far_grad = attend_back(q, k, v, mixed, gmix, rl, p)
-    gx, dw, gain_one_part = finish(x, gain_one, nrm, dq, dk, dv, attn_w, gres)
-    dw = lax.psum_scatter(
-        jnp.concatenate([dw, dwo], axis=-1).reshape(fsdp * tp, rows, 4 * cols), ("fsdp", "tp")
-    ).astype(f32)
-
-    picker = (bucket.reshape(-1)[:, None] == jnp.arange(buckets)[None, :]).astype(f32)
-    table_grad = jnp.dot(
-        band_grad.reshape(heads, -1), picker, precision=highest, preferred_element_type=f32
-    )
-    table_grad = table_grad.at[:, farthest].add(jnp.sum(far_grad[:, 0, :], axis=-1))
-    table_grad = table_grad.at[:, buckets - 1].add(jnp.sum(far_grad[:, 1, :], axis=-1))
+    dq, dk, dv, diag = attend_back(q, k, v, mixed, gmix, rl, p)
+    gx, dw, gain_one_part = finish(x, gain_one, nrm, dq, dk, dv, attn_w, gres, dwo)
+    table_grad = jnp.dot(diag[:, 0], picker, precision=highest, preferred_element_type=f32)
+    table_grad = table_grad.at[:, farthest].add(jnp.sum(diag[:, 1], axis=-1))
+    table_grad = table_grad.at[:, buckets - 1].add(jnp.sum(diag[:, 2], axis=-1))
     sums = jnp.concatenate(
         [gain_one_part[0], gain_two_part[0]]
         + [router_part[e] for e in range(expert_count)]
         + [table_grad.reshape(-1)]
     )
-    sums = lax.psum(sums, ("fsdp", "tp"))
+    sums_len = sums.shape[0]
+    tall = -(-sums_len // (8 * TILE)) * 8
+    sums = jnp.pad(sums, (0, tall * TILE - sums_len)).reshape(tall, TILE)
+    split = (fsdp // grid_sizes(fsdp)["y"] // 2, grid_sizes(fsdp)["y"], 2, tp)
+    dw, d1, d2, sums, out, gx = reduce(
+        dw.reshape(split + dw.shape[2:]), d1.reshape(split + ffn_shape),
+        d2.reshape(split + ffn_shape), sums, out, gx, fsdp, expert_count,
+    )
+    sums = jnp.sum(sums.reshape(fsdp * tp, tall * TILE), axis=0)
     start = (lax.axis_index("fsdp") * tp + me) * small
     own = [
         lax.dynamic_slice_in_dim(sums, n * depth + start, small) for n in range(2 + expert_count)
     ]
     table_own = lax.dynamic_slice_in_dim(
-        sums[(2 + expert_count) * depth :].reshape(heads, buckets), me * heads_here, heads_here
-    )
-
-    def halves(array, kind):
-        array = array.reshape(tp, half_len, depth)
-        keep, take = exchange(array.astype(bf16))
-        keep = lax.dynamic_index_in_dim(array, me, 0, keepdims=False).astype(kind)
-        take = take.astype(kind)
-        both = jnp.where(me == 0, jnp.stack([keep, take]), jnp.stack([take, keep]))
-        return both[:, None]
+        sums[(2 + expert_count) * depth : sums_len].reshape(heads, buckets), me * heads_here, heads_here
+    )
 
     ffn_out = inner_weight.shape
     return (
-        halves(out, bf16),
-        halves(gx, f32),
+        out,
+        gx,
         own[0],
         dw[:, :cols],
         dw[:, cols : 2 * cols],
@@ -651,8 +1195,8 @@
         table_own,
         own[1],
         jnp.stack(own[2:], axis=1),
-        d1.astype(f32).reshape(ffn_out),
-        d2.astype(f32).reshape(ffn_out),
+        d1.reshape(ffn_out),
+        d2.reshape(ffn_out),
     )
 
 

time: 874 us -> 594 us (0.68)
  Pallas kernels: 173 us -> 554 us
  waiting for transfers between devices: 304 us -> 0 us
  local copies, waits for them, and re-layouts: 207 us -> 29 us
  blocking collectives: 131 us -> 0 us
  other arithmetic: 26 us -> 7.47 us
  between operations: 14.9 us -> 0.83 us
    pallas_call x0 -> x2, Pallas kernels: none -> 380 us  [the longest x1 195 us: reduce(): pl.pallas_call(functools.partial(reduce_kernel, fsdp=fsdp, expert_count=e...]
    reduce_scatter x3 -> x0, waiting for transfers between devices: 303 us -> none  [the longest x1 140 us: body(): d2 = lax.psum_scatter(d2.reshape(fsdp * tp, *ffn_shape), ('fsdp', 'tp'))]
    gather x2 -> x0, local copies, waits for them, and re-layouts: 178 us -> none  [body(): jnp.take(low_table, bucket.reshape(-1), axis=1)]
    unnamed x1 -> x0, blocking collectives: 73.6 us -> none
    psum x1 -> x0, blocking collectives: 57 us -> none  [body(): sums = lax.psum(sums, ('fsdp', 'tp'))]
    select_n x5 -> x0, other arithmetic: 9.64 us -> none  [the longest x2 5.01 us: whole_sequence(): jnp.where(me == 0, jnp.concatenate([keep, take]), jnp.concatenate([take,...]
  transfers between devices with their start and end apart: 10 -> 0, of which waited for: 3 -> 0; matrix products, arithmetic and copies ran while one was open for 26% -> 0% of each run, Pallas kernels for 7% -> 0%
where the time goes in v2:
time: 594 us; the launch traced here: 593 us
  Pallas kernels  554 us (93%)
  local copies, waits for them, and re-layouts  29 us (5%)
  other arithmetic  7.47 us (1%)
    pallas_call x1, Pallas kernels, reduce(): pl.pallas_call(functools.partial(reduce_kernel, fsdp=fsdp, expert_count=e...  195 us
    pallas_call x1, Pallas kernels, gather(): pl.pallas_call(functools.partial(gather_kernel, fsdp=fsdp, expert_count=e...  185 us
    pallas_call x1, Pallas kernels, experts(): pl.pallas_call(experts_kernel, grid=(expert_count, halves * per), in_spec...  48.6 us
    pallas_call x1, Pallas kernels, attend_back(): pl.pallas_call(attend_back_kernel, grid=(heads,), in_specs=[pair, pair, p...  29.8 us
    pallas_call x1, Pallas kernels, attend(): pl.pallas_call(attend_kernel, grid=(heads,), in_specs=[SMEM, SMEM, pair,...  28.3 us
    pallas_call x1, Pallas kernels, dispatch(): pl.pallas_call(functools.partial(dispatch_kernel, cols=cols), out_shape=[...  20.7 us
    pallas_call x1, Pallas kernels, finish(): pl.pallas_call(functools.partial(finish_kernel, cols=cols), out_shape=[ja...  19.1 us
    pallas_call x1, Pallas kernels, combine(): pl.pallas_call(functools.partial(combine_kernel, cols=cols), out_shape=[j...  17.2 us

profile of v2, /device:TPU:0, one launch (start us, length us, event | category | flops | bytes accessed | tf_op | source)
XLA Modules:
  0.0 593.1 jit_solution(15414908827370930621)
XLA Ops:
  0.6 0.0 copy-start
  0.7 1.7 copy.63
  2.4 1.7 copy.64
  4.1 0.8 reshape.240
  4.8 0.8 reshape.239
  5.6 0.7 select_maximum_fusion
  6.3 0.6 broadcast_in_dim.10.vec
  7.0 185.2 %gather.1 = (bf16[4,2,2,2,48,1536]{5,4,3,2,1,0:T(8,128)(2,1)}, bf16[4,2,2,2,48,3072]{5,4,3,2,1,0:T(8,128)(2,1)}, bf16[4,2,2,2,48,3072]{5,4,3,2,1,0:T(8,128)(2,1)...) custom-call(bf16[48,384]{1,0:T(8,128)(2,1)} %wq.1, bf16[48,384]{1,0:T(8,128)(2,1)} %wk.1, ...), custom_call_target="tpu_custom_call" | custom-call | tf_op jit(solution)/shard_map/gather/pallas_call | solution.py:827
  192.2 1.0 slice.134
  193.2 0.1 fusion.24
  193.3 0.7 reshape.242.gain_ref
  194.0 10.6 %project.1 = (bf16[1024,768]{1,0:T(8,128)(2,1)}, bf16[1024,768]{1,0:T(8,128)(2,1)}, bf16[1024,768]{1,0:T(8,128)(2,1)}, bf16[1024,768]{1,0:T(8,128)(2,1)}) custom-call(bf16[1024,768]{1,0:T(8,128)(2,1)} %get-tuple-element.77.x_ref, f32[1,768]{1,0:T(1,128)} %reshape.242.gain_ref, bf16[16,2,48,1536]{3,2,1,0:T(8,128)(2,1)} %bitcast.42), custom_call_target="tpu_custom_call" | custom-call | tf_op jit(solution)/shard_map/project/pallas_call | solution.py:68
  204.6 0.0 copy-done
  204.6 0.6 constant_dynamic-slice_fusion.2
  205.2 0.1 slice.163
  205.3 0.1 convert_element_type.84
  205.4 0.2 slice_reduce_fusion.4
  205.5 0.5 sub.23.far_ref
  206.1 0.3 convolution_subtract_fusion
  206.3 0.7 broadcast_in_dim.11.bias_ref
  207.0 28.3 %attend.1 = (bf16[1024,768]{1,0:T(8,128)(2,1)}, f32[1024,128]{1,0:T(8,128)}, bf16[12,1024,1024]{2,1,0:T(8,128)(2,1)}) custom-call(s32[1]{0:T(128)} %bitcast.4.prefix_ref, f32[12]{0:T(128)} %sub.23.far_ref, bf16[1024,768]{1,0:T(8,128)(2,1)} %get-tuple-element.81.q_ref, bf16[1024,768]{1,0:T(8,128)(2,1)} %get-tuple-element.82.k_ref, ...), custom_call_target="tpu_custom_call" | custom-call | tf_op jit(solution)/shard_map/attend/pallas_call | solution.py:147
  235.3 2.4 slice.139.w_ref
  237.7 0.7 reshape.244.gain_ref
  238.4 0.1 stack_reshape.7
  238.5 0.1 stack_reshape.6
  238.6 0.2 copy.62
  238.8 0.8 pad.21.clone.router_ref
  239.6 0.0 copy-done.4
  239.6 0.2 copy.52.route_ref
  239.8 0.0 copy-start.2
  239.9 0.8 fusion.4
  240.7 1.2 slice_reduce_fusion
  241.9 0.6 fusion.15.slot_ref
  242.5 20.7 %dispatch.1 = (f32[1024,768]{1,0:T(8,128)}, bf16[1024,768]{1,0:T(8,128)(2,1)}, f32[1024,128]{1,0:T(8,128)}, bf16[1280,768]{1,0:T(8,128)(2,1)}, bf16[1280,768]{1,0:T(8,128)(2,1)}) custom-call(bf16[1024,768]{1,0:T(8,128)(2,1)} %get-tuple-element.77.x_ref, bf16[1024,768]{1,0:T(8,128)(2,1)} %get-tuple-element.85.c_ref, ...), custom_call_target="tpu_custom_call" | custom-call | tf_op jit(solution)/shard_map/dispatch/pallas_call | solution.py:225
  263.2 48.6 %experts.1 = (bf16[1280,768]{1,0:T(8,128)(2,1)}, bf16[1280,768]{1,0:T(8,128)(2,1)}, bf16[16,2,48,3072]{3,2,1,0:T(8,128)(2,1)}, bf16[16,2,48,3072]{3,2,1,0:T(8,128)(2,1)}) custom-call(bf16[1280,768]{1,0:T(8,128)(2,1)} %get-tuple-element.89.x_ref, bf16[1280,768]{1,0:T(8,128)(2,1)} %get-tuple-element.90.g_ref, bf16[16,2,48,3072]{3,2,1,0:T(8,128)(2,1)} %bitcast.47, ...), custom_call_target="tpu_custom_call" | custom-call | tf_op jit(solution)/shard_map/experts/pallas_call | solution.py:287
  311.8 0.6 pad.22.router_ref
  312.4 17.2 %combine.1 = (bf16[1024,768]{1,0:T(8,128)(2,1)}, f32[1024,768]{1,0:T(8,128)}, bf16[1024,768]{1,0:T(8,128)(2,1)}, bf16[16,2,48,384]{3,2,1,0:T(8,128)(2,1)}, f32[8,768]{1,0:T(8,128)}, /*index=5*/f32[8,768]{1,0:T(8,128)}) custom-call(f32[1024,768]{1,0:T(8,128)} %get-tuple-element.86.res_ref, bf16[1024,768]{1,0:T(8,128)(2,1)} %get-tuple-element.85.c_ref, ...), custom_call_target="tpu_custom_call" | custom-call | tf_op jit(solution)/shard_map/combine/pallas_call | solution.py:362
  329.6 29.8 %attend_back.1 = (bf16[1024,768]{1,0:T(8,128)(2,1)}, bf16[1024,768]{1,0:T(8,128)(2,1)}, bf16[1024,768]{1,0:T(8,128)(2,1)}, f32[12,8,512]{2,1,0:T(8,128)}) custom-call(bf16[1024,768]{1,0:T(8,128)(2,1)} %get-tuple-element.81.q_ref, bf16[1024,768]{1,0:T(8,128)(2,1)} %get-tuple-element.82.k_ref, bf16[1024,768]{1,0:T(8,128)(2,1)} %get-tuple-element.83.v_ref, ...), custom_call_target="tpu_custom_call" | custom-call | tf_op jit(solution)/shard_map/attend_back/pallas_call | solution.py:457
  359.4 19.1 %finish.1 = (f32[1024,768]{1,0:T(8,128)}, bf16[16,2,48,1536]{3,2,1,0:T(8,128)(2,1)}, f32[8,768]{1,0:T(8,128)}) custom-call(bf16[1024,768]{1,0:T(8,128)(2,1)} %get-tuple-element.77.x_ref, f32[1,768]{1,0:T(1,128)} %reshape.242.gain_ref, bf16[1024,768]{1,0:T(8,128)(2,1)} %get-tuple-element.80.nrm_ref, bf16[1024,768]{1,0:T(8,128)(2,1)} %get-tuple-element.98.dq_ref, ...), custom_call_target="tpu_custom_call" | custom-call | tf_op jit(solution)/shard_map/finish/pallas_call | solution.py:525
  378.5 0.8 slice_reduce_fusion.9
  379.2 0.8 slice_reduce_fusion.6
  380.1 1.3 slice_reduce_fusion.2
  381.4 0.3 fusion.10
  381.7 0.1 copy.57
  381.8 0.6 compare_reduce_fusion
  382.4 0.7 add_select_fusion
  383.2 0.1 scatter-add.6
  383.2 0.1 copy.58
  383.3 0.1 slice_add_fusion
  383.4 0.1 scatter-add.9
  383.5 0.1 reshape.252
  383.6 0.6 pad_bitcast_fusion.vec
  384.2 195.0 %reduce.30 = (f32[48,1536]{1,0:T(8,128)}, f32[48,3072]{1,0:T(8,128)}, f32[48,3072]{1,0:T(8,128)}, f32[4,2,2,2,32,128]{5,4,3,2,1,0:T(8,128)}, bf16[2,1,512,768]{3...) custom-call(bf16[4,2,2,2,48,1536]{5,4,3,2,1,0:T(8,128)(2,1)} %bitcast.49, bf16[4,2,2,2,48,3072]{5,4,3,2,1,0:T(8,128)(2,1)} %bitcast.45, ...), custom_call_target="tpu_custom_call" | custom-call | tf_op jit(solution)/shard_map/reduce/pallas_call | solution.py:1063
  579.2 1.1 reduce_sum.31
  580.3 0.6 dynamic-slice_bitcast_fusion.1
  580.9 1.7 fusion.23
  582.6 0.1 slice.133
  582.7 0.6 constant_dynamic-slice_fusion
  583.3 0.6 pad_maximum_fusion.1
  583.9 2.4 reshape.254
  586.2 2.5 reshape.255
  588.8 2.7 copy.80
  591.4 0.0 copy-done.3
  591.4 1.7 copy.81
  (19 shorter events, 0.1 us)
Async XLA Ops:
  0.6 204.0 %copy-start = (s32[2,1]{0,1:T(1,128)S(1)}, s32[2,1]{0,1:T(1,128)}, u32[]{:S(2)}) copy-start(s32[2,1]{0,1:T(1,128)} %param.21) | copy-start | bytes 28
  235.3 4.3 copy-start.4
  239.8 0.9 copy-start.2
  586.2 5.2 copy-start.3
  588.8 4.3 copy-start.1

commit v3 on v2

v3 whole, which is shorter than its diff:
```python
import functools

import jax
import jax.numpy as jnp
from jax import lax
from jax.experimental import pallas as pl
from jax.experimental.pallas import tpu as pltpu
from jax.sharding import PartitionSpec as P

epsilon = 1e-06
masked = -1e30
bucket_edges = (12, 16, 23, 32, 46, 64, 91)
TILE = 128
f32, bf16 = jnp.float32, jnp.bfloat16
highest = lax.Precision.HIGHEST
VMEM = pl.BlockSpec(memory_space=pltpu.VMEM)
SMEM = pl.BlockSpec(memory_space=pltpu.SMEM)
ANY = pl.BlockSpec(memory_space=pl.ANY)


def params(**more):
    return pltpu.CompilerParams(vmem_limit_bytes=60 * 2**20, **more)


def lasts(microseconds):
    return pl.CostEstimate(
        flops=int(microseconds * 1.1e9), transcendentals=0, bytes_accessed=1024
    )


def mm(a, b):
    return lax.dot_general(a, b, (((1,), (0,)), ((), ())), preferred_element_type=f32)


def mm_nt(a, b):
    return lax.dot_general(a, b, (((1,), (1,)), ((), ())), preferred_element_type=f32)


def bucket_of(offset):
    distance = jnp.abs(offset)
    far_bucket = jnp.full_like(distance, 8)
    for edge_value in bucket_edges:
        far_bucket = far_bucket + (distance >= edge_value).astype(jnp.int32)
    near_bucket = jnp.where(distance < 8, distance, far_bucket)
    return near_bucket + 16 * (offset > 0).astype(jnp.int32)


def experts_kernel(
    x_ref, g_ref, w1_ref, w2_ref, y_ref, gb_ref, d1_ref, d2_ref, xt, gt, y_acc, gb_acc
):
    step = pl.program_id(1)
    last = pl.num_programs(1) - 1
    group, _, rows, chunk = w1_ref.shape
    depth = group * rows

    @pl.when(step == 0)
    def _():
        xt[...] = x_ref[...].T
        gt[...] = g_ref[...].T
        y_acc[...] = jnp.zeros_like(y_acc)
        gb_acc[...] = jnp.zeros_like(gb_acc)

    w1 = w1_ref[:, 0].reshape(depth, chunk)
    w2 = w2_ref[:, 0].reshape(depth, chunk)
    inner = mm(x_ref[...], w1)
    hidden = mm(g_ref[...], w2)
    phi = 0.5 + 0.5 * lax.erf(inner * 0.7071067811865476)
    act = (inner * phi).astype(bf16)
    slope = phi + inner * (jnp.exp(inner * inner * -0.5) * 0.3989422804014327)
    grad = (hidden * slope).astype(bf16)
    y_acc[...] += mm_nt(act, w2)
    gb_acc[...] += mm_nt(grad, w1)
    d2_ref[:, 0] = mm(gt[...], act).astype(bf16).reshape(group, rows, chunk)
    d1_ref[:, 0] = mm(xt[...], grad).astype(bf16).reshape(group, rows, chunk)

    @pl.when(step == last)
    def _():
        y_ref[...] = y_acc[...].astype(bf16)
        gb_ref[...] = gb_acc[...].astype(bf16)


def expert(xs, gs, w1, w2, number, expert_count, after):
    slots, depth = xs.shape
    capacity = slots // expert_count
    group, halves, rows, hidden = w1.shape
    chunk = 512
    per = hidden // chunk
    row_block = pl.BlockSpec((capacity, depth), lambda e, s: (number, 0))
    out_block = pl.BlockSpec((capacity, depth), lambda e, s: (0, 0))
    weight_block = pl.BlockSpec(
        (group, 1, rows, chunk), lambda e, s: (0, s // per, 0, lax.rem(s, per))
    )

    def kernel(*refs):
        experts_kernel(*refs[:4], *refs[4 + len(after) :])

    return pl.pallas_call(
        kernel,
        grid=(1, halves * per),
        in_specs=[row_block, row_block, weight_block, weight_block] + [ANY] * len(after),
        out_specs=[out_block, out_block, weight_block, weight_block],
        out_shape=[
            jax.ShapeDtypeStruct((capacity, depth), bf16),
            jax.ShapeDtypeStruct((capacity, depth), bf16),
            jax.ShapeDtypeStruct(w1.shape, bf16),
            jax.ShapeDtypeStruct(w2.shape, bf16),
        ],
        scratch_shapes=[
            pltpu.VMEM((depth, capacity), bf16),
            pltpu.VMEM((depth, capacity), bf16),
            pltpu.VMEM((capacity, depth), f32),
            pltpu.VMEM((capacity, depth), f32),
        ],
        compiler_params=params(),
        cost_estimate=lasts(26),
        name="expert",
    )(xs, gs, w1, w2, *after)


def combine_kernel(
    res_ref, c_ref, nt_ref, prob_ref, route_ref, slot_ref, y0_ref, y1_ref, gb0_ref, gb1_ref, mixed_ref,
    w_ref, gain_ref, router_ref, out_ref, gres_ref, gmix_ref, dwo_ref, gain_part_ref, router_part_ref, gat, *, cols,
):
    length, depth = res_ref.shape
    capacity = y0_ref.shape[0]
    slots = 2 * capacity
    block = 256
    gain_part_ref[...] = jnp.zeros_like(gain_part_ref)
    router_part_ref[...] = jnp.zeros_like(router_part_ref)

    def rows_body(i, _):
        rows = pl.ds(pl.multiple_of(i * block, block), block)
        lane = lax.broadcasted_iota(jnp.int32, (1, slots), 1)
        pick = (slot_ref[rows, :] == lane).astype(bf16)
        y = mm(pick[:, :capacity], y0_ref[...]) + mm(pick[:, capacity:], y1_ref[...])
        gn = mm(pick[:, :capacity], gb0_ref[...]) + mm(pick[:, capacity:], gb1_ref[...])
        res = res_ref[rows, :]
        c = c_ref[rows, :].astype(f32)
        prob = prob_ref[rows, :]
        p0, p1, gate = prob[:, 0:1], prob[:, 1:2], prob[:, 2:3]
        out_ref[rows, :] = (res + gate * y).astype(bf16)
        grad_gate = jnp.sum(c * y, axis=-1, keepdims=True)
        route = route_ref[rows, :]
        gl0 = p0 * (jnp.where(route == 0, 1.0, 0.0) - gate) * grad_gate
        gl1 = p1 * (jnp.where(route == 1, 1.0, 0.0) - gate) * grad_gate
        gn = gn + gl0 * router_ref[0:1, :] + gl1 * router_ref[1:2, :]
        nt = nt_ref[rows, :].astype(f32)
        router_part_ref[0:1, :] += jnp.sum(nt * gl0, axis=0, keepdims=True)
        router_part_ref[1:2, :] += jnp.sum(nt * gl1, axis=0, keepdims=True)
        r = lax.rsqrt(jnp.mean(res * res, axis=-1, keepdims=True) + epsilon)
        n2 = res * r
        gain_part_ref[0:1, :] += jnp.sum(gn * n2, axis=0, keepdims=True)
        g2 = gn * gain_ref[...]
        gres = c + r * (g2 - n2 * jnp.mean(g2 * n2, axis=-1, keepdims=True))
        gres_ref[rows, :] = gres
        ga = gres.astype(bf16)
        gat[:, rows] = ga.T
        for t in range(2):
            w = w_ref[:, t].reshape(depth, cols)
            gmix_ref[rows, t * cols : (t + 1) * cols] = mm(ga, w).astype(bf16)
        return 0

    lax.fori_loop(0, length // block, rows_body, 0)
    group = dwo_ref.shape[0]
    rows = dwo_ref.shape[2]
    for t in range(2):
        d = mm(gat[...], mixed_ref[:, t * cols : (t + 1) * cols])
        dwo_ref[:, t] = d.astype(bf16).reshape(group, rows, cols)


def combine(res, c, nt, prob, route, slot_col, ys, gbs, mixed, w, gain, router_rows):
    length, depth = res.shape
    cols = w.shape[3]
    return pl.pallas_call(
        functools.partial(combine_kernel, cols=cols),
        out_shape=[
            jax.ShapeDtypeStruct((length, depth), bf16),
            jax.ShapeDtypeStruct((length, depth), f32),
            jax.ShapeDtypeStruct((length, depth), bf16),
            jax.ShapeDtypeStruct(w.shape, bf16),
            jax.ShapeDtypeStruct((8, depth), f32),
            jax.ShapeDtypeStruct((8, depth), f32),
        ],
        in_specs=[VMEM] * 14,
        out_specs=[VMEM] * 6,
        scratch_shapes=[pltpu.VMEM((depth, length), bf16)],
        compiler_params=params(),
        cost_estimate=lasts(18),
        name="combine",
    )(res, c, nt, prob, route, slot_col, *ys, *gbs, mixed, w, gain, router_rows)


def attend_back_kernel(
    q_ref, k_ref, v_ref, mixed_ref, g_ref, rl_ref, p_ref,
    dq_ref, dk_ref, dv_ref, diag_ref, kext, qt, dkt, dvt, band_ref,
):
    h = pl.program_id(0)
    length = q_ref.shape[0]
    tiles = length // TILE
    half = lax.rem(h, 2)
    lane = lax.broadcasted_iota(jnp.int32, (1, TILE), 1)
    mine = (lane // 64) == half
    block = 256

    @pl.when(h == 0)
    def _():
        row = lax.broadcasted_iota(jnp.int32, (length, TILE), 0)
        col = lax.broadcasted_iota(jnp.int32, (length, TILE), 1)
        kext[:, TILE:] = (row // TILE == col).astype(bf16)

    @pl.when(half == 0)
    def _():
        kext[:, :TILE] = k_ref[...]
        qt[...] = q_ref[...].T

    band_ref[...] = jnp.zeros_like(band_ref)
    left = jnp.zeros((1, TILE), f32)
    right = jnp.zeros((1, TILE), f32)
    for b in range(length // block):
        rows = slice(b * block, (b + 1) * block)
        rl = jnp.sum(jnp.where(lane == h, rl_ref[rows, :], 0.0), axis=-1, keepdims=True)
        g = jnp.where(mine, g_ref[rows, :].astype(f32) * rl, 0.0)
        delta = jnp.sum(g * mixed_ref[rows, :].astype(f32), axis=-1, keepdims=True)
        g = g.astype(bf16)
        gp = mm_nt(g, v_ref[...])
        p = p_ref[0, rows, :]
        ds = p.astype(f32) * (gp - delta)
        low = ds.astype(bf16)
        dq = mm(low, kext[...])
        dq_ref[rows, :] = jnp.where(mine, (dq[:, :TILE] * 0.125).astype(bf16), dq_ref[rows, :])
        gv = mm(g.T, p)
        gk = mm(qt[:, rows], low)
        if b == 0:
            dvt[...] = gv
            dkt[...] = gk
        else:
            dvt[...] += gv
            dkt[...] += gk
        for part in range(block // TILE):
            i = b * (block // TILE) + part
            sums = dq[part * TILE : (part + 1) * TILE, TILE:]
            sums = jnp.sum(sums, axis=0, keepdims=True)
            left = left + jnp.where(lane <= i - 2, sums, 0.0)
            right = right + jnp.where(lane >= i + 2, sums, 0.0)
            for side in (-1, 0, 1):
                j = i + side
                if 0 <= j < tiles:
                    band_ref[:, (side + 1) * TILE : (side + 2) * TILE] += ds[
                        part * TILE : (part + 1) * TILE, j * TILE : (j + 1) * TILE
                    ]
    turned = band_ref[0:8, :]
    for g in range(1, TILE // 8):
        turned = turned + pltpu.roll(band_ref[8 * g : 8 * g + 8, :], 4 * TILE - 8 * g, 1)
    diag = turned[0:1, :]
    for r in range(1, 8):
        diag = diag + pltpu.roll(turned[r : r + 1, :], 4 * TILE - r, 1)
    diag_ref[0] = jnp.zeros((8, 4 * TILE), f32)
    diag_ref[0, 0:1, :] = diag
    diag_ref[0, 1:2, :TILE] = left
    diag_ref[0, 2:3, :TILE] = right
    dk_ref[...] = jnp.where(mine, dkt[...].T.astype(bf16), dk_ref[...])
    dv_ref[...] = jnp.where(mine, dvt[...].T.astype(bf16), dv_ref[...])


def attend_back(q, k, v, mixed, g, rl, p):
    length, width = q.shape
    heads = p.shape[0]
    pair = pl.BlockSpec((length, TILE), lambda h: (0, h // 2))
    shape = jax.ShapeDtypeStruct((length, width), bf16)
    return pl.pallas_call(
        attend_back_kernel,
        grid=(heads,),
        in_specs=[
            pair, pair, pair, pair, pair,
            pl.BlockSpec((length, TILE), lambda h: (0, 0)),
            pl.BlockSpec((1, length, length), lambda h: (h, 0, 0)),
        ],
        out_specs=[
            pair, pair, pair,
            pl.BlockSpec((1, 8, 4 * TILE), lambda h: (h, 0, 0)),
        ],
        out_shape=[
            shape, shape, shape,
            jax.ShapeDtypeStruct((heads, 8, 4 * TILE), f32),
        ],
        scratch_shapes=[
            pltpu.VMEM((length, 2 * TILE), bf16),
            pltpu.VMEM((TILE, length), bf16),
            pltpu.VMEM((TILE, length), f32),
            pltpu.VMEM((TILE, length), f32),
            pltpu.VMEM((TILE, 4 * TILE), f32),
        ],
        compiler_params=params(),
        cost_estimate=lasts(30),
        name="attend_back",
    )(q, k, v, mixed, g, rl, p)


def finish_kernel(
    x_ref, gain_ref, nrm_ref, dq_ref, dk_ref, dv_ref, w_ref, gres_ref, dwo_ref,
    gx_ref, dw_ref, gain_part_ref, nt, *, cols,
):
    length, depth = x_ref.shape
    group, _, rows_per, _ = dw_ref.shape
    block = 256
    gain_part_ref[...] = jnp.zeros_like(gain_part_ref)
    nt[...] = nrm_ref[...].T
    dw_ref[:, :, :, 3 * cols :] = dwo_ref[...]
    for t in range(2):
        at = slice(t * cols, (t + 1) * cols)
        for n, ref in enumerate((dq_ref, dk_ref, dv_ref)):
            d = mm(nt[...], ref[:, at]).astype(bf16)
            dw_ref[:, t, :, n * cols : (n + 1) * cols] = d.reshape(group, rows_per, cols)

    def rows_body(i, _):
        rows = pl.ds(pl.multiple_of(i * block, block), block)
        gn = jnp.zeros((block, depth), f32)
        for t in range(2):
            w = w_ref[:, t].reshape(depth, 4 * cols)
            at = slice(t * cols, (t + 1) * cols)
            for n, ref in enumerate((dq_ref, dk_ref, dv_ref)):
                gn = gn + mm_nt(ref[rows, at], w[:, n * cols : (n + 1) * cols])
        x = x_ref[rows, :].astype(f32)
        r = lax.rsqrt(jnp.mean(x * x, axis=-1, keepdims=True) + epsilon)
        n1 = x * r
        gain_part_ref[0:1, :] += jnp.sum(gn * n1, axis=0, keepdims=True)
        g1 = gn * gain_ref[...]
        gx_ref[rows, :] = gres_ref[rows, :] + r * (
            g1 - n1 * jnp.mean(g1 * n1, axis=-1, keepdims=True)
        )
        return 0

    lax.fori_loop(0, length // block, rows_body, 0)


def finish(x, gain, nrm, dq, dk, dv, w, gres, dwo):
    length, depth = x.shape
    cols = w.shape[3] // 4
    return pl.pallas_call(
        functools.partial(finish_kernel, cols=cols),
        out_shape=[
            jax.ShapeDtypeStruct((length, depth), f32),
            jax.ShapeDtypeStruct(w.shape, bf16),
            jax.ShapeDtypeStruct((8, depth), f32),
        ],
        in_specs=[VMEM] * 9,
        out_specs=[VMEM] * 3,
        scratch_shapes=[pltpu.VMEM((depth, length), bf16)],
        compiler_params=params(),
        cost_estimate=lasts(19),
        name="finish",
    )(x, gain, nrm, dq, dk, dv, w, gres, dwo)


def grid_sizes(fsdp):
    ny = 2 if fsdp <= 16 else 4
    return {"z": fsdp // (2 * ny), "y": ny, "c": 2, "x": 2}


class Grid:
    def __init__(self, fsdp):
        self.size = grid_sizes(fsdp)
        ny = self.size["y"]
        i = lax.axis_index("fsdp")
        self.at = {
            "z": i // (2 * ny),
            "y": lax.rem(i // 2, ny),
            "c": lax.rem(i, 2),
            "x": lax.axis_index("tp"),
        }

    def device(self, dim, to):
        at = dict(self.at)
        at[dim] = to
        return ((at["z"] * self.size["y"] + at["y"]) * 2 + at["c"], at["x"])

    def enter(self):
        barrier = pltpu.get_barrier_semaphore()

        def greet(device):
            pl.semaphore_signal(barrier, inc=1, device_id=device, device_id_type=pl.DeviceIdType.MESH)

        count = 0
        for dim in "czyx":
            n, me = self.size[dim], self.at[dim]
            if n == 2:
                greet(self.device(dim, 1 - me))
                count = count + 1
            elif n > 2:
                run(me > 0, functools.partial(greet, self.device(dim, me - 1)))
                run(me < n - 1, functools.partial(greet, self.device(dim, me + 1)))
                count = count + (me > 0).astype(jnp.int32) + (me < n - 1).astype(jnp.int32)
        pl.semaphore_wait(barrier, count)


def run(when, act):
    if when is None:
        act()
    else:
        pl.when(when)(act)


class Draft:
    def __init__(self, fsdp):
        self.size = grid_sizes(fsdp)
        self.at = dict.fromkeys("zycx", 0)
        self.used, self.credits, self.shapes = 0, 0, []

    def pick(self):
        self.used += 1

    def pick_credit(self):
        self.credits += 1

    def buffer(self, shape, kind):
        self.shapes.append(pltpu.VMEM(shape, kind))


class Wire:
    def __init__(self, grid, sends, receives, credit=None, buffers=()):
        self.grid, self.sends, self.receives = grid, sends, receives
        self.size, self.at = grid.size, grid.at
        self.used, self.closing, self.buffers = 0, False, list(buffers)
        self.credit, self.credits = credit, 0

    def pick(self):
        self.used += 1
        return self.used - 1

    def pick_credit(self):
        self.credits += 1
        return self.credits - 1

    def give(self, dim, to, number):
        pl.semaphore_signal(
            self.credit.at[number], inc=1, device_id=self.grid.device(dim, to),
            device_id_type=pl.DeviceIdType.MESH,
        )

    def buffer(self, shape, kind):
        return self.buffers.pop(0)

    def send(self, src, dst, dim, to, sem, when=None, credit=None):
        copy = pltpu.make_async_remote_copy(
            src_ref=src, dst_ref=dst, send_sem=self.sends.at[sem], recv_sem=self.receives.at[sem],
            device_id=self.grid.device(dim, to), device_id_type=pl.DeviceIdType.MESH,
        )

        def act():
            if self.closing:
                copy.wait_send()
            else:
                if credit is not None:
                    pl.semaphore_wait(self.credit.at[credit], 1)
                copy.start()

        run(when, act)

    def wait(self, dst, sem, when=None):
        copy = pltpu.make_async_remote_copy(
            src_ref=dst, dst_ref=dst, send_sem=self.sends.at[sem], recv_sem=self.receives.at[sem],
            device_id=self.grid.device("x", 1 - self.at["x"]), device_id_type=pl.DeviceIdType.MESH,
        )
        run(when, copy.wait_recv)

    def close(self, chains):
        self.closing = True
        for _, phases in chains:
            for phase in phases:
                phase[2]()


link_rate = {"z": 87e3, "y": 87e3, "x": 87e3, "c": 300e3}
link_delay = 2.0


def schedule(chains, room=3, want_ends=False):
    here = [0] * len(chains)
    begun = [False] * len(chains)
    free = dict.fromkeys(link_rate, 0.0)
    busy = dict.fromkeys(link_rate, 0)
    flying, acts, now = [], [], 0.0
    ends = [0.0] * len(chains)

    def opens(n):
        phase = chains[n][1][here[n]]
        return phase[4] if len(phase) > 4 else 0.0

    def rest(n):
        return sum(p[1] / link_rate[p[0]] + link_delay for p in chains[n][1][here[n] :])

    while True:
        for dim in link_rate:
            while busy[dim] < room:
                able = [
                    n
                    for n in range(len(chains))
                    if not begun[n] and here[n] < len(chains[n][1])
                    and chains[n][1][here[n]][0] == dim and opens(n) <= now
                ]
                if not able:
                    break
                n = min(able, key=lambda n: (chains[n][0], -rest(n), n))
                phase = chains[n][1][here[n]]
                free[dim] = max(now, free[dim]) + phase[1] / link_rate[dim]
                flying.append((free[dim] + link_delay, n))
                acts.append((now, phase[2]))
                busy[dim] += 1
                begun[n] = True
        later = [
            opens(n)
            for n in range(len(chains))
            if not begun[n] and here[n] < len(chains[n][1]) and opens(n) > now
        ]
        if not flying and not later:
            return (acts, ends) if want_ends else acts
        flying.sort()
        if later and (not flying or min(later) < flying[0][0]):
            now = min(later)
            continue
        now, n = flying.pop(0)
        phase = chains[n][1][here[n]]
        acts.append((now, phase[3]))
        busy[phase[0]] -= 1
        begun[n] = False
        here[n] += 1
        ends[n] = now


def spot(fixed, at, dim, slot):
    return tuple(
        slot if d == dim else at[d] if d in fixed else slice(None) for d in "zycx"
    )


def gather_chain(wire, full, columns, width, order):
    phases = []
    todo = [d for d in order + "c" if wire.size[d] > 1]
    bytes_here = width * 2 * 2

    def look(fixed, dim, slot):
        return full.at[spot(fixed, wire.at, dim, slot) + (slice(None), columns)]

    for n_dim, dim in enumerate(todo):
        n, me = wire.size[dim], wire.at[dim]
        view = functools.partial(look, todo[n_dim:], dim)
        cost = bytes_here if dim != "c" else bytes_here // 2
        if n == 2:
            sem = wire.pick()

            def start(view=view, dim=dim, me=me, sem=sem):
                wire.send(view(me), view(me), dim, 1 - me, sem)

            def finish(view=view, me=me, sem=sem):
                wire.wait(view(1 - me), sem)

            phases.append((dim, cost, start, finish))
        else:
            for hop in range(1, n):
                up, down = wire.pick(), wire.pick()

                def start(view=view, dim=dim, n=n, me=me, hop=hop, up=up, down=down):
                    low, high = me - (hop - 1), me + (hop - 1)
                    wire.send(view(low), view(low), dim, me + 1, up, (me + 1 < n) & (low >= 0))
                    wire.send(view(high), view(high), dim, me - 1, down, (me > 0) & (high < n))

                def finish(view=view, n=n, me=me, hop=hop, up=up, down=down):
                    wire.wait(view(me - hop), up, me - hop >= 0)
                    wire.wait(view(me + hop), down, me + hop < n)

                phases.append((dim, cost, start, finish))
        bytes_here *= n
    return phases


def swap_chain(wire, pairs, size):
    phases = []
    for src, dst, mine in pairs:
        sem = wire.pick()

        def start(src=src, dst=dst, sem=sem):
            wire.send(src, dst, "x", 1 - wire.at["x"], sem)

        def finish(mine=mine, sem=sem):
            wire.wait(mine, sem)

        phases.append(("x", size, start, finish))
    return phases


def parts_of(start, width):
    tiles = width // TILE
    small = max(tiles // 6, 1)
    large = (tiles - small) // 2
    edges = [start, start + large * TILE, start + (large + small) * TILE, start + width]
    return [slice(a, b) for a, b in zip(edges, edges[1:])]


ORDERS = ("zyx", "xyz", "xzy")


def gather_group(wire, full, start, width, rows, rank):
    return [
        (rank, gather_chain(wire, full, at, rows * (at.stop - at.start), order))
        for at, order in zip(parts_of(start, width), ORDERS)
    ]


def gather_plan(wire, refs, rows, cols, widths, half, depth):
    attn, vec, table, tokens, x_all, cotangent, c_all, *wide = refs
    chains = [(0, gather_chain(wire, vec, slice(None), 2 * 8 * depth, "zyx"))]
    x = wire.at["x"]
    pair = (None,) * 3 if table is None else (table.at[x], table.at[x], table.at[1 - x])
    chains.append((0, swap_chain(wire, [pair], 4 * 8 * TILE)))
    chains += gather_group(wire, attn, 0, 4 * cols, rows, 0)
    for rank, src, dst in ((0, tokens, x_all), (3, cotangent, c_all)):
        pairs = [(None, None, None)] * 2
        if src is not None:
            piece = half // 2
            pairs = []
            for n in range(2):
                own = pl.ds(pl.multiple_of(x * half + n * piece, piece), piece)
                other = pl.ds(pl.multiple_of((1 - x) * half + n * piece, piece), piece)
                pairs.append(
                    (src.at[1 - x, 0, pl.ds(n * piece, piece)], dst.at[own], dst.at[other])
                )
        chains += [(rank, swap_chain(wire, [pair], 2 * half * depth)) for pair in pairs]
    for n, (full, width) in enumerate(zip(wide, widths)):
        chains += gather_group(wire, full, 0, width, rows, 1 + n)
    return chains


class Agenda:
    def __init__(self, acts):
        self.acts, self.now = list(acts), 0.0

    def until(self, time):
        self.now = max(self.now, time)
        due = [act for at, act in self.acts if at <= self.now]
        self.acts = [(at, act) for at, act in self.acts if at > self.now]
        return due

    def catch_up(self, time):
        for act in self.until(time):
            act()

    def loop(self, count, lasts_each, body):
        due = []
        for _ in range(count):
            due.append(self.until(self.now))
            self.now += lasts_each

        def turn(i, _):
            for n, acts in enumerate(due):
                if acts:

                    @pl.when(i == n)
                    def _(acts=acts):
                        for act in acts:
                            act()

            body(i)
            return 0

        lax.fori_loop(0, count, turn, 0)


def forward_kernel(*refs, fsdp, wide, heads, slots):
    wq, wk, wv, wo, vec, table, tokens, cotangent, prefix_ref, route_ref, slot_ref, picker_ref = refs[:12]
    shards, refs = refs[12 : 12 + wide], refs[12 + wide :]
    (
        attn_all, vec_sum, x_all, c_all, nrm_ref, q_ref, k_ref, v_ref, mixed_ref, rl_ref, p_all,
        res_ref, nt_ref, prob_ref, xs_ref, gs_ref,
    ) = refs[:16]
    alls, refs = refs[16 : 16 + wide], refs[16 + wide :]
    sends, receives, local, vec_all, tables, bias, vext, p_two, low_ref = refs
    grid = Grid(fsdp)
    wire = Wire(grid, sends, receives)
    here = tuple(grid.at[d] for d in "zycx")
    rows_per, cols = wq.shape
    half_len, depth = tokens.shape[2], tokens.shape[3]
    length = 2 * half_len
    x_at = grid.at["x"]
    own_rows = pl.ds(pl.multiple_of(x_at * half_len, half_len), half_len)
    moves = [(tokens.at[x_at, 0], x_all.at[own_rows]), (cotangent.at[x_at, 0], c_all.at[own_rows])]
    moves += [(shard, full.at[here]) for shard, full in zip(shards, alls)]
    copies = [pltpu.make_async_copy(a, b, local.at[n]) for n, (a, b) in enumerate(moves)]
    for copy in copies:
        copy.start()
    for n, ref in enumerate((wq, wk, wv, wo)):
        attn_all[here + (slice(None), slice(n * cols, (n + 1) * cols))] = ref[...]
    vec_all[here] = vec[...]
    tables[x_at] = table[...]
    grid.enter()
    for copy in copies:
        copy.wait()
    chains = gather_plan(
        wire, (attn_all, vec_all, tables, tokens, x_all, cotangent, c_all, *alls),
        rows_per, cols, [shard.shape[1] for shard in shards], half_len, depth,
    )
    acts, ends = schedule(chains, 3, True)
    agenda = Agenda(acts)
    agenda.catch_up(max(end for (rank, _), end in zip(chains, ends) if rank == 0))

    total = vec_all[0, 0, 0, 0]
    for z in range(grid.size["z"]):
        for y in range(grid.size["y"]):
            for c in range(2):
                for t in range(2):
                    if z + y + c + t:
                        total = total + vec_all[z, y, c, t]
    vec_sum[...] = total
    here_heads = heads // 2
    for t in range(2):
        near = mm(tables[t].astype(bf16), picker_ref[...])
        near = near - near[:, 0:1]
        for n in range(here_heads):
            bias[t * here_heads + n] = jnp.broadcast_to(near[n : n + 1, :], (8, 4 * TILE))

    block = 256
    lane = lax.broadcasted_iota(jnp.int32, (1, TILE), 1)

    def project(i):
        rows = pl.ds(pl.multiple_of(i * block, block), block)
        x = x_all[rows, :].astype(f32)
        r = lax.rsqrt(jnp.mean(x * x, axis=-1, keepdims=True) + epsilon)
        n = (x * r * vec_sum[0:1, :]).astype(bf16)
        nrm_ref[rows, :] = n
        for t in range(2):
            w = attn_all[:, :, :, t].reshape(depth, 4 * cols)
            at = slice(t * cols, (t + 1) * cols)
            q_ref[rows, at] = mm(n, w[:, :cols]).astype(bf16) * 0.125
            k_ref[rows, at] = mm(n, w[:, cols : 2 * cols]).astype(bf16)
            v_ref[rows, at] = mm(n, w[:, 2 * cols : 3 * cols]).astype(bf16)

    agenda.loop(length // block, 2.6, project)

    tiles = length // TILE
    prefix = prefix_ref[0]
    key = lax.broadcasted_iota(jnp.int32, (1, length), 1)
    hidden = jnp.where(key < prefix, 0.0, masked)
    tri = jnp.where(
        lax.broadcasted_iota(jnp.int32, (TILE, TILE), 1)
        <= lax.broadcasted_iota(jnp.int32, (TILE, TILE), 0),
        0.0,
        masked,
    )
    vext[:, TILE:] = jnp.ones((length, TILE), bf16)

    def stash(h):
        return pltpu.make_async_copy(
            p_two.at[lax.rem(h, 2)], p_all.at[h], local.at[len(moves) + lax.rem(h, 2)]
        )

    def attend(h):
        two = lax.rem(h, 2)
        mine = (lane // 64) == two
        pair = pl.ds(pl.multiple_of((h // 2) * TILE, TILE), TILE)

        @pl.when(h >= 2)
        def _():
            stash(h - 2).wait()

        vext[:, :TILE] = v_ref[:, pair]
        row = bias[h, 0:1, :]
        band = pltpu.roll(jnp.broadcast_to(row, (TILE, 4 * TILE)), 0, 1, stride=1, stride_axis=0)
        beyond = hidden + row[:, 3 * TILE - 1 : 3 * TILE]
        keys = k_ref[:, pair]
        for b in range(length // block):
            rows = slice(b * block, (b + 1) * block)
            q = jnp.where(mine, q_ref[rows, pair], jnp.zeros((), bf16))
            s = mm_nt(q, keys)
            for part in range(2):
                i = b * 2 + part
                pieces = []
                for j in range(tiles):
                    at = slice(j * TILE, (j + 1) * TILE)
                    piece = s[part * TILE : (part + 1) * TILE, at]
                    if j == i - 1:
                        piece = piece + band[:, :TILE]
                    elif j == i:
                        piece = piece + (
                            band[:, TILE : 2 * TILE] + jnp.maximum(tri, hidden[:, at])
                        )
                    elif j == i + 1:
                        piece = piece + (band[:, 2 * TILE : 3 * TILE] + hidden[:, at])
                    elif j > i:
                        piece = piece + beyond[:, at]
                    pieces.append(piece)
                top = functools.reduce(jnp.maximum, pieces)
                top = jnp.max(top, axis=-1, keepdims=True)
                for j in range(tiles):
                    at = slice(j * TILE, (j + 1) * TILE)
                    p_two[two, i * TILE : (i + 1) * TILE, at] = jnp.exp(pieces[j] - top).astype(
                        bf16
                    )
            o = mm(p_two[two, rows, :], vext[...])
            rl = 1.0 / o[:, TILE:]
            out = (o[:, :TILE] * rl).astype(bf16)
            mixed_ref[rows, pair] = jnp.where(mine, out, mixed_ref[rows, pair])
            rl_ref[rows, :] = jnp.where(lane == h, rl, rl_ref[rows, :])
        stash(h).start()

    agenda.loop(heads, 2.4, attend)

    def residual(i):
        rows = pl.ds(pl.multiple_of(i * block, block), block)
        attended = jnp.zeros((block, depth), f32)
        for t in range(2):
            w = attn_all[:, :, :, t].reshape(depth, 4 * cols)[:, 3 * cols :]
            attended = attended + mm_nt(mixed_ref[rows, t * cols : (t + 1) * cols], w)
        res = x_all[rows, :].astype(f32) + attended
        res_ref[rows, :] = res
        r = lax.rsqrt(jnp.mean(res * res, axis=-1, keepdims=True) + epsilon)
        nt = (res * r * vec_sum[1:2, :]).astype(bf16)
        nt_ref[rows, :] = nt
        logits = lax.dot_general(
            nt.astype(f32), vec_sum[...], (((1,), (1,)), ((), ())),
            precision=highest, preferred_element_type=f32,
        )
        first, second = logits[:, 2:3], logits[:, 3:4]
        top = jnp.maximum(first, second)
        a, b = jnp.exp(first - top), jnp.exp(second - top)
        p0, p1 = a / (a + b), b / (a + b)
        gate = jnp.where(route_ref[rows, :] == 0, p0, p1)
        prob_ref[rows, :] = jnp.where(lane == 0, p0, jnp.where(lane == 1, p1, gate))
        low_ref[rows, :] = (gate * c_all[rows, :].astype(f32)).astype(bf16)

    agenda.catch_up(max(end for (rank, chain), end in zip(chains, ends) if rank == 3 and len(chain) == 1))
    agenda.loop(length // block, 3.0, residual)
    step = 320

    def sort(i):
        at = pl.multiple_of(i * step, 64)
        place = lax.broadcasted_iota(jnp.int32, (step, 1), 0) + at
        pick = (slot_ref[...] == place).astype(bf16)
        xs_ref[pl.ds(at, step), :] = mm(pick, nt_ref[...]).astype(bf16)
        gs_ref[pl.ds(at, step), :] = mm(pick, low_ref[...]).astype(bf16)

    agenda.loop(slots // step, 2.2, sort)
    agenda.catch_up(1e9)
    stash(heads - 2).wait()
    stash(heads - 1).wait()
    wire.close(chains)


def forward(squares, vec, table, tokens, cotangent, prefix, route, slot_row, picker, shards, fsdp, heads, slots):
    size = grid_sizes(fsdp)
    shape = tuple(size[d] for d in "zycx")
    rows, cols = squares[0].shape
    half, depth = tokens.shape[2], tokens.shape[3]
    length = 2 * half
    wide = len(shards)
    draft = Draft(fsdp)
    gather_plan(
        draft, (None,) * (7 + wide), rows, cols, [shard.shape[1] for shard in shards], half, depth
    )
    low = jax.ShapeDtypeStruct((length, depth), bf16)
    return pl.pallas_call(
        functools.partial(forward_kernel, fsdp=fsdp, wide=wide, heads=heads, slots=slots),
        out_shape=[
            jax.ShapeDtypeStruct(shape + (rows, 4 * cols), bf16),
            jax.ShapeDtypeStruct(vec.shape, f32),
            low, low, low, low, low, low, low,
            jax.ShapeDtypeStruct((length, TILE), f32),
            jax.ShapeDtypeStruct((heads, length, length), bf16),
            jax.ShapeDtypeStruct((length, depth), f32),
            low,
            jax.ShapeDtypeStruct((length, TILE), f32),
            jax.ShapeDtypeStruct((slots, depth), bf16),
            jax.ShapeDtypeStruct((slots, depth), bf16),
        ]
        + [jax.ShapeDtypeStruct(shape + shard.shape, bf16) for shard in shards],
        in_specs=[VMEM] * 6 + [ANY] * 2 + [SMEM] + [VMEM] * 3 + [VMEM] * wide,
        out_specs=[VMEM] * 10 + [ANY] + [VMEM] * 5 + [ANY] * wide,
        scratch_shapes=[
            pltpu.SemaphoreType.DMA((draft.used,)),
            pltpu.SemaphoreType.DMA((draft.used,)),
            pltpu.SemaphoreType.DMA((4 + wide,)),
            pltpu.VMEM(shape + vec.shape, f32),
            pltpu.VMEM((2,) + table.shape, f32),
            pltpu.VMEM((heads, 8, 4 * TILE), f32),
            pltpu.VMEM((length, 2 * TILE), bf16),
            pltpu.VMEM((2, length, length), bf16),
            pltpu.VMEM((length, depth), bf16),
        ],
        compiler_params=params(collective_id=0, has_side_effects=True),
        cost_estimate=lasts(120),
        name="forward",
    )(*squares, vec, table, tokens, cotangent, prefix, route, slot_row, picker, *shards)


def add_into(total, index, part):
    lead = next((n for n, i in enumerate(index[:3]) if isinstance(i, slice)), None)
    if lead is None:
        total[index] = total[index] + part[...]
        return

    def body(n, _):
        at = index[:lead] + (n,) + index[lead + 1 :]
        total[at] = total[at] + part[n]
        return 0

    lax.fori_loop(0, total.shape[lead], body, 0)


def reduce_chain(wire, jobs, columns, total, rows, sem_load, order):
    width = columns.stop - columns.start
    size, at = wire.size, wire.at
    bytes_all = rows * width * 2 * size["z"] * size["y"] * size["x"]
    todo = [d for d in order if size[d] > 1]
    links = [("c", "", [size[d] for d in "zyx"])]
    done = ""
    for dim in todo:
        links.append((dim, done, [size[d] for d in "zyx" if d != dim and d not in done]))
        done += dim
    slots = []
    for dim, _, lead in links:
        n = size[dim]
        many = 1 if n == 2 else 2 * (n - 1)
        shape = tuple(lead) if n == 2 else (many,) + tuple(lead)
        incoming = wire.buffer(shape + (rows, width), bf16)
        slots.append((incoming, [(wire.pick(), wire.pick_credit()) for _ in range(many)]))

    def block(done, dim, slot):
        lead = tuple(
            slot if d == dim else at[d] if d in done else slice(None) for d in "zyx"
        )
        return lead + (slice(None), columns)

    chain = []
    for number, (grads, use, earliest) in enumerate(jobs):
        first, final = number == 0, number == len(jobs) - 1
        phases = []
        incoming, [(sem, credit)] = slots[0]

        def load(grads=grads):
            return pltpu.make_async_copy(
                grads.at[:, :, at["c"], :, :, columns], total.at[:, :, :, :, columns], sem_load
            )

        def start(grads=grads, load=load, first=first, incoming=incoming, sem=sem, credit=credit):
            c = at["c"]
            if not wire.closing:
                load().start()
            wire.send(
                grads.at[:, :, 1 - c, :, :, columns], incoming, "c", 1 - c, sem,
                credit=None if first else credit,
            )

        def finish(load=load, final=final, incoming=incoming, sem=sem, credit=credit):
            load().wait()
            wire.wait(incoming, sem)
            add_into(total, block("", None, None), incoming)
            if not final:
                wire.give("c", 1 - at["c"], credit)

        phases.append(("c", bytes_all, start, finish, earliest))
        cost = 2 * bytes_all
        for (dim, done, _), (incoming, marks) in zip(links[1:], slots[1:]):
            n, me = size[dim], at[dim]
            look = functools.partial(block, done, dim)
            cost //= n
            if n == 2:
                [(sem, credit)] = marks

                def start(look=look, dim=dim, me=me, sem=sem, credit=credit, incoming=incoming, first=first):
                    wire.send(
                        total.at[look(1 - me)], incoming, dim, 1 - me, sem,
                        credit=None if first else credit,
                    )

                def finish(look=look, dim=dim, me=me, sem=sem, credit=credit, incoming=incoming, final=final):
                    wire.wait(incoming, sem)
                    add_into(total, look(me), incoming)
                    if not final:
                        wire.give(dim, 1 - me, credit)

                phases.append((dim, cost, start, finish))
                continue
            for t in range(n - 1):
                up, down = marks[t], marks[n - 1 + t]

                def start(look=look, dim=dim, n=n, me=me, t=t, up=up, down=down, incoming=incoming, first=first):
                    wire.send(
                        total.at[look(n - 1 - t + me)], incoming.at[t], dim, me + 1, up[0],
                        me <= t, None if first else up[1],
                    )
                    back = n - 1 - me
                    wire.send(
                        total.at[look(t - back)], incoming.at[n - 1 + t], dim, me - 1, down[0],
                        back <= t, None if first else down[1],
                    )

                def finish(look=look, dim=dim, n=n, me=me, t=t, up=up, down=down, incoming=incoming, final=final):
                    back = n - 1 - me

                    def take_up():
                        wire.wait(incoming.at[t], up[0])
                        add_into(total, look(n - 2 - t + me), incoming.at[t])
                        if not final:
                            wire.give(dim, me - 1, up[1])

                    def take_down():
                        wire.wait(incoming.at[n - 1 + t], down[0])
                        add_into(total, look(t + 1 - back), incoming.at[n - 1 + t])
                        if not final:
                            wire.give(dim, me + 1, down[1])

                    run((me > 0) & (me - 1 <= t), take_up)
                    run((back > 0) & (back - 1 <= t), take_down)

                phases.append((dim, cost, start, finish))
        last = phases[-1]

        def end(last=last, phases=tuple(phases), use=use):
            last[3]()
            wire.closing = True
            for phase in phases:
                phase[2]()
            wire.closing = False
            use(columns, total[at["z"], at["y"], at["x"], :, columns])

        phases[-1] = last[:3] + (end,) + last[4:]
        chain += phases
    return chain


def reduce_groups(wire, jobs, width, rows, local):
    size = wire.size
    chains = []
    for half in range(min(2, len(jobs))):
        total = wire.buffer((size["z"], size["y"], size["x"], rows, width), bf16)
        for n, (columns, order) in enumerate(zip(parts_of(0, width), ORDERS)):
            sem = None if local is None else local.at[3 * half + n]
            chains.append(
                (half, reduce_chain(wire, jobs[half::2], columns, total, rows, sem, order[::-1]))
            )
    return chains


def reduce_plan(wire, refs, local, rows, width, count, half, depth):
    vec, out, out_end, low, low_in, *grads = refs
    chains = reduce_groups(wire, grads if vec is not None else [(None, None, 0.0)] * count, width, rows, local)
    chains.append((0, gather_chain(wire, vec, slice(None), 16 * TILE, "zyx")))
    pairs = [(None, None, None)] * 2
    if out is not None:
        x = wire.at["x"]
        other = pl.ds(pl.multiple_of((1 - x) * half, half), half)
        pairs = [
            (out.at[other], out_end.at[x, 0], out_end.at[1 - x, 0]),
            (low, low_in, low_in),
        ]
    chains += [(rank, swap_chain(wire, [pair], 4 * half * depth)) for rank, pair in enumerate(pairs)]
    return chains


def reduce_kernel(*refs, fsdp, wide):
    dw, vec, out, gx = refs[:4]
    grads = refs[4 : 4 + wide]
    dw_own, vec_all, out_end, gx_end = refs[4 + wide : 8 + wide]
    owns = refs[8 + wide : 8 + 2 * wide]
    sends, receives, local, credit, low, low_in, *buffers = refs[8 + 2 * wide :]
    grid = Grid(fsdp)
    wire = Wire(grid, sends, receives, credit, buffers)
    at = grid.at
    rows, width = dw_own.shape
    half, depth = gx_end.shape[2], gx_end.shape[3]
    x = at["x"]
    here = tuple(at[d] for d in "zycx")
    own = pl.ds(pl.multiple_of(x * half, half), half)
    other = pl.ds(pl.multiple_of((1 - x) * half, half), half)
    grid.enter()
    low[...] = gx[other, :].astype(bf16)
    vec_all[here] = vec[...]
    out_end[x, 0] = out[own, :]
    gx_end[x, 0] = gx[own, :]

    def into(end):
        def use(columns, block):
            end[:, columns] = block.astype(f32)

        return use

    jobs = [(ref, into(end), 0.0) for ref, end in zip((*grads, dw), (*owns, dw_own))]
    chains = reduce_plan(
        wire, (vec_all, out, out_end, low, low_in, *jobs), local, rows, width, len(jobs), half, depth
    )
    for _, act in schedule(chains):
        act()
    gx_end[1 - x, 0] = low_in[...].astype(f32)
    wire.close(chains[-3:])


def reduce(dw, vec, out, gx, grads, fsdp):
    size = grid_sizes(fsdp)
    shape = tuple(size[d] for d in "zycx")
    rows, width = dw.shape[-2], dw.shape[-1]
    half, depth = gx.shape[0] // 2, gx.shape[1]
    wide = len(grads)
    draft = Draft(fsdp)
    reduce_plan(draft, (None,) * 5, None, rows, width, wide + 1, half, depth)
    return pl.pallas_call(
        functools.partial(reduce_kernel, fsdp=fsdp, wide=wide),
        out_shape=[
            jax.ShapeDtypeStruct((rows, width), f32),
            jax.ShapeDtypeStruct(shape + vec.shape, f32),
            jax.ShapeDtypeStruct((2, 1, half, depth), bf16),
            jax.ShapeDtypeStruct((2, 1, half, depth), f32),
        ]
        + [jax.ShapeDtypeStruct((rows, width), f32)] * wide,
        in_specs=[ANY] + [VMEM] * 3 + [ANY] * wide,
        out_specs=[VMEM] * (4 + wide),
        scratch_shapes=[
            pltpu.SemaphoreType.DMA((draft.used,)),
            pltpu.SemaphoreType.DMA((draft.used,)),
            pltpu.SemaphoreType.DMA((6,)),
            pltpu.SemaphoreType.REGULAR((draft.credits,)),
            pltpu.VMEM((half, depth), bf16),
            pltpu.VMEM((half, depth), bf16),
        ]
        + draft.shapes,
        compiler_params=params(collective_id=1, has_side_effects=True),
        cost_estimate=lasts(120),
        name="reduce",
    )(dw, vec, out, gx, *grads)


def body(
    tokens, cotangent, routes, prefix, attn_gain, query_weight, key_weight, value_weight,
    out_weight_t, bias_table, ffn_gain, router, inner_weight, down_weight_t,
):
    fsdp, tp = lax.axis_size("fsdp"), lax.axis_size("tp")
    half_len, depth = tokens.shape[2], tokens.shape[3]
    length = half_len * tp
    heads_here, buckets = bias_table.shape
    heads = heads_here * tp
    expert_count = router.shape[1]
    capacity = length * 5 // (4 * expert_count)
    slots = capacity * expert_count
    rows, cols = query_weight.shape
    small = attn_gain.shape[0]
    me = lax.axis_index("tp")
    shards = [w[:, e] for e in range(expert_count) for w in (inner_weight, down_weight_t)]
    number = lax.axis_index("fsdp") * tp + me
    shares = jnp.concatenate(
        [attn_gain[None], ffn_gain[None], router.T, jnp.zeros((8 - 2 - expert_count, small), f32)]
    )
    owned = jnp.arange(depth)[None, :] // small == number
    vectors = jnp.where(owned, jnp.tile(shares, (1, depth // small)), 0.0)
    table = jnp.pad(bias_table, ((0, 8 - heads_here), (0, TILE - buckets)))
    offset = jnp.arange(4 * TILE)
    bucket = bucket_of(jnp.where(offset < 3 * TILE, offset - TILE, offset - 5 * TILE))
    picker = (bucket[:, None] == jnp.arange(buckets)[None, :]).astype(f32)
    picker_low = (jnp.arange(TILE)[:, None] == bucket[None, :]).astype(bf16)
    farthest = buckets // 2 - 1

    route = lax.dynamic_index_in_dim(routes, me, 0, keepdims=False)[0]
    prefix_len = lax.dynamic_index_in_dim(prefix, me, 0, keepdims=False)
    chosen = (route == jnp.arange(expert_count)[None, :]).astype(bf16)
    before = jnp.tril(jnp.ones((length, length), bf16), -1)
    rank = jnp.dot(before, chosen, preferred_element_type=f32).astype(jnp.int32)
    slot_ids = route[:, 0] * capacity + jnp.where(route[:, 0] == 0, rank[:, 0], rank[:, 1])

    (
        attn_w, vectors, x, c, nrm, q, k, v, mixed, rl, p, res, nt, prob, xs, gs, *weights,
    ) = forward(
        (query_weight, key_weight, value_weight, out_weight_t), vectors, table, tokens, cotangent,
        prefix_len, route, slot_ids[None, :], picker_low, shards, fsdp, heads, slots,
    )
    attn_w = attn_w.reshape(fsdp, tp, rows, 4 * cols)
    out_w = attn_w[..., 3 * cols :]
    weights = [w.reshape((fsdp, tp) + shards[0].shape) for w in weights]
    gain_one, gain_two = vectors[0:1], vectors[1:2]
    router_rows = jnp.pad(vectors[2:4], ((0, 6), (0, 0)))
    ys, gbs, grads = [], [], []
    for e in range(expert_count):
        y, gb, *both = expert(
            xs, gs, weights[2 * e], weights[2 * e + 1], e, expert_count, []
        )
        ys.append(y)
        gbs.append(gb)
        grads += both
    out, gres, gmix, dwo, gain_two_part, router_part = combine(
        res, c, nt, prob, route, slot_ids[:, None], ys, gbs, mixed, out_w, gain_two, router_rows
    )
    dq, dk, dv, diag = attend_back(q, k, v, mixed, gmix, rl, p)
    gx, dw, gain_one_part = finish(x, gain_one, nrm, dq, dk, dv, attn_w, gres, dwo)
    table_grad = jnp.dot(diag[:, 0], picker, precision=highest, preferred_element_type=f32)
    table_grad = table_grad.at[:, farthest].add(jnp.sum(diag[:, 1], axis=-1))
    table_grad = table_grad.at[:, buckets - 1].add(jnp.sum(diag[:, 2], axis=-1))
    sums = jnp.concatenate(
        [gain_one_part[0], gain_two_part[0]]
        + [router_part[e] for e in range(expert_count)]
        + [table_grad.reshape(-1)]
    )
    sums_len = sums.shape[0]
    tall = -(-sums_len // (8 * TILE)) * 8
    sums = jnp.pad(sums, (0, tall * TILE - sums_len)).reshape(tall, TILE)
    split = (fsdp // grid_sizes(fsdp)["y"] // 2, grid_sizes(fsdp)["y"], 2, tp)
    dw, sums, out, gx, *own_grads = reduce(
        dw.reshape(split + dw.shape[2:]), sums, out, gx,
        [grad.reshape(split + grad.shape[2:]) for grad in grads], fsdp,
    )
    sums = jnp.sum(sums.reshape(fsdp * tp, tall * TILE), axis=0)
    start = (lax.axis_index("fsdp") * tp + me) * small
    own = [
        lax.dynamic_slice_in_dim(sums, n * depth + start, small) for n in range(2 + expert_count)
    ]
    table_own = lax.dynamic_slice_in_dim(
        sums[(2 + expert_count) * depth : sums_len].reshape(heads, buckets), me * heads_here, heads_here
    )

    return (
        out,
        gx,
        own[0],
        dw[:, :cols],
        dw[:, cols : 2 * cols],
        dw[:, 2 * cols : 3 * cols],
        dw[:, 3 * cols :],
        table_own,
        own[1],
        jnp.stack(own[2:], axis=1),
        jnp.stack(own_grads[0::2], axis=1),
        jnp.stack(own_grads[1::2], axis=1),
    )


def solution(mesh):
    tokens = P(None, "fsdp", "tp", None)
    every = P(("fsdp", "tp"))
    square = P("fsdp", "tp")
    expert = P("fsdp", None, "tp")
    in_specs = (
        tokens, tokens, P(None, "fsdp", None, None), P(None, "fsdp"), every, square, square, square,
        square, P("tp", None), every, P(("fsdp", "tp"), None), expert, expert,
    )
    out_specs = (
        tokens, tokens, every, square, square, square, square, P("tp", None), every,
        P(("fsdp", "tp"), None), expert, expert,
    )
    return jax.shard_map(body, mesh=mesh, in_specs=in_specs, out_specs=out_specs, check_vma=False)
```

time: 594 us -> 436 us (0.73)
  Pallas kernels: 554 us -> 403 us
  local copies, waits for them, and re-layouts: 29 us -> 21.6 us
    pallas_call x6 -> x4, Pallas kernels: 488 us -> 336 us  [the longest x1 143 us: reduce(): pl.pallas_call(functools.partial(reduce_kernel, fsdp=fsdp, wide=wide), ou...]
    reshape x6 -> x0, local copies, waits for them, and re-layouts: 7.78 us -> none  [the longest x1 2.52 us: body(): d2.reshape(ffn_out)]
where the time goes in v3:
time: 436 us; the launch traced here: 435 us
  Pallas kernels  403 us (92%)
  local copies, waits for them, and re-layouts  21.6 us (5%)
  other arithmetic  8.89 us (2%)
    pallas_call x1, Pallas kernels, reduce(): pl.pallas_call(functools.partial(reduce_kernel, fsdp=fsdp, wide=wide), ou...  143 us
    pallas_call x1, Pallas kernels, forward(): pl.pallas_call(functools.partial(forward_kernel, fsdp=fsdp, wide=wide, he...  141 us
    pallas_call x2, Pallas kernels, expert(): pl.pallas_call(kernel, grid=(1, halves * per), in_specs=[row_block, row_b...  52.3 us
    pallas_call x1, Pallas kernels, attend_back(): pl.pallas_call(attend_back_kernel, grid=(heads,), in_specs=[pair, pair, p...  29.8 us
    pallas_call x1, Pallas kernels, finish(): pl.pallas_call(functools.partial(finish_kernel, cols=cols), out_shape=[ja...  19.1 us
    pallas_call x1, Pallas kernels, combine(): pl.pallas_call(functools.partial(combine_kernel, cols=cols), out_shape=[j...  18.2 us

profile of v3, /device:TPU:0, one launch (start us, length us, event | category | flops | bytes accessed | tf_op | source)
XLA Modules:
  0.0 435.4 jit_solution(13057730666095603320)
XLA Ops:
  0.6 0.0 copy-start
  0.7 0.7 fusion.30
  1.4 0.2 copy.53.refs_9_.route_ref
  1.6 0.0 copy-start.3
  1.6 0.7 constant_dynamic-slice_fusion.1
  2.3 0.8 fusion.4
  3.2 0.0 copy-start.9
  3.2 0.0 copy-start.14
  3.2 0.0 copy-start.15
  3.2 0.0 copy-start.16
  3.2 0.0 copy-start.4
  3.2 0.0 copy-start.5
  3.2 1.2 slice_reduce_fusion
  4.4 0.0 copy-done.9
  4.4 0.6 fusion.18.refs_10_
  5.0 0.6 constant_dynamic-slice_fusion.2
  5.6 0.1 pad.28.clone
  5.7 0.0 copy-done.15
  5.7 0.1 maximum_maximum_fusion
  5.8 0.1 tile.10
  5.9 0.6 broadcast_select_fusion.refs_4_
  6.5 0.4 fusion.28
  6.9 0.8 copy_bitcast_fusion.1
  7.7 0.0 copy-done.5
  7.7 0.4 fusion.27
  8.1 0.7 copy_bitcast_fusion
  8.9 0.7 fusion.10.refs_11_
  9.5 0.0 copy-done.13
  9.5 0.6 pad.16.refs_5_
  10.1 140.9 %forward.1 = (bf16[4,2,2,2,48,1536]{5,4,3,2,1,0:T(8,128)(2,1)}, f32[8,768]{1,0:T(8,128)}, bf16[1024,768]{1,0:T(8,128)(2,1)}, bf16[1024,768]{1,0:T(8,128)(2,1)}, ...) custom-call(bf16[48,384]{1,0:T(8,128)(2,1)} %refs_0_.1, ...), custom_call_target="tpu_custom_call" | custom-call | flops 131999997952 | bytes 1024 | tf_op jit(solution)/shard_map/forward/pallas_call | solution.py:859
  151.1 26.0 %expert.3 = (bf16[640,768]{1,0:T(8,128)(2,1)}, bf16[640,768]{1,0:T(8,128)(2,1)}, bf16[16,2,48,1536]{3,2,1,0:T(8,128)(2,1)}, bf16[16,2,48,1536]{3,2,1,0:T(8,128)(2,1)}) custom-call(bf16[1280,768]{1,0:T(8,128)(2,1)} %get-tuple-element.96.refs_0_, bf16[1280,768]{1,0:T(8,128)(2,1)} %get-tuple-element.97.refs_1_, bf16[16,2,48,1536]{3,2,1,0:T(8,128)(2,1)} %bitcast.71, ...), custom_call_target="tpu_custom_call" | custom-call | flops 28600000512 | bytes 1024 | tf_op jit(solution)/shard_map/expert/pallas_call | solution.py:97
  177.1 26.2 %expert.2 = (bf16[640,768]{1,0:T(8,128)(2,1)}, bf16[640,768]{1,0:T(8,128)(2,1)}, bf16[16,2,48,1536]{3,2,1,0:T(8,128)(2,1)}, bf16[16,2,48,1536]{3,2,1,0:T(8,128)(2,1)}) custom-call(bf16[1280,768]{1,0:T(8,128)(2,1)} %get-tuple-element.96.refs_0_, bf16[1280,768]{1,0:T(8,128)(2,1)} %get-tuple-element.97.refs_1_, bf16[16,2,48,1536]{3,2,1,0:T(8,128)(2,1)} %bitcast.69, ...), custom_call_target="tpu_custom_call" | custom-call | flops 28600000512 | bytes 1024 | tf_op jit(solution)/shard_map/expert/pallas_call | solution.py:97
  203.3 0.6 fusion.29
  203.9 2.4 slice.131.w_ref
  206.4 0.6 pad.17.router_ref
  207.0 18.2 %combine.1 = (bf16[1024,768]{1,0:T(8,128)(2,1)}, f32[1024,768]{1,0:T(8,128)}, bf16[1024,768]{1,0:T(8,128)(2,1)}, bf16[16,2,48,384]{3,2,1,0:T(8,128)(2,1)}, f32[8,768]{1,0:T(8,128)}, /*index=5*/f32[8,768]{1,0:T(8,128)}) custom-call(f32[1024,768]{1,0:T(8,128)} %get-tuple-element.92.res_ref, bf16[1024,768]{1,0:T(8,128)(2,1)} %get-tuple-element.93.c_ref, ...), custom_call_target="tpu_custom_call" | custom-call | flops 19800000512 | bytes 1024 | tf_op jit(solution)/shard_map/combine/pallas_call | solution.py:174
  225.2 29.8 %attend_back.1 = (bf16[1024,768]{1,0:T(8,128)(2,1)}, bf16[1024,768]{1,0:T(8,128)(2,1)}, bf16[1024,768]{1,0:T(8,128)(2,1)}, f32[12,8,512]{2,1,0:T(8,128)}) custom-call(bf16[1024,768]{1,0:T(8,128)(2,1)} %get-tuple-element.88.q_ref, bf16[1024,768]{1,0:T(8,128)(2,1)} %get-tuple-element.89.k_ref, bf16[1024,768]{1,0:T(8,128)(2,1)} %get-tuple-element.90.v_ref, ...), custom_call_target="tpu_custom_call" | custom-call | flops 32999999488 | bytes 1024 | tf_op jit(solution)/shard_map/attend_back/pallas_call | solution.py:270
  255.0 1.3 slice_reduce_fusion.2
  256.3 0.3 fusion.11
  256.6 0.1 copy.58
  256.7 0.6 compare_reduce_fusion
  257.4 0.7 add_select_fusion
  258.1 0.1 scatter-add.6
  258.2 0.1 copy.59
  258.3 0.1 slice_add_fusion
  258.3 0.3 scatter-add.9
  258.7 0.1 reshape.291
  258.7 19.1 %finish.1 = (f32[1024,768]{1,0:T(8,128)}, bf16[16,2,48,1536]{3,2,1,0:T(8,128)(2,1)}, f32[8,768]{1,0:T(8,128)}) custom-call(bf16[1024,768]{1,0:T(8,128)(2,1)} %get-tuple-element.85.x_ref, f32[1,768]{1,0:T(1,128)} %get-tuple-element.187.gain_ref, bf16[1024,768]{1,0:T(8,128)(2,1)} %get-tuple-element.87.nrm_ref, bf16[1024,768]{1,0:T(8,128)(2,1)} %get-tuple-element.110.dq_ref, ...), custom_call_target="tpu_custom_call" | custom-call | flops 20899999744 | bytes 1024 | tf_op jit(solution)/shard_map/finish/pallas_call | solution.py:339
  277.8 0.8 slice_reduce_fusion.7
  278.6 0.8 slice_reduce_fusion.6
  279.4 0.8 slice_reduce_fusion.4
  280.2 0.6 pad_bitcast_fusion.refs_1_
  280.9 142.6 %reduce.26 = (f32[48,1536]{1,0:T(8,128)}, f32[4,2,2,2,32,128]{5,4,3,2,1,0:T(8,128)}, bf16[2,1,512,768]{3,2,1,0:T(8,128)(2,1)}, f32[2,1,512,768]{3,2,1,0:T(8,128)...) custom-call(bf16[4,2,2,2,48,1536]{5,4,3,2,1,0:T(8,128)(2,1)} %bitcast.68, ...), custom_call_target="tpu_custom_call" | custom-call | flops 131999997952 | bytes 1024 | tf_op jit(solution)/shard_map/reduce/pallas_call | solution.py:1103
  423.5 1.1 pad_maximum_fusion.1
  424.6 1.3 copy.61
  425.9 1.3 copy.60
  427.2 1.2 reduce_sum.31
  428.5 0.6 dynamic-slice_bitcast_fusion.1
  429.1 0.6 pad_maximum_fusion.2
  429.6 0.7 fusion.26
  430.3 0.1 slice.128
  430.4 0.6 constant_dynamic-slice_fusion
  431.0 2.7 copy.85
  433.7 1.7 copy.86
  (36 shorter events, 0.2 us)
Async XLA Ops:
  0.6 4.4 %copy-start = (s32[2,1]{0,1:T(1,128)S(1)}, s32[2,1]{0,1:T(1,128)}, u32[]{:S(2)}) copy-start(s32[2,1]{0,1:T(1,128)} %param.21) | copy-start | bytes 28
  1.6 1.6 copy-start.3
  3.2 1.2 copy-start.9
  3.2 2.5 copy-start.14
  3.2 2.5 copy-start.15
  3.2 2.5 copy-start.16
  3.2 3.3 copy-start.4
  3.2 4.5 %copy-start.5 = (bf16[48,2,1536]{2,1,0:T(2,128)(2,1)S(1)}, bf16[48,2,1536]{2,1,0:T(2,128)(2,1)}, u32[]{:S(2)}) copy-start(bf16[48,2,1536]{2,1,0:T(2,128)(2,1)} %param.31) | copy-start | bytes 884740
  6.5 3.0 copy-start.13
  8.9 142.2 %copy-start.10 = (s32[512]{0:T(512)}, s32[512]{0:T(512)S(1)}, u32[]{:S(2)}) copy-start(s32[512]{0:T(512)S(1)} %fusion.23) | copy-start | bytes 6148
  177.1 26.2 %copy-start.12 = (f32[8,768]{1,0:T(8,128)S(1)}, f32[8,768]{1,0:T(8,128)}, u32[]{:S(2)}) copy-start(f32[8,768]{1,0:T(8,128)} %get-tuple-element.86) | copy-start | bytes 73732
  225.2 31.1 %copy-start.11 = (s32[512]{0:T(512)S(1)}, s32[512]{0:T(512)}, u32[]{:S(2)}) copy-start(s32[512]{0:T(512)} %copy-done.10) | copy-start | bytes 6148
  423.4 2.5 copy-start.7
  423.4 2.4 copy-start.8
  424.6 5.0 %copy-start.6 = (f32[48,1536]{1,0:T(8,128)S(1)}, f32[48,1536]{1,0:T(8,128)}, u32[]{:S(2)}) copy-start(f32[48,1536]{1,0:T(8,128)} %get-tuple-element.129) | copy-start | bytes 884740
  427.2 6.5 %copy-start.2 = (f32[2,1,512,768]{3,2,1,0:T(8,128)S(1)}, f32[2,1,512,768]{3,2,1,0:T(8,128)}, u32[]{:S(2)}) copy-start(f32[2,1,512,768]{3,2,1,0:T(8,128)} %get-tuple-element.209) | copy-start | bytes 9437188
  431.0 4.3 copy-start.1

commit v4 on v3

--- a/solution.py
+++ b/solution.py
@@ -19,7 +19,7 @@
 
 
 def params(**more):
-    return pltpu.CompilerParams(vmem_limit_bytes=60 * 2**20, **more)
+    return pltpu.CompilerParams(vmem_limit_bytes=62 * 2**20, **more)
 
 
 def lasts(microseconds):
@@ -188,168 +188,6 @@
         cost_estimate=lasts(18),
         name="combine",
     )(res, c, nt, prob, route, slot_col, *ys, *gbs, mixed, w, gain, router_rows)
-
-
-def attend_back_kernel(
-    q_ref, k_ref, v_ref, mixed_ref, g_ref, rl_ref, p_ref,
-    dq_ref, dk_ref, dv_ref, diag_ref, kext, qt, dkt, dvt, band_ref,
-):
-    h = pl.program_id(0)
-    length = q_ref.shape[0]
-    tiles = length // TILE
-    half = lax.rem(h, 2)
-    lane = lax.broadcasted_iota(jnp.int32, (1, TILE), 1)
-    mine = (lane // 64) == half
-    block = 256
-
-    @pl.when(h == 0)
-    def _():
-        row = lax.broadcasted_iota(jnp.int32, (length, TILE), 0)
-        col = lax.broadcasted_iota(jnp.int32, (length, TILE), 1)
-        kext[:, TILE:] = (row // TILE == col).astype(bf16)
-
-    @pl.when(half == 0)
-    def _():
-        kext[:, :TILE] = k_ref[...]
-        qt[...] = q_ref[...].T
-
-    band_ref[...] = jnp.zeros_like(band_ref)
-    left = jnp.zeros((1, TILE), f32)
-    right = jnp.zeros((1, TILE), f32)
-    for b in range(length // block):
-        rows = slice(b * block, (b + 1) * block)
-        rl = jnp.sum(jnp.where(lane == h, rl_ref[rows, :], 0.0), axis=-1, keepdims=True)
-        g = jnp.where(mine, g_ref[rows, :].astype(f32) * rl, 0.0)
-        delta = jnp.sum(g * mixed_ref[rows, :].astype(f32), axis=-1, keepdims=True)
-        g = g.astype(bf16)
-        gp = mm_nt(g, v_ref[...])
-        p = p_ref[0, rows, :]
-        ds = p.astype(f32) * (gp - delta)
-        low = ds.astype(bf16)
-        dq = mm(low, kext[...])
-        dq_ref[rows, :] = jnp.where(mine, (dq[:, :TILE] * 0.125).astype(bf16), dq_ref[rows, :])
-        gv = mm(g.T, p)
-        gk = mm(qt[:, rows], low)
-        if b == 0:
-            dvt[...] = gv
-            dkt[...] = gk
-        else:
-            dvt[...] += gv
-            dkt[...] += gk
-        for part in range(block // TILE):
-            i = b * (block // TILE) + part
-            sums = dq[part * TILE : (part + 1) * TILE, TILE:]
-            sums = jnp.sum(sums, axis=0, keepdims=True)
-            left = left + jnp.where(lane <= i - 2, sums, 0.0)
-            right = right + jnp.where(lane >= i + 2, sums, 0.0)
-            for side in (-1, 0, 1):
-                j = i + side
-                if 0 <= j < tiles:
-                    band_ref[:, (side + 1) * TILE : (side + 2) * TILE] += ds[
-                        part * TILE : (part + 1) * TILE, j * TILE : (j + 1) * TILE
-                    ]
-    turned = band_ref[0:8, :]
-    for g in range(1, TILE // 8):
-        turned = turned + pltpu.roll(band_ref[8 * g : 8 * g + 8, :], 4 * TILE - 8 * g, 1)
-    diag = turned[0:1, :]
-    for r in range(1, 8):
-        diag = diag + pltpu.roll(turned[r : r + 1, :], 4 * TILE - r, 1)
-    diag_ref[0] = jnp.zeros((8, 4 * TILE), f32)
-    diag_ref[0, 0:1, :] = diag
-    diag_ref[0, 1:2, :TILE] = left
-    diag_ref[0, 2:3, :TILE] = right
-    dk_ref[...] = jnp.where(mine, dkt[...].T.astype(bf16), dk_ref[...])
-    dv_ref[...] = jnp.where(mine, dvt[...].T.astype(bf16), dv_ref[...])
-
-
-def attend_back(q, k, v, mixed, g, rl, p):
-    length, width = q.shape
-    heads = p.shape[0]
-    pair = pl.BlockSpec((length, TILE), lambda h: (0, h // 2))
-    shape = jax.ShapeDtypeStruct((length, width), bf16)
-    return pl.pallas_call(
-        attend_back_kernel,
-        grid=(heads,),
-        in_specs=[
-            pair, pair, pair, pair, pair,
-            pl.BlockSpec((length, TILE), lambda h: (0, 0)),
-            pl.BlockSpec((1, length, length), lambda h: (h, 0, 0)),
-        ],
-        out_specs=[
-            pair, pair, pair,
-            pl.BlockSpec((1, 8, 4 * TILE), lambda h: (h, 0, 0)),
-        ],
-        out_shape=[
-            shape, shape, shape,
-            jax.ShapeDtypeStruct((heads, 8, 4 * TILE), f32),
-        ],
-        scratch_shapes=[
-            pltpu.VMEM((length, 2 * TILE), bf16),
-            pltpu.VMEM((TILE, length), bf16),
-            pltpu.VMEM((TILE, length), f32),
-            pltpu.VMEM((TILE, length), f32),
-            pltpu.VMEM((TILE, 4 * TILE), f32),
-        ],
-        compiler_params=params(),
-        cost_estimate=lasts(30),
-        name="attend_back",
-    )(q, k, v, mixed, g, rl, p)
-
-
-def finish_kernel(
-    x_ref, gain_ref, nrm_ref, dq_ref, dk_ref, dv_ref, w_ref, gres_ref, dwo_ref,
-    gx_ref, dw_ref, gain_part_ref, nt, *, cols,
-):
-    length, depth = x_ref.shape
-    group, _, rows_per, _ = dw_ref.shape
-    block = 256
-    gain_part_ref[...] = jnp.zeros_like(gain_part_ref)
-    nt[...] = nrm_ref[...].T
-    dw_ref[:, :, :, 3 * cols :] = dwo_ref[...]
-    for t in range(2):
-        at = slice(t * cols, (t + 1) * cols)
-        for n, ref in enumerate((dq_ref, dk_ref, dv_ref)):
-            d = mm(nt[...], ref[:, at]).astype(bf16)
-            dw_ref[:, t, :, n * cols : (n + 1) * cols] = d.reshape(group, rows_per, cols)
-
-    def rows_body(i, _):
-        rows = pl.ds(pl.multiple_of(i * block, block), block)
-        gn = jnp.zeros((block, depth), f32)
-        for t in range(2):
-            w = w_ref[:, t].reshape(depth, 4 * cols)
-            at = slice(t * cols, (t + 1) * cols)
-            for n, ref in enumerate((dq_ref, dk_ref, dv_ref)):
-                gn = gn + mm_nt(ref[rows, at], w[:, n * cols : (n + 1) * cols])
-        x = x_ref[rows, :].astype(f32)
-        r = lax.rsqrt(jnp.mean(x * x, axis=-1, keepdims=True) + epsilon)
-        n1 = x * r
-        gain_part_ref[0:1, :] += jnp.sum(gn * n1, axis=0, keepdims=True)
-        g1 = gn * gain_ref[...]
-        gx_ref[rows, :] = gres_ref[rows, :] + r * (
-            g1 - n1 * jnp.mean(g1 * n1, axis=-1, keepdims=True)
-        )
-        return 0
-
-    lax.fori_loop(0, length // block, rows_body, 0)
-
-
-def finish(x, gain, nrm, dq, dk, dv, w, gres, dwo):
-    length, depth = x.shape
-    cols = w.shape[3] // 4
-    return pl.pallas_call(
-        functools.partial(finish_kernel, cols=cols),
-        out_shape=[
-            jax.ShapeDtypeStruct((length, depth), f32),
-            jax.ShapeDtypeStruct(w.shape, bf16),
-            jax.ShapeDtypeStruct((8, depth), f32),
-        ],
-        in_specs=[VMEM] * 9,
-        out_specs=[VMEM] * 3,
-        scratch_shapes=[pltpu.VMEM((depth, length), bf16)],
-        compiler_params=params(),
-        cost_estimate=lasts(19),
-        name="finish",
-    )(x, gain, nrm, dq, dk, dv, w, gres, dwo)
 
 
 def grid_sizes(fsdp):
@@ -1039,10 +877,11 @@
     return chains
 
 
-def reduce_plan(wire, refs, local, rows, width, count, half, depth):
-    vec, out, out_end, low, low_in, *grads = refs
-    chains = reduce_groups(wire, grads if vec is not None else [(None, None, 0.0)] * count, width, rows, local)
-    chains.append((0, gather_chain(wire, vec, slice(None), 16 * TILE, "zyx")))
+def backward_plan(wire, refs, local, rows, width, count, half, depth, late):
+    vec, out, out_end, low, low_in, *jobs = refs
+    chains = reduce_groups(wire, jobs or [(None, None, 0.0)] * count, width, rows, local)
+    phases = gather_chain(wire, vec, slice(None), 2 * 8 * depth, "zyx")
+    chains.append((0, [phases[0] + (late,)] + phases[1:]))
     pairs = [(None, None, None)] * 2
     if out is not None:
         x = wire.at["x"]
@@ -1051,30 +890,64 @@
             (out.at[other], out_end.at[x, 0], out_end.at[1 - x, 0]),
             (low, low_in, low_in),
         ]
-    chains += [(rank, swap_chain(wire, [pair], 4 * half * depth)) for rank, pair in enumerate(pairs)]
+    for pair, earliest in zip(pairs, (0.0, late)):
+        phases = swap_chain(wire, [pair], 4 * half * depth)
+        chains.append((0, [phases[0] + (earliest,)]))
     return chains
 
 
-def reduce_kernel(*refs, fsdp, wide):
-    dw, vec, out, gx = refs[:4]
-    grads = refs[4 : 4 + wide]
-    dw_own, vec_all, out_end, gx_end = refs[4 + wide : 8 + wide]
-    owns = refs[8 + wide : 8 + 2 * wide]
-    sends, receives, local, credit, low, low_in, *buffers = refs[8 + 2 * wide :]
+HEAD, ROWS, WEIGHT = 2.5, 2.6, 1.5
+
+
+def backward_late(heads, length):
+    return heads * HEAD + length // 256 * ROWS + 6 * WEIGHT + 2.0
+
+
+def backward_kernel(*refs, fsdp, wide, heads):
+    (
+        x_ref, gains_ref, parts_ref, picker_ref, attn_w, mixed_ref, gmix_ref, rl_ref, q_all, k_all, v_all, p_all,
+        gres_all, dwo_all, out,
+    ) = refs[:15]
+    grads, refs = refs[15 : 15 + wide], refs[15 + wide :]
+    dw_own, sums_ref, out_end, gx_end = refs[:4]
+    owns, refs = refs[4 : 4 + wide], refs[4 + wide :]
+    (
+        sends, receives, local, credit, moved, low, low_in, q_ref, k_ref, v_ref, gx_ref, p_two, hold, kext, qt,
+        dkt, dvt, band_ref, diag_all, side_all, nt, dw, vec_all, *buffers,
+    ) = refs
     grid = Grid(fsdp)
     wire = Wire(grid, sends, receives, credit, buffers)
     at = grid.at
-    rows, width = dw_own.shape
-    half, depth = gx_end.shape[2], gx_end.shape[3]
-    x = at["x"]
+    rows_per, width = dw_own.shape
+    cols = width // 4
+    length, depth = x_ref.shape
+    half = length // 2
+    x_at = at["x"]
     here = tuple(at[d] for d in "zycx")
-    own = pl.ds(pl.multiple_of(x * half, half), half)
-    other = pl.ds(pl.multiple_of((1 - x) * half, half), half)
+    own = pl.ds(pl.multiple_of(x_at * half, half), half)
+    other = pl.ds(pl.multiple_of((1 - x_at) * half, half), half)
+    first = [
+        pltpu.make_async_copy(a, b, moved.at[n])
+        for n, (a, b) in enumerate(((q_all, q_ref), (k_all, k_ref), (v_all, v_ref)))
+    ]
+    later = [
+        pltpu.make_async_copy(gres_all, gx_ref, moved.at[3]),
+        pltpu.make_async_copy(
+            dwo_all, dw.at[:, :, :, :, :, slice(3 * cols, 4 * cols)], moved.at[4]
+        ),
+        pltpu.make_async_copy(out.at[own], out_end.at[x_at, 0], moved.at[5]),
+    ]
+
+    def fetch(h):
+        two = lax.rem(h, 2)
+        return pltpu.make_async_copy(p_all.at[h], p_two.at[two], moved.at[6 + two])
+
+    for copy in first:
+        copy.start()
+    fetch(0).start()
+    for copy in later:
+        copy.start()
     grid.enter()
-    low[...] = gx[other, :].astype(bf16)
-    vec_all[here] = vec[...]
-    out_end[x, 0] = out[own, :]
-    gx_end[x, 0] = gx[own, :]
 
     def into(end):
         def use(columns, block):
@@ -1082,48 +955,210 @@
 
         return use
 
-    jobs = [(ref, into(end), 0.0) for ref, end in zip((*grads, dw), (*owns, dw_own))]
-    chains = reduce_plan(
-        wire, (vec_all, out, out_end, low, low_in, *jobs), local, rows, width, len(jobs), half, depth
-    )
-    for _, act in schedule(chains):
-        act()
-    gx_end[1 - x, 0] = low_in[...].astype(f32)
+    late = backward_late(heads, length)
+    jobs = [(ref, into(end), 0.0) for ref, end in zip(grads, owns)]
+    jobs.append((dw, into(dw_own), late))
+    chains = backward_plan(
+        wire, (vec_all, out, out_end, low, low_in, *jobs), local, rows_per, width, len(jobs), half,
+        depth, late,
+    )
+    agenda = Agenda(schedule(chains, 3))
+    agenda.catch_up(0.0)
+
+    tiles = length // TILE
+    block = 256
+    lane = lax.broadcasted_iota(jnp.int32, (1, TILE), 1)
+    row = lax.broadcasted_iota(jnp.int32, (length, TILE), 0)
+    col = lax.broadcasted_iota(jnp.int32, (length, TILE), 1)
+    kext[:, TILE:] = (row // TILE == col).astype(bf16)
+    for copy in first:
+        copy.wait()
+
+    def attend_back(h):
+        two = lax.rem(h, 2)
+        mine = (lane // 64) == two
+        pair = pl.ds(pl.multiple_of((h // 2) * TILE, TILE), TILE)
+
+        @pl.when(h + 1 < heads)
+        def _():
+            fetch(h + 1).start()
+
+        kext[:, :TILE] = k_ref[:, pair]
+        qt[...] = q_ref[:, pair].T
+        band_ref[...] = jnp.zeros_like(band_ref)
+        left = jnp.zeros((1, TILE), f32)
+        right = jnp.zeros((1, TILE), f32)
+        fetch(h).wait()
+        for b in range(length // block):
+            rows = slice(b * block, (b + 1) * block)
+            rl = jnp.sum(jnp.where(lane == h, rl_ref[rows, :], 0.0), axis=-1, keepdims=True)
+            g = jnp.where(mine, gmix_ref[rows, pair].astype(f32) * rl, 0.0)
+            delta = jnp.sum(g * mixed_ref[rows, pair].astype(f32), axis=-1, keepdims=True)
+            g = g.astype(bf16)
+            gp = mm_nt(g, v_ref[:, pair])
+            p = p_two[two, rows, :]
+            ds = p.astype(f32) * (gp - delta)
+            ds_low = ds.astype(bf16)
+            dq = mm(ds_low, kext[...])
+            hold[0, rows, :] = jnp.where(mine, (dq[:, :TILE] * 0.125).astype(bf16), hold[0, rows, :])
+            gv = mm(g.T, p)
+            gk = mm(qt[:, rows], ds_low)
+            if b == 0:
+                dvt[...] = gv
+                dkt[...] = gk
+            else:
+                dvt[...] += gv
+                dkt[...] += gk
+            for part in range(block // TILE):
+                i = b * (block // TILE) + part
+                sums = dq[part * TILE : (part + 1) * TILE, TILE:]
+                sums = jnp.sum(sums, axis=0, keepdims=True)
+                left = left + jnp.where(lane <= i - 2, sums, 0.0)
+                right = right + jnp.where(lane >= i + 2, sums, 0.0)
+                for side in (-1, 0, 1):
+                    j = i + side
+                    if 0 <= j < tiles:
+                        band_ref[:, (side + 1) * TILE : (side + 2) * TILE] += ds[
+                            part * TILE : (part + 1) * TILE, j * TILE : (j + 1) * TILE
+                        ]
+        turned = band_ref[0:8, :]
+        for g in range(1, TILE // 8):
+            turned = turned + pltpu.roll(band_ref[8 * g : 8 * g + 8, :], 4 * TILE - 8 * g, 1)
+        diag = turned[0:1, :]
+        for r in range(1, 8):
+            diag = diag + pltpu.roll(turned[r : r + 1, :], 4 * TILE - r, 1)
+        diag_all[h, 0:1, :] = diag
+        farthest = 15
+        sides = jnp.where(lane == farthest, jnp.sum(left, axis=-1, keepdims=True), 0.0)
+        sides = sides + jnp.where(
+            lane == 2 * farthest + 1, jnp.sum(right, axis=-1, keepdims=True), 0.0
+        )
+        side_all[h, 0:1, :] = sides
+        hold[1] = jnp.where(mine, dkt[...].T.astype(bf16), hold[1])
+        hold[2] = jnp.where(mine, dvt[...].T.astype(bf16), hold[2])
+
+        @pl.when(two == 1)
+        def _():
+            q_ref[:, pair] = hold[0]
+            k_ref[:, pair] = hold[1]
+            v_ref[:, pair] = hold[2]
+
+    hold[...] = jnp.zeros_like(hold)
+    diag_all[...] = jnp.zeros_like(diag_all)
+    agenda.loop(heads, HEAD, attend_back)
+    for copy in later:
+        copy.wait()
+    vec_all[here] = parts_ref[...]
+
+    def input_grad(i):
+        rows = pl.ds(pl.multiple_of(i * block, block), block)
+        gn = jnp.zeros((block, depth), f32)
+        for t in range(2):
+            w = attn_w[:, t].reshape(depth, 4 * cols)
+            span = slice(t * cols, (t + 1) * cols)
+            for n, ref in enumerate((q_ref, k_ref, v_ref)):
+                gn = gn + mm_nt(ref[rows, span], w[:, n * cols : (n + 1) * cols])
+        x = x_ref[rows, :].astype(f32)
+        r = lax.rsqrt(jnp.mean(x * x, axis=-1, keepdims=True) + epsilon)
+        n1 = x * r
+        nt[:, rows] = (n1 * gains_ref[0:1, :]).astype(bf16).T
+        vec_all[here + (slice(0, 1), slice(None))] += jnp.sum(gn * n1, axis=0, keepdims=True)
+        g1 = gn * gains_ref[0:1, :]
+        gx_ref[rows, :] = gx_ref[rows, :] + r * (
+            g1 - n1 * jnp.mean(g1 * n1, axis=-1, keepdims=True)
+        )
+
+    agenda.loop(length // block, ROWS, input_grad)
+    for t in range(2):
+        span = slice(t * cols, (t + 1) * cols)
+        for n, ref in enumerate((q_ref, k_ref, v_ref)):
+            agenda.catch_up(agenda.now)
+            d = mm(nt[...], ref[:, span]).astype(bf16)
+            dw[:, :, :, t, :, n * cols : (n + 1) * cols] = d.reshape(
+                dw.shape[:3] + (rows_per, cols)
+            )
+            agenda.now += WEIGHT
+    low[...] = gx_ref[other, :].astype(bf16)
+    keep = pltpu.make_async_copy(gx_ref.at[own], gx_end.at[x_at, 0], moved.at[0])
+    keep.start()
+    for h in range(heads):
+        entry = lax.dot_general(
+            diag_all[h], picker_ref[...], (((1,), (0,)), ((), ())), precision=highest,
+            preferred_element_type=f32,
+        )
+        n = h % (heads // 2)
+        vec_all[here + (slice(4 + h // (heads // 2), 5 + h // (heads // 2)), slice(n * TILE, (n + 1) * TILE))] = (
+            entry[0:1, :] + side_all[h, 0:1, :]
+        )
+    agenda.catch_up(1e9)
+    keep.wait()
+    gx_ref[0:half, :] = low_in[...].astype(f32)
+    give = pltpu.make_async_copy(gx_ref.at[0:half], gx_end.at[1 - x_at, 0], moved.at[1])
+    give.start()
+    total = vec_all[0, 0, 0, 0]
+    for z in range(grid.size["z"]):
+        for y in range(grid.size["y"]):
+            for c in range(2):
+                for t in range(2):
+                    if z + y + c + t:
+                        total = total + vec_all[z, y, c, t]
+    sums_ref[...] = total
+    give.wait()
     wire.close(chains[-3:])
 
 
-def reduce(dw, vec, out, gx, grads, fsdp):
+def backward(x, gains, parts, picker, attn_w, mixed, gmix, rl, q, k, v, p, gres, dwo, out, grads, fsdp):
     size = grid_sizes(fsdp)
     shape = tuple(size[d] for d in "zycx")
-    rows, width = dw.shape[-2], dw.shape[-1]
-    half, depth = gx.shape[0] // 2, gx.shape[1]
+    rows, width = attn_w.shape[-2:]
+    length, depth = x.shape
+    half = length // 2
+    heads = p.shape[0]
     wide = len(grads)
     draft = Draft(fsdp)
-    reduce_plan(draft, (None,) * 5, None, rows, width, wide + 1, half, depth)
+    backward_plan(draft, (None,) * 5, None, rows, width, wide + 1, half, depth, 0.0)
+    pair = (length, TILE)
     return pl.pallas_call(
-        functools.partial(reduce_kernel, fsdp=fsdp, wide=wide),
+        functools.partial(backward_kernel, fsdp=fsdp, wide=wide, heads=heads),
         out_shape=[
             jax.ShapeDtypeStruct((rows, width), f32),
-            jax.ShapeDtypeStruct(shape + vec.shape, f32),
+            jax.ShapeDtypeStruct((8, depth), f32),
             jax.ShapeDtypeStruct((2, 1, half, depth), bf16),
             jax.ShapeDtypeStruct((2, 1, half, depth), f32),
         ]
         + [jax.ShapeDtypeStruct((rows, width), f32)] * wide,
-        in_specs=[ANY] + [VMEM] * 3 + [ANY] * wide,
-        out_specs=[VMEM] * (4 + wide),
+        in_specs=[VMEM] * 8 + [ANY] * (7 + wide),
+        out_specs=[VMEM] * 2 + [ANY] * 2 + [VMEM] * wide,
         scratch_shapes=[
             pltpu.SemaphoreType.DMA((draft.used,)),
             pltpu.SemaphoreType.DMA((draft.used,)),
             pltpu.SemaphoreType.DMA((6,)),
             pltpu.SemaphoreType.REGULAR((draft.credits,)),
+            pltpu.SemaphoreType.DMA((8,)),
             pltpu.VMEM((half, depth), bf16),
             pltpu.VMEM((half, depth), bf16),
+            pltpu.VMEM((length, depth), bf16),
+            pltpu.VMEM((length, depth), bf16),
+            pltpu.VMEM((length, depth), bf16),
+            pltpu.VMEM((length, depth), f32),
+            pltpu.VMEM((2, length, length), bf16),
+            pltpu.VMEM((3,) + pair, bf16),
+            pltpu.VMEM((length, 2 * TILE), bf16),
+            pltpu.VMEM((TILE, length), bf16),
+            pltpu.VMEM((TILE, length), f32),
+            pltpu.VMEM((TILE, length), f32),
+            pltpu.VMEM((TILE, 4 * TILE), f32),
+            pltpu.VMEM((heads, 8, 4 * TILE), f32),
+            pltpu.VMEM((heads, 8, TILE), f32),
+            pltpu.VMEM((depth, length), bf16),
+            pltpu.VMEM(shape + (rows, width), bf16),
+            pltpu.VMEM(shape + (8, depth), f32),
         ]
         + draft.shapes,
         compiler_params=params(collective_id=1, has_side_effects=True),
-        cost_estimate=lasts(120),
-        name="reduce",
-    )(dw, vec, out, gx, *grads)
+        cost_estimate=lasts(150),
+        name="backward",
+    )(x, gains, parts, picker, attn_w, mixed, gmix, rl, q, k, v, p, gres, dwo, out, *grads)
 
 
 def body(
@@ -1151,9 +1186,8 @@
     table = jnp.pad(bias_table, ((0, 8 - heads_here), (0, TILE - buckets)))
     offset = jnp.arange(4 * TILE)
     bucket = bucket_of(jnp.where(offset < 3 * TILE, offset - TILE, offset - 5 * TILE))
-    picker = (bucket[:, None] == jnp.arange(buckets)[None, :]).astype(f32)
+    picker = (bucket[:, None] == jnp.arange(TILE)[None, :]).astype(f32)
     picker_low = (jnp.arange(TILE)[:, None] == bucket[None, :]).astype(bf16)
-    farthest = buckets // 2 - 1
 
     route = lax.dynamic_index_in_dim(routes, me, 0, keepdims=False)[0]
     prefix_len = lax.dynamic_index_in_dim(prefix, me, 0, keepdims=False)
@@ -1184,33 +1218,17 @@
     out, gres, gmix, dwo, gain_two_part, router_part = combine(
         res, c, nt, prob, route, slot_ids[:, None], ys, gbs, mixed, out_w, gain_two, router_rows
     )
-    dq, dk, dv, diag = attend_back(q, k, v, mixed, gmix, rl, p)
-    gx, dw, gain_one_part = finish(x, gain_one, nrm, dq, dk, dv, attn_w, gres, dwo)
-    table_grad = jnp.dot(diag[:, 0], picker, precision=highest, preferred_element_type=f32)
-    table_grad = table_grad.at[:, farthest].add(jnp.sum(diag[:, 1], axis=-1))
-    table_grad = table_grad.at[:, buckets - 1].add(jnp.sum(diag[:, 2], axis=-1))
-    sums = jnp.concatenate(
-        [gain_one_part[0], gain_two_part[0]]
-        + [router_part[e] for e in range(expert_count)]
-        + [table_grad.reshape(-1)]
-    )
-    sums_len = sums.shape[0]
-    tall = -(-sums_len // (8 * TILE)) * 8
-    sums = jnp.pad(sums, (0, tall * TILE - sums_len)).reshape(tall, TILE)
-    split = (fsdp // grid_sizes(fsdp)["y"] // 2, grid_sizes(fsdp)["y"], 2, tp)
-    dw, sums, out, gx, *own_grads = reduce(
-        dw.reshape(split + dw.shape[2:]), sums, out, gx,
+    split = tuple(grid_sizes(fsdp)[d] for d in "zycx")
+    parts = jnp.concatenate(
+        [jnp.zeros((1, depth), f32), gain_two_part[:1], router_part[:2], jnp.zeros((4, depth), f32)]
+    )
+    dw, sums, out, gx, *own_grads = backward(
+        x, vectors, parts, picker, attn_w, mixed, gmix, rl, q, k, v, p, gres,
+        dwo.reshape(split + dwo.shape[2:]), out,
         [grad.reshape(split + grad.shape[2:]) for grad in grads], fsdp,
     )
-    sums = jnp.sum(sums.reshape(fsdp * tp, tall * TILE), axis=0)
-    start = (lax.axis_index("fsdp") * tp + me) * small
-    own = [
-        lax.dynamic_slice_in_dim(sums, n * depth + start, small) for n in range(2 + expert_count)
-    ]
-    table_own = lax.dynamic_slice_in_dim(
-        sums[(2 + expert_count) * depth : sums_len].reshape(heads, buckets), me * heads_here, heads_here
-    )
-
+    own = lax.dynamic_slice_in_dim(sums[: 2 + expert_count], number * small, small, axis=1)
+    table_own = lax.dynamic_slice_in_dim(sums, 4 + me, 1)[0].reshape(-1, TILE)[:heads_here, :buckets]
     return (
         out,
         gx,
@@ -1221,7 +1239,7 @@
         dw[:, 3 * cols :],
         table_own,
         own[1],
-        jnp.stack(own[2:], axis=1),
+        own[2:].T,
         jnp.stack(own_grads[0::2], axis=1),
         jnp.stack(own_grads[1::2], axis=1),
     )

time: 436 us -> 390 us (0.89)
  Pallas kernels: 403 us -> 355 us
    pallas_call x3 -> x1, Pallas kernels: 191 us -> 143 us  [backward(): pl.pallas_call(functools.partial(backward_kernel, fsdp=fsdp, wide=wide, h...]
where the time goes in v4:
time: 390 us; the launch traced here: 387 us
  Pallas kernels  355 us (91%)
  local copies, waits for them, and re-layouts  23 us (6%)
  other arithmetic  6.6 us (2%)
    pallas_call x1, Pallas kernels, backward(): pl.pallas_call(functools.partial(backward_kernel, fsdp=fsdp, wide=wide, h...  143 us
    pallas_call x1, Pallas kernels, forward(): pl.pallas_call(functools.partial(forward_kernel, fsdp=fsdp, wide=wide, he...  141 us
    pallas_call x2, Pallas kernels, expert(): pl.pallas_call(kernel, grid=(1, halves * per), in_specs=[row_block, row_b...  52.3 us
    pallas_call x1, Pallas kernels, combine(): pl.pallas_call(functools.partial(combine_kernel, cols=cols), out_shape=[j...  18.2 us

profile of v4, /device:TPU:0, one launch (start us, length us, event | category | flops | bytes accessed | tf_op | source)
XLA Modules:
  0.0 386.7 jit_solution(6209433876002488120)
XLA Ops:
  0.6 0.0 copy-start
  0.7 0.1 pad.21.clone
  0.7 0.8 maximum_maximum_fusion.1
  1.5 0.0 copy-done.12
  1.5 0.1 tile.10
  1.7 0.6 broadcast_select_fusion.refs_4_
  2.3 1.3 pad.8.refs_5_
  3.6 0.0 copy-done
  3.6 0.6 constant_dynamic-slice_fusion.2
  4.2 0.7 fusion.26
  4.8 0.2 copy.49.refs_9_.route_ref
  5.1 0.0 copy-start.3
  5.1 0.7 constant_dynamic-slice_fusion.1
  5.8 0.8 fusion.4
  6.7 0.0 copy-done.3
  6.7 0.0 copy-start.11
  6.7 0.0 copy-start.5
  6.7 0.0 copy-start.6
  6.7 1.2 slice_reduce_fusion
  7.9 0.0 copy-done.11
  7.9 0.6 fusion.15.refs_10_
  8.5 0.0 copy-start.9
  8.5 0.7 fusion.10.refs_11_
  9.2 0.0 copy-done.5
  9.2 0.4 fusion.25
  9.6 0.8 copy_bitcast_fusion.1
  10.3 0.0 copy-done.6
  10.3 0.4 fusion.24
  10.8 0.8 copy_bitcast_fusion
  11.5 0.0 copy-done.9
  11.5 141.0 %forward.1 = (bf16[4,2,2,2,48,1536]{5,4,3,2,1,0:T(8,128)(2,1)}, f32[8,768]{1,0:T(8,128)}, bf16[1024,768]{1,0:T(8,128)(2,1)}, bf16[1024,768]{1,0:T(8,128)(2,1)}, ...) custom-call(bf16[48,384]{1,0:T(8,128)(2,1)} %refs_0_.1, ...), custom_call_target="tpu_custom_call" | custom-call | flops 131999997952 | bytes 1024 | tf_op jit(solution)/shard_map/forward/pallas_call | solution.py:697
  152.6 26.0 %expert.2 = (bf16[640,768]{1,0:T(8,128)(2,1)}, bf16[640,768]{1,0:T(8,128)(2,1)}, bf16[16,2,48,1536]{3,2,1,0:T(8,128)(2,1)}, bf16[16,2,48,1536]{3,2,1,0:T(8,128)(2,1)}) custom-call(bf16[1280,768]{1,0:T(8,128)(2,1)} %get-tuple-element.59.refs_0_, bf16[1280,768]{1,0:T(8,128)(2,1)} %get-tuple-element.60.refs_1_, bf16[16,2,48,1536]{3,2,1,0:T(8,128)(2,1)} %bitcast.65, ...), custom_call_target="tpu_custom_call" | custom-call | flops 28600000512 | bytes 1024 | tf_op jit(solution)/shard_map/expert/pallas_call | solution.py:97
  178.6 26.3 %expert.3 = (bf16[640,768]{1,0:T(8,128)(2,1)}, bf16[640,768]{1,0:T(8,128)(2,1)}, bf16[16,2,48,1536]{3,2,1,0:T(8,128)(2,1)}, bf16[16,2,48,1536]{3,2,1,0:T(8,128)(2,1)}) custom-call(bf16[1280,768]{1,0:T(8,128)(2,1)} %get-tuple-element.59.refs_0_, bf16[1280,768]{1,0:T(8,128)(2,1)} %get-tuple-element.60.refs_1_, bf16[16,2,48,1536]{3,2,1,0:T(8,128)(2,1)} %bitcast.63, ...), custom_call_target="tpu_custom_call" | custom-call | flops 28600000512 | bytes 1024 | tf_op jit(solution)/shard_map/expert/pallas_call | solution.py:97
  204.9 2.4 slice.82.w_ref
  207.3 1.3 slice.67.gain_ref
  208.6 0.7 slice.68
  209.4 0.6 pad.9.router_ref
  210.0 18.2 %combine.1 = (bf16[1024,768]{1,0:T(8,128)(2,1)}, f32[1024,768]{1,0:T(8,128)}, bf16[1024,768]{1,0:T(8,128)(2,1)}, bf16[16,2,48,384]{3,2,1,0:T(8,128)(2,1)}, f32[8,768]{1,0:T(8,128)}, /*index=5*/f32[8,768]{1,0:T(8,128)}) custom-call(f32[1024,768]{1,0:T(8,128)} %get-tuple-element.55.res_ref, bf16[1024,768]{1,0:T(8,128)(2,1)} %get-tuple-element.56.c_ref, ...), custom_call_target="tpu_custom_call" | custom-call | flops 19800000512 | bytes 1024 | tf_op jit(solution)/shard_map/combine/pallas_call | solution.py:174
  228.2 0.7 slice.70
  229.0 0.7 slice.69
  229.7 0.0 copy-done.13
  229.7 0.7 maximum_maximum_fusion.refs_2_
  230.4 0.0 copy-done.10
  230.4 0.8 fusion.11.refs_3_
  231.2 143.4 %backward.1 = (f32[48,1536]{1,0:T(8,128)}, f32[8,768]{1,0:T(8,128)}, bf16[2,1,512,768]{3,2,1,0:T(8,128)(2,1)}, f32[2,1,512,768]{3,2,1,0:T(8,128)}, f32[48,1536]{...) custom-call(bf16[1024,768]{1,0:T(8,128)(2,1)} %get-tuple-element.53.refs_0_, ...), custom_call_target="tpu_custom_call" | custom-call | flops 165000003584 | bytes 1024 | tf_op jit(solution)/shard_map/backward/pallas_call | solution.py:1121
  374.6 0.0 copy-start.7
  374.7 0.0 copy-start.8
  374.7 0.8 slice.71
  375.5 0.1 constant_dynamic-slice_fusion
  375.5 0.5 slice_bitcast_fusion.1
  376.1 1.7 fusion.23
  377.8 1.3 dynamic-slice_reduce_fusion
  379.1 0.6 slice_bitcast_fusion
  379.7 1.2 pad_maximum_fusion
  380.9 1.3 copy.54
  382.2 0.0 copy-done.7
  382.2 0.0 copy-done.8
  382.2 0.0 copy-start.2
  382.2 1.3 copy.55
  383.5 0.0 copy-done.4
  383.5 1.1 copy.67
  384.6 0.0 copy-done.2
  384.6 1.7 copy.68
  386.3 0.0 copy-done.1
  (12 shorter events, 0.1 us)
Async XLA Ops:
  0.6 2.9 copy-start
  0.7 0.8 copy-start.12
  5.1 1.6 copy-start.3
  6.7 1.2 copy-start.11
  6.7 2.5 copy-start.5
  6.7 3.6 copy-start.6
  8.5 3.0 copy-start.9
  210.0 19.7 %copy-start.13 = (f32[8]{0:T(128)S(1)}, f32[8]{0:T(128)}, u32[]{:S(2)}) copy-start(f32[8]{0:T(128)} %copy-done.12) | copy-start | bytes 100
  210.0 20.4 %copy-start.10 = (s32[512]{0:T(512)S(1)}, s32[512]{0:T(512)}, u32[]{:S(2)}) copy-start(s32[512]{0:T(512)} %copy-done.9) | copy-start | bytes 6148
  374.6 7.5 %copy-start.7 = (f32[48,1536]{1,0:T(8,128)S(1)}, f32[48,1536]{1,0:T(8,128)}, u32[]{:S(2)}) copy-start(f32[48,1536]{1,0:T(8,128)} %get-tuple-element.92) | copy-start | bytes 884740
  374.7 7.5 %copy-start.8 = (f32[48,1536]{1,0:T(8,128)S(1)}, f32[48,1536]{1,0:T(8,128)}, u32[]{:S(2)}) copy-start(f32[48,1536]{1,0:T(8,128)} %get-tuple-element.93) | copy-start | bytes 884740
  379.7 3.8 copy-start.4
  382.2 2.4 copy-start.2
  383.5 2.8 copy-start.1

commit v5 on v4

--- a/solution.py
+++ b/solution.py
@@ -43,151 +43,6 @@
         far_bucket = far_bucket + (distance >= edge_value).astype(jnp.int32)
     near_bucket = jnp.where(distance < 8, distance, far_bucket)
     return near_bucket + 16 * (offset > 0).astype(jnp.int32)
-
-
-def experts_kernel(
-    x_ref, g_ref, w1_ref, w2_ref, y_ref, gb_ref, d1_ref, d2_ref, xt, gt, y_acc, gb_acc
-):
-    step = pl.program_id(1)
-    last = pl.num_programs(1) - 1
-    group, _, rows, chunk = w1_ref.shape
-    depth = group * rows
-
-    @pl.when(step == 0)
-    def _():
-        xt[...] = x_ref[...].T
-        gt[...] = g_ref[...].T
-        y_acc[...] = jnp.zeros_like(y_acc)
-        gb_acc[...] = jnp.zeros_like(gb_acc)
-
-    w1 = w1_ref[:, 0].reshape(depth, chunk)
-    w2 = w2_ref[:, 0].reshape(depth, chunk)
-    inner = mm(x_ref[...], w1)
-    hidden = mm(g_ref[...], w2)
-    phi = 0.5 + 0.5 * lax.erf(inner * 0.7071067811865476)
-    act = (inner * phi).astype(bf16)
-    slope = phi + inner * (jnp.exp(inner * inner * -0.5) * 0.3989422804014327)
-    grad = (hidden * slope).astype(bf16)
-    y_acc[...] += mm_nt(act, w2)
-    gb_acc[...] += mm_nt(grad, w1)
-    d2_ref[:, 0] = mm(gt[...], act).astype(bf16).reshape(group, rows, chunk)
-    d1_ref[:, 0] = mm(xt[...], grad).astype(bf16).reshape(group, rows, chunk)
-
-    @pl.when(step == last)
-    def _():
-        y_ref[...] = y_acc[...].astype(bf16)
-        gb_ref[...] = gb_acc[...].astype(bf16)
-
-
-def expert(xs, gs, w1, w2, number, expert_count, after):
-    slots, depth = xs.shape
-    capacity = slots // expert_count
-    group, halves, rows, hidden = w1.shape
-    chunk = 512
-    per = hidden // chunk
-    row_block = pl.BlockSpec((capacity, depth), lambda e, s: (number, 0))
-    out_block = pl.BlockSpec((capacity, depth), lambda e, s: (0, 0))
-    weight_block = pl.BlockSpec(
-        (group, 1, rows, chunk), lambda e, s: (0, s // per, 0, lax.rem(s, per))
-    )
-
-    def kernel(*refs):
-        experts_kernel(*refs[:4], *refs[4 + len(after) :])
-
-    return pl.pallas_call(
-        kernel,
-        grid=(1, halves * per),
-        in_specs=[row_block, row_block, weight_block, weight_block] + [ANY] * len(after),
-        out_specs=[out_block, out_block, weight_block, weight_block],
-        out_shape=[
-            jax.ShapeDtypeStruct((capacity, depth), bf16),
-            jax.ShapeDtypeStruct((capacity, depth), bf16),
-            jax.ShapeDtypeStruct(w1.shape, bf16),
-            jax.ShapeDtypeStruct(w2.shape, bf16),
-        ],
-        scratch_shapes=[
-            pltpu.VMEM((depth, capacity), bf16),
-            pltpu.VMEM((depth, capacity), bf16),
-            pltpu.VMEM((capacity, depth), f32),
-            pltpu.VMEM((capacity, depth), f32),
-        ],
-        compiler_params=params(),
-        cost_estimate=lasts(26),
-        name="expert",
-    )(xs, gs, w1, w2, *after)
-
-
-def combine_kernel(
-    res_ref, c_ref, nt_ref, prob_ref, route_ref, slot_ref, y0_ref, y1_ref, gb0_ref, gb1_ref, mixed_ref,
-    w_ref, gain_ref, router_ref, out_ref, gres_ref, gmix_ref, dwo_ref, gain_part_ref, router_part_ref, gat, *, cols,
-):
-    length, depth = res_ref.shape
-    capacity = y0_ref.shape[0]
-    slots = 2 * capacity
-    block = 256
-    gain_part_ref[...] = jnp.zeros_like(gain_part_ref)
-    router_part_ref[...] = jnp.zeros_like(router_part_ref)
-
-    def rows_body(i, _):
-        rows = pl.ds(pl.multiple_of(i * block, block), block)
-        lane = lax.broadcasted_iota(jnp.int32, (1, slots), 1)
-        pick = (slot_ref[rows, :] == lane).astype(bf16)
-        y = mm(pick[:, :capacity], y0_ref[...]) + mm(pick[:, capacity:], y1_ref[...])
-        gn = mm(pick[:, :capacity], gb0_ref[...]) + mm(pick[:, capacity:], gb1_ref[...])
-        res = res_ref[rows, :]
-        c = c_ref[rows, :].astype(f32)
-        prob = prob_ref[rows, :]
-        p0, p1, gate = prob[:, 0:1], prob[:, 1:2], prob[:, 2:3]
-        out_ref[rows, :] = (res + gate * y).astype(bf16)
-        grad_gate = jnp.sum(c * y, axis=-1, keepdims=True)
-        route = route_ref[rows, :]
-        gl0 = p0 * (jnp.where(route == 0, 1.0, 0.0) - gate) * grad_gate
-        gl1 = p1 * (jnp.where(route == 1, 1.0, 0.0) - gate) * grad_gate
-        gn = gn + gl0 * router_ref[0:1, :] + gl1 * router_ref[1:2, :]
-        nt = nt_ref[rows, :].astype(f32)
-        router_part_ref[0:1, :] += jnp.sum(nt * gl0, axis=0, keepdims=True)
-        router_part_ref[1:2, :] += jnp.sum(nt * gl1, axis=0, keepdims=True)
-        r = lax.rsqrt(jnp.mean(res * res, axis=-1, keepdims=True) + epsilon)
-        n2 = res * r
-        gain_part_ref[0:1, :] += jnp.sum(gn * n2, axis=0, keepdims=True)
-        g2 = gn * gain_ref[...]
-        gres = c + r * (g2 - n2 * jnp.mean(g2 * n2, axis=-1, keepdims=True))
-        gres_ref[rows, :] = gres
-        ga = gres.astype(bf16)
-        gat[:, rows] = ga.T
-        for t in range(2):
-            w = w_ref[:, t].reshape(depth, cols)
-            gmix_ref[rows, t * cols : (t + 1) * cols] = mm(ga, w).astype(bf16)
-        return 0
-
-    lax.fori_loop(0, length // block, rows_body, 0)
-    group = dwo_ref.shape[0]
-    rows = dwo_ref.shape[2]
-    for t in range(2):
-        d = mm(gat[...], mixed_ref[:, t * cols : (t + 1) * cols])
-        dwo_ref[:, t] = d.astype(bf16).reshape(group, rows, cols)
-
-
-def combine(res, c, nt, prob, route, slot_col, ys, gbs, mixed, w, gain, router_rows):
-    length, depth = res.shape
-    cols = w.shape[3]
-    return pl.pallas_call(
-        functools.partial(combine_kernel, cols=cols),
-        out_shape=[
-            jax.ShapeDtypeStruct((length, depth), bf16),
-            jax.ShapeDtypeStruct((length, depth), f32),
-            jax.ShapeDtypeStruct((length, depth), bf16),
-            jax.ShapeDtypeStruct(w.shape, bf16),
-            jax.ShapeDtypeStruct((8, depth), f32),
-            jax.ShapeDtypeStruct((8, depth), f32),
-        ],
-        in_specs=[VMEM] * 14,
-        out_specs=[VMEM] * 6,
-        scratch_shapes=[pltpu.VMEM((depth, length), bf16)],
-        compiler_params=params(),
-        cost_estimate=lasts(18),
-        name="combine",
-    )(res, c, nt, prob, route, slot_col, *ys, *gbs, mixed, w, gain, router_rows)
 
 
 def grid_sizes(fsdp):
@@ -503,15 +358,98 @@
         lax.fori_loop(0, count, turn, 0)
 
 
+CHUNK, PIECE = 512, 4.3
+
+
+def expert_scratch(shape, rows, capacity, depth):
+    lead = tuple(shape[d] for d in "zyc")
+    return [
+        pltpu.VMEM((2, 2) + lead + (rows, CHUNK), bf16),
+        pltpu.VMEM((2,) + lead + (rows, CHUNK), bf16),
+        pltpu.VMEM((2, depth, capacity), bf16),
+        pltpu.VMEM((2, capacity, depth), f32),
+        pltpu.SemaphoreType.DMA((6,)),
+    ]
+
+
+def run_expert(agenda, x_ref, g_ref, weights, grads, y_ref, gb_ref, scratch):
+    w_two, d_two, turned, total, sems = scratch
+    depth = x_ref.shape[1]
+    per = weights[0].shape[5] // CHUNK
+    count = 2 * per
+
+    def where(array, s):
+        at = pl.ds(pl.multiple_of(lax.rem(s, per) * CHUNK, CHUNK), CHUNK)
+        return array.at[:, :, :, s // per, :, at]
+
+    def fetch(s):
+        two = lax.rem(s, 2)
+        return [
+            pltpu.make_async_copy(where(w, s), w_two.at[two, n], sems.at[two * 2 + n])
+            for n, w in enumerate(weights)
+        ]
+
+    def put(s):
+        return [
+            pltpu.make_async_copy(d_two.at[n], where(d, s), sems.at[4 + n])
+            for n, d in enumerate(grads)
+        ]
+
+    for copy in fetch(0):
+        copy.start()
+    turned[0] = x_ref[...].T
+    turned[1] = g_ref[...].T
+    total[...] = jnp.zeros_like(total)
+
+    def step(s):
+        two = lax.rem(s, 2)
+
+        @pl.when(s + 1 < count)
+        def _():
+            for copy in fetch(s + 1):
+                copy.start()
+
+        for copy in fetch(s):
+            copy.wait()
+
+        w1 = w_two[two, 0].reshape(depth, CHUNK)
+        w2 = w_two[two, 1].reshape(depth, CHUNK)
+        inner = mm(x_ref[...], w1)
+        hidden = mm(g_ref[...], w2)
+        phi = 0.5 + 0.5 * lax.erf(inner * 0.7071067811865476)
+        act = (inner * phi).astype(bf16)
+        slope = phi + inner * (jnp.exp(inner * inner * -0.5) * 0.3989422804014327)
+        grad = (hidden * slope).astype(bf16)
+        total[0] += mm_nt(act, w2)
+        total[1] += mm_nt(grad, w1)
+        shape = d_two.shape[1:]
+
+        @pl.when(s > 0)
+        def _():
+            for copy in put(s - 1):
+                copy.wait()
+
+        d_two[1] = mm(turned[1], act).astype(bf16).reshape(shape)
+        d_two[0] = mm(turned[0], grad).astype(bf16).reshape(shape)
+        for copy in put(s):
+            copy.start()
+
+    agenda.loop(count, PIECE, step)
+    y_ref[...] = total[0].astype(bf16)
+    gb_ref[...] = total[1].astype(bf16)
+    for copy in put(count - 1):
+        copy.wait()
+
+
 def forward_kernel(*refs, fsdp, wide, heads, slots):
     wq, wk, wv, wo, vec, table, tokens, cotangent, prefix_ref, route_ref, slot_ref, picker_ref = refs[:12]
     shards, refs = refs[12 : 12 + wide], refs[12 + wide :]
     (
-        attn_all, vec_sum, x_all, c_all, nrm_ref, q_ref, k_ref, v_ref, mixed_ref, rl_ref, p_all,
-        res_ref, nt_ref, prob_ref, xs_ref, gs_ref,
-    ) = refs[:16]
-    alls, refs = refs[16 : 16 + wide], refs[16 + wide :]
-    sends, receives, local, vec_all, tables, bias, vext, p_two, low_ref = refs
+        attn_all, vec_sum, x_all, c_all, q_ref, k_ref, v_ref, mixed_ref, rl_ref, p_all,
+        res_ref, nt_ref, prob_ref, xs_ref, gs_ref, y_ref, gb_ref, d1_all, d2_all,
+    ) = refs[:19]
+    alls, refs = refs[19 : 19 + wide], refs[19 + wide :]
+    sends, receives, local, vec_all, tables, bias, vext, p_two, low_ref, *scratch = refs
     grid = Grid(fsdp)
     wire = Wire(grid, sends, receives)
     here = tuple(grid.at[d] for d in "zycx")
@@ -563,7 +501,6 @@
         x = x_all[rows, :].astype(f32)
         r = lax.rsqrt(jnp.mean(x * x, axis=-1, keepdims=True) + epsilon)
         n = (x * r * vec_sum[0:1, :]).astype(bf16)
-        nrm_ref[rows, :] = n
         for t in range(2):
             w = attn_all[:, :, :, t].reshape(depth, 4 * cols)
             at = slice(t * cols, (t + 1) * cols)
@@ -676,6 +613,12 @@
         gs_ref[pl.ds(at, step), :] = mm(pick, low_ref[...]).astype(bf16)
 
     agenda.loop(slots // step, 2.2, sort)
+    agenda.catch_up(max(end for (rank, _), end in zip(chains, ends) if rank in (1, 2)))
+    capacity = y_ref.shape[0]
+    run_expert(
+        agenda, xs_ref.at[0:capacity], gs_ref.at[0:capacity], alls[:2], (d1_all, d2_all), y_ref, gb_ref,
+        scratch,
+    )
     agenda.catch_up(1e9)
     stash(heads - 2).wait()
     stash(heads - 1).wait()
@@ -689,6 +632,7 @@
     half, depth = tokens.shape[2], tokens.shape[3]
     length = 2 * half
     wide = len(shards)
+    capacity = slots // 2
     draft = Draft(fsdp)
     gather_plan(
         draft, (None,) * (7 + wide), rows, cols, [shard.shape[1] for shard in shards], half, depth
@@ -699,7 +643,7 @@
         out_shape=[
             jax.ShapeDtypeStruct(shape + (rows, 4 * cols), bf16),
             jax.ShapeDtypeStruct(vec.shape, f32),
-            low, low, low, low, low, low, low,
+            low, low, low, low, low, low,
             jax.ShapeDtypeStruct((length, TILE), f32),
             jax.ShapeDtypeStruct((heads, length, length), bf16),
             jax.ShapeDtypeStruct((length, depth), f32),
@@ -707,10 +651,13 @@
             jax.ShapeDtypeStruct((length, TILE), f32),
             jax.ShapeDtypeStruct((slots, depth), bf16),
             jax.ShapeDtypeStruct((slots, depth), bf16),
+            jax.ShapeDtypeStruct((capacity, depth), bf16),
+            jax.ShapeDtypeStruct((capacity, depth), bf16),
         ]
+        + [jax.ShapeDtypeStruct(shape + shards[0].shape, bf16)] * 2
         + [jax.ShapeDtypeStruct(shape + shard.shape, bf16) for shard in shards],
         in_specs=[VMEM] * 6 + [ANY] * 2 + [SMEM] + [VMEM] * 3 + [VMEM] * wide,
-        out_specs=[VMEM] * 10 + [ANY] + [VMEM] * 5 + [ANY] * wide,
+        out_specs=[VMEM] * 9 + [ANY] + [VMEM] * 7 + [ANY] * (2 + wide),
         scratch_shapes=[
             pltpu.SemaphoreType.DMA((draft.used,)),
             pltpu.SemaphoreType.DMA((draft.used,)),
@@ -721,9 +668,10 @@
             pltpu.VMEM((length, 2 * TILE), bf16),
             pltpu.VMEM((2, length, length), bf16),
             pltpu.VMEM((length, depth), bf16),
-        ],
+        ]
+        + expert_scratch(size, rows, capacity, depth),
         compiler_params=params(collective_id=0, has_side_effects=True),
-        cost_estimate=lasts(120),
+        cost_estimate=lasts(150),
         name="forward",
     )(*squares, vec, table, tokens, cotangent, prefix, route, slot_row, picker, *shards)
 
@@ -875,6 +823,136 @@
                 (half, reduce_chain(wire, jobs[half::2], columns, total, rows, sem, order[::-1]))
             )
     return chains
+
+
+def middle_kernel(*refs, fsdp):
+    (
+        c_ref, nt_ref, prob_ref, tags_ref, y0_ref, gb0_ref, mixed_ref, gains_ref, xs_all, gs_all,
+        res_all, attn_all, w1_all, w2_all, d1_before, d2_before,
+        out_ref, gres_ref, gmix_ref, dwo_ref, parts_ref, d1_own, d2_own, d1_all, d2_all,
+        sends, receives, local, credit, moved, wo, xs_ref, gs_ref, y1_ref, gb1_ref, gat, *more,
+    ) = refs
+    scratch, buffers = more[:5], more[5:]
+    grid = Grid(fsdp)
+    wire = Wire(grid, sends, receives, credit, buffers)
+    length, depth = gres_ref.shape
+    rows_per, width = d1_own.shape
+    cols = wo.shape[5]
+    capacity = y0_ref.shape[0]
+    bring = pltpu.make_async_copy(
+        attn_all.at[:, :, :, :, :, slice(3 * cols, 4 * cols)], wo, moved.at[0]
+    )
+    bring_res = pltpu.make_async_copy(res_all, gres_ref, moved.at[1])
+    second = slice(capacity, 2 * capacity)
+    tokens_in = [
+        pltpu.make_async_copy(xs_all.at[second], xs_ref, moved.at[2]),
+        pltpu.make_async_copy(gs_all.at[second], gs_ref, moved.at[3]),
+    ]
+    for copy in (*tokens_in, bring, bring_res):
+        copy.start()
+    grid.enter()
+
+    def into(end):
+        def use(columns, block):
+            end[:, columns] = block.astype(f32)
+
+        return use
+
+    jobs = [(d1_before, into(d1_own), 0.0), (d2_before, into(d2_own), 0.0)]
+    agenda = Agenda(schedule(reduce_groups(wire, jobs, width, rows_per, local), 3))
+    agenda.catch_up(0.0)
+    parts_ref[...] = jnp.zeros_like(parts_ref)
+    for copy in tokens_in:
+        copy.wait()
+    run_expert(
+        agenda, xs_ref, gs_ref, (w1_all, w2_all),
+        (d1_all, d2_all), y1_ref, gb1_ref, scratch,
+    )
+    bring.wait()
+    bring_res.wait()
+    block = 256
+
+    def combine(i):
+        rows = pl.ds(pl.multiple_of(i * block, block), block)
+        lane = lax.broadcasted_iota(jnp.int32, (1, 2 * capacity), 1)
+        pick = (tags_ref[rows, 1:2] == lane).astype(bf16)
+        y = mm(pick[:, :capacity], y0_ref[...]) + mm(pick[:, capacity:], y1_ref[...])
+        gn = mm(pick[:, :capacity], gb0_ref[...]) + mm(pick[:, capacity:], gb1_ref[...])
+        res = gres_ref[rows, :]
+        c = c_ref[rows, :].astype(f32)
+        prob = prob_ref[rows, :]
+        p0, p1, gate = prob[:, 0:1], prob[:, 1:2], prob[:, 2:3]
+        out_ref[rows, :] = (res + gate * y).astype(bf16)
+        grad_gate = jnp.sum(c * y, axis=-1, keepdims=True)
+        route = tags_ref[rows, 0:1]
+        gl0 = p0 * (jnp.where(route == 0, 1.0, 0.0) - gate) * grad_gate
+        gl1 = p1 * (jnp.where(route == 1, 1.0, 0.0) - gate) * grad_gate
+        gn = gn + gl0 * gains_ref[2:3, :] + gl1 * gains_ref[3:4, :]
+        nt = nt_ref[rows, :].astype(f32)
+        parts_ref[2:3, :] += jnp.sum(nt * gl0, axis=0, keepdims=True)
+        parts_ref[3:4, :] += jnp.sum(nt * gl1, axis=0, keepdims=True)
+        r = lax.rsqrt(jnp.mean(res * res, axis=-1, keepdims=True) + epsilon)
+        n2 = res * r
+        parts_ref[1:2, :] += jnp.sum(gn * n2, axis=0, keepdims=True)
+        g2 = gn * gains_ref[1:2, :]
+        gres = c + r * (g2 - n2 * jnp.mean(g2 * n2, axis=-1, keepdims=True))
+        gres_ref[rows, :] = gres
+        ga = gres.astype(bf16)
+        gat[:, rows] = ga.T
+        for t in range(2):
+            w = wo[:, :, :, t].reshape(depth, cols)
+            gmix_ref[rows, t * cols : (t + 1) * cols] = mm(ga, w).astype(bf16)
+
+    agenda.loop(length // block, 4.0, combine)
+    for t in range(2):
+        d = mm(gat[...], mixed_ref[:, t * cols : (t + 1) * cols])
+        dwo_ref[:, :, :, t] = d.astype(bf16).reshape(dwo_ref.shape[:3] + (rows_per, cols))
+    agenda.catch_up(1e9)
+
+
+def middle(xs, gs, c, nt, prob, tags, y0, gb0, mixed, gains, res, attn_w, w1, w2, d1, d2, fsdp):
+    size = grid_sizes(fsdp)
+    shape = tuple(size[d] for d in "zycx")
+    length, depth = res.shape
+    rows, width = d1.shape[-2:]
+    cols = attn_w.shape[-1] // 4
+    capacity = y0.shape[0]
+    draft = Draft(fsdp)
+    reduce_groups(draft, [(None, None, 0.0)] * 2, width, rows, None)
+    return pl.pallas_call(
+        functools.partial(middle_kernel, fsdp=fsdp),
+        out_shape=[
+            jax.ShapeDtypeStruct((length, depth), bf16),
+            jax.ShapeDtypeStruct((length, depth), f32),
+            jax.ShapeDtypeStruct((length, depth), bf16),
+            jax.ShapeDtypeStruct(shape + (rows, cols), bf16),
+            jax.ShapeDtypeStruct((8, depth), f32),
+            jax.ShapeDtypeStruct((rows, width), f32),
+            jax.ShapeDtypeStruct((rows, width), f32),
+            jax.ShapeDtypeStruct(d1.shape, bf16),
+            jax.ShapeDtypeStruct(d2.shape, bf16),
+        ],
+        in_specs=[VMEM] * 8 + [ANY] * 8,
+        out_specs=[VMEM] * 7 + [ANY] * 2,
+        scratch_shapes=[
+            pltpu.SemaphoreType.DMA((draft.used,)),
+            pltpu.SemaphoreType.DMA((draft.used,)),
+            pltpu.SemaphoreType.DMA((6,)),
+            pltpu.SemaphoreType.REGULAR((draft.credits,)),
+            pltpu.SemaphoreType.DMA((4,)),
+            pltpu.VMEM(shape + (rows, cols), bf16),
+            pltpu.VMEM((capacity, depth), bf16),
+            pltpu.VMEM((capacity, depth), bf16),
+            pltpu.VMEM((capacity, depth), bf16),
+            pltpu.VMEM((capacity, depth), bf16),
+            pltpu.VMEM((depth, length), bf16),
+        ]
+        + expert_scratch(size, rows, capacity, depth)
+        + draft.shapes,
+        compiler_params=params(collective_id=2, has_side_effects=True),
+        cost_estimate=lasts(60),
+        name="middle",
+    )(c, nt, prob, tags, y0, gb0, mixed, gains, xs, gs, res, attn_w, w1, w2, d1, d2)
 
 
 def backward_plan(wire, refs, local, rows, width, count, half, depth, late):
@@ -1054,7 +1132,7 @@
         rows = pl.ds(pl.multiple_of(i * block, block), block)
         gn = jnp.zeros((block, depth), f32)
         for t in range(2):
-            w = attn_w[:, t].reshape(depth, 4 * cols)
+            w = attn_w[:, :, :, t].reshape(depth, 4 * cols)
             span = slice(t * cols, (t + 1) * cols)
             for n, ref in enumerate((q_ref, k_ref, v_ref)):
                 gn = gn + mm_nt(ref[rows, span], w[:, n * cols : (n + 1) * cols])
@@ -1197,36 +1275,21 @@
     slot_ids = route[:, 0] * capacity + jnp.where(route[:, 0] == 0, rank[:, 0], rank[:, 1])
 
     (
-        attn_w, vectors, x, c, nrm, q, k, v, mixed, rl, p, res, nt, prob, xs, gs, *weights,
+        attn_w, vectors, x, c, q, k, v, mixed, rl, p, res, nt, prob, xs, gs, y0, gb0, d1_first, d2_first,
+        *weights,
     ) = forward(
         (query_weight, key_weight, value_weight, out_weight_t), vectors, table, tokens, cotangent,
         prefix_len, route, slot_ids[None, :], picker_low, shards, fsdp, heads, slots,
     )
-    attn_w = attn_w.reshape(fsdp, tp, rows, 4 * cols)
-    out_w = attn_w[..., 3 * cols :]
-    weights = [w.reshape((fsdp, tp) + shards[0].shape) for w in weights]
-    gain_one, gain_two = vectors[0:1], vectors[1:2]
-    router_rows = jnp.pad(vectors[2:4], ((0, 6), (0, 0)))
-    ys, gbs, grads = [], [], []
-    for e in range(expert_count):
-        y, gb, *both = expert(
-            xs, gs, weights[2 * e], weights[2 * e + 1], e, expert_count, []
-        )
-        ys.append(y)
-        gbs.append(gb)
-        grads += both
-    out, gres, gmix, dwo, gain_two_part, router_part = combine(
-        res, c, nt, prob, route, slot_ids[:, None], ys, gbs, mixed, out_w, gain_two, router_rows
-    )
-    split = tuple(grid_sizes(fsdp)[d] for d in "zycx")
-    parts = jnp.concatenate(
-        [jnp.zeros((1, depth), f32), gain_two_part[:1], router_part[:2], jnp.zeros((4, depth), f32)]
+    tags = jnp.concatenate([route, slot_ids[:, None]], axis=1)
+    out, gres, gmix, dwo, parts, d1_own, d2_own, d1, d2 = middle(
+        xs, gs, c, nt, prob, tags, y0, gb0, mixed, vectors, res, attn_w,
+        *weights[2:4], d1_first, d2_first, fsdp,
     )
     dw, sums, out, gx, *own_grads = backward(
-        x, vectors, parts, picker, attn_w, mixed, gmix, rl, q, k, v, p, gres,
-        dwo.reshape(split + dwo.shape[2:]), out,
-        [grad.reshape(split + grad.shape[2:]) for grad in grads], fsdp,
-    )
+        x, vectors, parts, picker, attn_w, mixed, gmix, rl, q, k, v, p, gres, dwo, out, [d1, d2], fsdp
+    )
+    own_grads = [d1_own, d2_own] + own_grads
     own = lax.dynamic_slice_in_dim(sums[: 2 + expert_count], number * small, small, axis=1)
     table_own = lax.dynamic_slice_in_dim(sums, 4 + me, 1)[0].reshape(-1, TILE)[:heads_here, :buckets]
     return (

time: 390 us -> 358 us (0.918)
  Pallas kernels: 355 us -> 332 us
  local copies, waits for them, and re-layouts: 23 us -> 16.6 us
    pallas_call x1, Pallas kernels: 143 us -> 106 us  [backward(): pl.pallas_call(functools.partial(backward_kernel, fsdp=fsdp, wide=wide, h...]
    pallas_call x1, Pallas kernels: 141 us -> 155 us  [forward(): pl.pallas_call(functools.partial(forward_kernel, fsdp=fsdp, wide=wide, he...]
    slice x5 -> x0, local copies, waits for them, and re-layouts: 5.97 us -> none  [the longest x1 2.43 us: body(): out_w = attn_w[..., 3 * cols:]]
    pallas_call x3 -> x1, Pallas kernels: 70.6 us -> 71.9 us  [middle(): pl.pallas_call(functools.partial(middle_kernel, fsdp=fsdp), out_shape=[ja...]
where the time goes in v5:
time: 358 us; the launch traced here: 355 us
  Pallas kernels  332 us (93%)
  local copies, waits for them, and re-layouts  16.6 us (5%)
  other arithmetic  4 us (1%)
    pallas_call x1, Pallas kernels, forward(): pl.pallas_call(functools.partial(forward_kernel, fsdp=fsdp, wide=wide, he...  155 us
    pallas_call x1, Pallas kernels, backward(): pl.pallas_call(functools.partial(backward_kernel, fsdp=fsdp, wide=wide, h...  106 us
    pallas_call x1, Pallas kernels, middle(): pl.pallas_call(functools.partial(middle_kernel, fsdp=fsdp), out_shape=[ja...  71.9 us
    unnamed x48, local copies, waits for them, and re-layouts  7.58 us

profile of v5, /device:TPU:0, one launch (start us, length us, event | category | flops | bytes accessed | tf_op | source)
XLA Modules:
  0.0 355.2 jit_solution(14095781030272603556)
XLA Ops:
  0.6 0.0 copy-start
  0.7 0.0 copy-start.13
  0.7 0.0 copy-start.21
  0.7 0.0 copy-start.20
  0.7 0.0 copy-start.19
  0.7 0.0 copy-start.3
  0.7 0.8 constant_dynamic-slice_fusion.1
  1.5 0.8 fusion.4
  2.3 0.0 copy-start.11
  2.3 0.6 copy-done.11
  2.9 0.0 copy-done.13
  2.9 0.0 copy-start.4
  2.9 0.6 fusion.16.refs_10_
  3.6 0.0 copy-start.9
  3.6 1.0 copy.48.refs_9_
  4.6 0.0 copy-done
  4.6 0.6 constant_dynamic-slice_fusion.2
  5.2 0.1 pad.14.clone
  5.3 0.0 copy-done.9
  5.3 0.0 copy-done.21
  5.3 0.0 copy-done.20
  5.3 0.0 copy-done.19
  5.3 0.1 maximum_maximum_fusion
  5.4 0.1 tile.10
  5.5 0.6 broadcast_select_fusion.refs_4_
  6.1 0.0 copy-done.3
  6.1 0.4 fusion.26
  6.5 0.8 copy_bitcast_fusion.1
  7.3 0.0 copy-done.4
  7.3 0.4 fusion.25
  7.7 0.7 copy_bitcast_fusion
  8.4 0.7 fusion.10.refs_11_
  9.1 0.0 copy-done.15
  9.1 0.0 copy-done.18
  9.1 0.6 pad.4.refs_5_
  9.7 154.8 %forward.1 = (bf16[4,2,2,2,48,1536]{5,4,3,2,1,0:T(8,128)(2,1)}, f32[8,768]{1,0:T(8,128)}, bf16[1024,768]{1,0:T(8,128)(2,1)}, bf16[1024,768]{1,0:T(8,128)(2,1)}, ...) custom-call(bf16[48,384]{1,0:T(8,128)(2,1)} %refs_0_.1, ...), custom_call_target="tpu_custom_call" | custom-call | flops 165000003584 | bytes 1024 | tf_op jit(solution)/shard_map/forward/pallas_call | solution.py:641
  164.5 0.0 copy-done.12
  164.5 0.0 copy-done.14
  164.5 0.0 copy-done.10
  164.6 1.0 copy.49.refs_3_
  165.6 71.9 %middle.1 = (bf16[1024,768]{1,0:T(8,128)(2,1)}, f32[1024,768]{1,0:T(8,128)}, bf16[1024,768]{1,0:T(8,128)(2,1)}, bf16[4,2,2,2,48,384]{5,4,3,2,1,0:T(8,128)(2,1)},...) custom-call(bf16[1024,768]{1,0:T(8,128)(2,1)} %get-tuple-element.50., ...), custom_call_target="tpu_custom_call" | custom-call | flops 65999998976 | bytes 1024 | tf_op jit(solution)/shard_map/middle/pallas_call | solution.py:922
  237.5 0.0 copy-done.16
  237.5 0.8 fusion.11.refs_3_
  238.3 105.8 %backward.1 = (f32[48,1536]{1,0:T(8,128)}, f32[8,768]{1,0:T(8,128)}, bf16[2,1,512,768]{3,2,1,0:T(8,128)(2,1)}, f32[2,1,512,768]{3,2,1,0:T(8,128)}, f32[48,1536]{1,0:T(8,128)}, /*index=5*/f32[48,1536]{1,0:T(8,128)}) custom-call(bf16[1024,768]{1,0:T(8,128)(2,1)} %get-tuple-element.48.refs_0_, f32[8,768]{1,0:T(8,128)} %get-tuple-element.49.refs_7_.refs_1_, ...), custom_call_target="tpu_custom_call" | custom-call | flops 165000003584 | bytes 1024 | tf_op jit(solution)/shard_map/backward/pallas_call | solution.py:1199
  344.2 0.0 copy-start.6
  344.2 0.0 copy-start.8
  344.2 0.0 copy-done.7
  344.2 0.0 copy-start.5
  344.2 1.1 pad_maximum_fusion.1
  345.3 1.3 copy.51
  346.6 0.0 copy-done.6
  346.6 0.0 copy-done.8
  346.7 1.3 copy.50
  347.9 0.0 copy-done.5
  347.9 0.7 fusion.24
  348.6 0.0 copy-done.17
  348.7 0.1 constant_dynamic-slice_fusion
  348.7 0.5 slice_bitcast_fusion.1
  349.2 0.6 slice_bitcast_fusion
  349.8 0.6 dynamic-slice_reduce_fusion
  350.4 2.7 copy.62
  353.1 0.0 copy-done.2
  353.1 1.7 copy.63
  354.8 0.0 copy-done.1
  (20 shorter events, 0.1 us)
Async XLA Ops:
  0.6 3.9 %copy-start = (s32[2,1]{0,1:T(1,128)S(1)}, s32[2,1]{0,1:T(1,128)}, u32[]{:S(2)}) copy-start(s32[2,1]{0,1:T(1,128)} %param.17) | copy-start | bytes 28
  0.7 2.3 copy-start.13
  0.7 4.6 %copy-start.21 = (f32[24]{0:T(128)S(1)}, f32[24]{0:T(128)}, u32[]{:S(2)}) copy-start(f32[24]{0:T(128)} %param.18) | copy-start | bytes 292
  0.7 4.6 %copy-start.20 = (f32[24]{0:T(128)S(1)}, f32[24]{0:T(128)}, u32[]{:S(2)}) copy-start(f32[24]{0:T(128)} %param.24) | copy-start | bytes 292
  0.7 4.6 %copy-start.19 = (f32[24,2]{0,1:T(2,128)S(1)}, f32[24,2]{0,1:T(2,128)}, u32[]{:S(2)}) copy-start(f32[24,2]{0,1:T(2,128)} %param.25) | copy-start | bytes 580
  0.7 5.4 %copy-start.3 = (bf16[48,2,1536]{2,1,0:T(2,128)(2,1)S(1)}, bf16[48,2,1536]{2,1,0:T(2,128)(2,1)}, u32[]{:S(2)}) copy-start(bf16[48,2,1536]{2,1,0:T(2,128)(2,1)} %param.26) | copy-start | bytes 884740
  2.3 0.6 copy-start.11
  2.9 4.3 %copy-start.4 = (bf16[48,2,1536]{2,1,0:T(2,128)(2,1)S(1)}, bf16[48,2,1536]{2,1,0:T(2,128)(2,1)}, u32[]{:S(2)}) copy-start(bf16[48,2,1536]{2,1,0:T(2,128)(2,1)} %param.27) | copy-start | bytes 884740
  3.6 1.7 copy-start.9
  6.1 3.0 copy-start.18
  8.4 0.7 copy-start.15
  9.7 154.8 %copy-start.12 = (s32[1024,2]{0,1:T(2,128)S(1)}, s32[1024,2]{0,1:T(2,128)}, u32[]{:S(2)}) copy-start(s32[1024,2]{0,1:T(2,128)} %copy-done.11) | copy-start | bytes 24580
  9.7 154.8 %copy-start.14 = (s32[2,1,1024,1]{2,3,1,0:T(1,128)S(1)}, s32[2,1,1024,1]{2,3,1,0:T(1,128)}, u32[]{:S(2)}) copy-start(s32[2,1,1024,1]{2,3,1,0:T(1,128)} %param.16) | copy-start | bytes 24580
  9.7 154.8 %copy-start.10 = (s32[1024,1]{0,1:T(1,128)S(1)}, s32[1024,1]{0,1:T(1,128)}, u32[]{:S(2)}) copy-start(s32[1024,1]{0,1:T(1,128)} %copy-done.9) | copy-start | bytes 12292
  165.6 71.9 %copy-start.16 = (s32[512]{0:T(512)S(1)}, s32[512]{0:T(512)}, u32[]{:S(2)}) copy-start(s32[512]{0:T(512)} %copy-done.15) | copy-start | bytes 6148
  238.3 105.9 %copy-start.7 = (f32[48,1536]{1,0:T(8,128)S(1)}, f32[48,1536]{1,0:T(8,128)}, u32[]{:S(2)}) copy-start(f32[48,1536]{1,0:T(8,128)} %get-tuple-element.82) | copy-start | bytes 884740
  344.2 2.4 copy-start.6
  344.2 2.4 copy-start.8
  344.2 3.7 %copy-start.5 = (f32[48,1536]{1,0:T(8,128)S(1)}, f32[48,1536]{1,0:T(8,128)}, u32[]{:S(2)}) copy-start(f32[48,1536]{1,0:T(8,128)} %get-tuple-element.79) | copy-start | bytes 884740
  345.3 3.3 copy-start.17
  347.9 5.2 %copy-start.2 = (f32[2,1,512,768]{3,2,1,0:T(8,128)S(1)}, f32[2,1,512,768]{3,2,1,0:T(8,128)}, u32[]{:S(2)}) copy-start(f32[2,1,512,768]{3,2,1,0:T(8,128)} %get-tuple-element.147) | copy-start | bytes 9437188
  350.4 4.3 %copy-start.1 = (s32[2,1]{0,1:T(1,128)S(1)}, s32[2,1]{0,1:T(1,128)}, u32[]{:S(2)}) copy-start(s32[2,1]{0,1:T(1,128)} %param.17) | copy-start | bytes 28

commit v6 on v5

--- a/solution.py
+++ b/solution.py
@@ -164,10 +164,9 @@
 
 
 link_rate = {"z": 87e3, "y": 87e3, "x": 87e3, "c": 300e3}
-link_delay = 2.0
-
-
-def schedule(chains, room=3, want_ends=False):
+
+
+def schedule(chains, room, link_delay, want_ends=False):
     here = [0] * len(chains)
     begun = [False] * len(chains)
     free = dict.fromkeys(link_rate, 0.0)
@@ -281,21 +280,19 @@
     return phases
 
 
-def parts_of(start, width):
-    tiles = width // TILE
-    small = max(tiles // 6, 1)
-    large = (tiles - small) // 2
-    edges = [start, start + large * TILE, start + (large + small) * TILE, start + width]
-    return [slice(a, b) for a, b in zip(edges, edges[1:])]
+def parts_of(start, width, shares):
+    tiles, whole = width // TILE, sum(shares)
+    cuts = [0, tiles * shares[0] // whole, tiles * (shares[0] + shares[1]) // whole, tiles]
+    return [slice(start + a * TILE, start + b * TILE) for a, b in zip(cuts, cuts[1:])]
 
 
 ORDERS = ("zyx", "xyz", "xzy")
 
 
-def gather_group(wire, full, start, width, rows, rank):
+def gather_group(wire, full, start, width, rows, rank, shares=(5, 2, 5)):
     return [
         (rank, gather_chain(wire, full, at, rows * (at.stop - at.start), order))
-        for at, order in zip(parts_of(start, width), ORDERS)
+        for at, order in zip(parts_of(start, width, shares), ORDERS)
     ]
 
 
@@ -305,7 +302,8 @@
     x = wire.at["x"]
     pair = (None,) * 3 if table is None else (table.at[x], table.at[x], table.at[1 - x])
     chains.append((0, swap_chain(wire, [pair], 4 * 8 * TILE)))
-    chains += gather_group(wire, attn, 0, 4 * cols, rows, 0)
+    chains += gather_group(wire, attn, 0, 3 * cols, rows, 0, (3, 2, 4))
+    chains += gather_group(wire, attn, 3 * cols, cols, rows, 1, (1, 1, 1))
     for rank, src, dst in ((0, tokens, x_all), (3, cotangent, c_all)):
         pairs = [(None, None, None)] * 2
         if src is not None:
@@ -319,7 +317,7 @@
                 )
         chains += [(rank, swap_chain(wire, [pair], 2 * half * depth)) for pair in pairs]
     for n, (full, width) in enumerate(zip(wide, widths)):
-        chains += gather_group(wire, full, 0, width, rows, 1 + n)
+        chains += gather_group(wire, full, 0, width, rows, 2 + n)
     return chains
 
 
@@ -474,7 +472,7 @@
         wire, (attn_all, vec_all, tables, tokens, x_all, cotangent, c_all, *alls),
         rows_per, cols, [shard.shape[1] for shard in shards], half_len, depth,
     )
-    acts, ends = schedule(chains, 3, True)
+    acts, ends = schedule(chains, 4, 4.0, True)
     agenda = Agenda(acts)
     agenda.catch_up(max(end for (rank, _), end in zip(chains, ends) if rank == 0))
 
@@ -502,7 +500,7 @@
         r = lax.rsqrt(jnp.mean(x * x, axis=-1, keepdims=True) + epsilon)
         n = (x * r * vec_sum[0:1, :]).astype(bf16)
         for t in range(2):
-            w = attn_all[:, :, :, t].reshape(depth, 4 * cols)
+            w = attn_all[:, :, :, t, :, 0 : 3 * cols].reshape(depth, 3 * cols)
             at = slice(t * cols, (t + 1) * cols)
             q_ref[rows, at] = mm(n, w[:, :cols]).astype(bf16) * 0.125
             k_ref[rows, at] = mm(n, w[:, cols : 2 * cols]).astype(bf16)
@@ -582,7 +580,7 @@
         rows = pl.ds(pl.multiple_of(i * block, block), block)
         attended = jnp.zeros((block, depth), f32)
         for t in range(2):
-            w = attn_all[:, :, :, t].reshape(depth, 4 * cols)[:, 3 * cols :]
+            w = attn_all[:, :, :, t, :, 3 * cols : 4 * cols].reshape(depth, cols)
             attended = attended + mm_nt(mixed_ref[rows, t * cols : (t + 1) * cols], w)
         res = x_all[rows, :].astype(f32) + attended
         res_ref[rows, :] = res
@@ -601,7 +599,7 @@
         prob_ref[rows, :] = jnp.where(lane == 0, p0, jnp.where(lane == 1, p1, gate))
         low_ref[rows, :] = (gate * c_all[rows, :].astype(f32)).astype(bf16)
 
-    agenda.catch_up(max(end for (rank, chain), end in zip(chains, ends) if rank == 3 and len(chain) == 1))
+    agenda.catch_up(max(end for (rank, chain), end in zip(chains, ends) if rank == 1 or (rank == 3 and len(chain) == 1)))
     agenda.loop(length // block, 3.0, residual)
     step = 320
 
@@ -613,7 +611,7 @@
         gs_ref[pl.ds(at, step), :] = mm(pick, low_ref[...]).astype(bf16)
 
     agenda.loop(slots // step, 2.2, sort)
-    agenda.catch_up(max(end for (rank, _), end in zip(chains, ends) if rank in (1, 2)))
+    agenda.catch_up(max(end for (rank, _), end in zip(chains, ends) if rank in (2, 3)))
     capacity = y_ref.shape[0]
     run_expert(
         agenda, xs_ref.at[0:capacity], gs_ref.at[0:capacity], alls[:2], (d1_all, d2_all), y_ref, gb_ref,
@@ -715,22 +713,24 @@
         return lead + (slice(None), columns)
 
     chain = []
-    for number, (grads, use, earliest) in enumerate(jobs):
+    for number, (grads, base, use, earliest) in enumerate(jobs):
         first, final = number == 0, number == len(jobs) - 1
         phases = []
         incoming, [(sem, credit)] = slots[0]
 
-        def load(grads=grads):
+        theirs = slice(base + columns.start, base + columns.stop)
+
+        def load(grads=grads, theirs=theirs):
             return pltpu.make_async_copy(
-                grads.at[:, :, at["c"], :, :, columns], total.at[:, :, :, :, columns], sem_load
+                grads.at[:, :, at["c"], :, :, theirs], total.at[:, :, :, :, columns], sem_load
             )
 
-        def start(grads=grads, load=load, first=first, incoming=incoming, sem=sem, credit=credit):
+        def start(grads=grads, theirs=theirs, load=load, first=first, incoming=incoming, sem=sem, credit=credit):
             c = at["c"]
             if not wire.closing:
                 load().start()
             wire.send(
-                grads.at[:, :, 1 - c, :, :, columns], incoming, "c", 1 - c, sem,
+                grads.at[:, :, 1 - c, :, :, theirs], incoming, "c", 1 - c, sem,
                 credit=None if first else credit,
             )
 
@@ -799,28 +799,36 @@
                 phases.append((dim, cost, start, finish))
         last = phases[-1]
 
-        def end(last=last, phases=tuple(phases), use=use):
+        def end(last=last, phases=tuple(phases), use=use, theirs=theirs):
             last[3]()
             wire.closing = True
             for phase in phases:
                 phase[2]()
             wire.closing = False
-            use(columns, total[at["z"], at["y"], at["x"], :, columns])
+            use(theirs, total[at["z"], at["y"], at["x"], :, columns])
 
         phases[-1] = last[:3] + (end,) + last[4:]
         chain += phases
     return chain
 
 
-def reduce_groups(wire, jobs, width, rows, local):
+SETS, GROUP = 4, 768
+
+
+def reduce_groups(wire, jobs, rows, local):
     size = wire.size
+    jobs = [
+        (grads, n * GROUP, use, earliest)
+        for grads, use, times in jobs
+        for n, earliest in enumerate(times)
+    ]
     chains = []
-    for half in range(min(2, len(jobs))):
-        total = wire.buffer((size["z"], size["y"], size["x"], rows, width), bf16)
-        for n, (columns, order) in enumerate(zip(parts_of(0, width), ORDERS)):
-            sem = None if local is None else local.at[3 * half + n]
+    for n in range(SETS):
+        total = wire.buffer((size["z"], size["y"], size["x"], rows, GROUP), bf16)
+        for m, (columns, order) in enumerate(zip(parts_of(0, GROUP, (3, 1, 2)), ORDERS)):
+            sem = None if local is None else local.at[3 * n + m]
             chains.append(
-                (half, reduce_chain(wire, jobs[half::2], columns, total, rows, sem, order[::-1]))
+                (n, reduce_chain(wire, jobs[n::SETS], columns, total, rows, sem, order[::-1]))
             )
     return chains
 
@@ -858,8 +866,9 @@
 
         return use
 
-    jobs = [(d1_before, into(d1_own), 0.0), (d2_before, into(d2_own), 0.0)]
-    agenda = Agenda(schedule(reduce_groups(wire, jobs, width, rows_per, local), 3))
+    none = [0.0] * (width // GROUP)
+    jobs = [(d1_before, into(d1_own), none), (d2_before, into(d2_own), none)]
+    agenda = Agenda(schedule(reduce_groups(wire, jobs, rows_per, local), 6, 2.0))
     agenda.catch_up(0.0)
     parts_ref[...] = jnp.zeros_like(parts_ref)
     for copy in tokens_in:
@@ -918,7 +927,7 @@
     cols = attn_w.shape[-1] // 4
     capacity = y0.shape[0]
     draft = Draft(fsdp)
-    reduce_groups(draft, [(None, None, 0.0)] * 2, width, rows, None)
+    reduce_groups(draft, [(None, None, [0.0] * (width // GROUP))] * 2, rows, None)
     return pl.pallas_call(
         functools.partial(middle_kernel, fsdp=fsdp),
         out_shape=[
@@ -937,7 +946,7 @@
         scratch_shapes=[
             pltpu.SemaphoreType.DMA((draft.used,)),
             pltpu.SemaphoreType.DMA((draft.used,)),
-            pltpu.SemaphoreType.DMA((6,)),
+            pltpu.SemaphoreType.DMA((3 * SETS,)),
             pltpu.SemaphoreType.REGULAR((draft.credits,)),
             pltpu.SemaphoreType.DMA((4,)),
             pltpu.VMEM(shape + (rows, cols), bf16),
@@ -957,7 +966,8 @@
 
 def backward_plan(wire, refs, local, rows, width, count, half, depth, late):
     vec, out, out_end, low, low_in, *jobs = refs
-    chains = reduce_groups(wire, jobs or [(None, None, 0.0)] * count, width, rows, local)
+    none = [0.0] * (width // GROUP)
+    chains = reduce_groups(wire, jobs or [(None, None, none)] * count, rows, local)
     phases = gather_chain(wire, vec, slice(None), 2 * 8 * depth, "zyx")
     chains.append((0, [phases[0] + (late,)] + phases[1:]))
     pairs = [(None, None, None)] * 2
@@ -974,11 +984,7 @@
     return chains
 
 
-HEAD, ROWS, WEIGHT = 2.5, 2.6, 1.5
-
-
-def backward_late(heads, length):
-    return heads * HEAD + length // 256 * ROWS + 6 * WEIGHT + 2.0
+TURN, HEAD, ROWS, WEIGHT = 0.8, 2.6, 2.6, 1.5
 
 
 def backward_kernel(*refs, fsdp, wide, heads):
@@ -1033,14 +1039,18 @@
 
         return use
 
-    late = backward_late(heads, length)
-    jobs = [(ref, into(end), 0.0) for ref, end in zip(grads, owns)]
-    jobs.append((dw, into(dw_own), late))
+    turns = length // 256
+    done = turns * TURN + heads * HEAD + 0.05
+    ready = [done + 4 * WEIGHT, done + 6 * WEIGHT]
+    late = ready[1] + turns * ROWS + 1.0
+    none = [0.0] * (width // GROUP)
+    jobs = [(ref, into(end), none) for ref, end in zip(grads, owns)]
+    jobs.append((dw, into(dw_own), ready))
     chains = backward_plan(
         wire, (vec_all, out, out_end, low, low_in, *jobs), local, rows_per, width, len(jobs), half,
         depth, late,
     )
-    agenda = Agenda(schedule(chains, 3))
+    agenda = Agenda(schedule(chains, 6, 3.0))
     agenda.catch_up(0.0)
 
     tiles = length // TILE
@@ -1121,12 +1131,28 @@
             k_ref[:, pair] = hold[1]
             v_ref[:, pair] = hold[2]
 
+    def turn(i):
+        rows = pl.ds(pl.multiple_of(i * block, block), block)
+        x = x_ref[rows, :].astype(f32)
+        r = lax.rsqrt(jnp.mean(x * x, axis=-1, keepdims=True) + epsilon)
+        nt[:, rows] = (x * r * gains_ref[0:1, :]).astype(bf16).T
+
     hold[...] = jnp.zeros_like(hold)
     diag_all[...] = jnp.zeros_like(diag_all)
+    agenda.loop(length // block, TURN, turn)
     agenda.loop(heads, HEAD, attend_back)
     for copy in later:
         copy.wait()
     vec_all[here] = parts_ref[...]
+    for n, ref in enumerate((q_ref, k_ref, v_ref)):
+        for t in range(2):
+            span = slice(t * cols, (t + 1) * cols)
+            agenda.catch_up(agenda.now)
+            d = mm(nt[...], ref[:, span]).astype(bf16)
+            dw[:, :, :, t, :, n * cols : (n + 1) * cols] = d.reshape(
+                dw.shape[:3] + (rows_per, cols)
+            )
+            agenda.now += WEIGHT
 
     def input_grad(i):
         rows = pl.ds(pl.multiple_of(i * block, block), block)
@@ -1139,23 +1165,14 @@
         x = x_ref[rows, :].astype(f32)
         r = lax.rsqrt(jnp.mean(x * x, axis=-1, keepdims=True) + epsilon)
         n1 = x * r
-        nt[:, rows] = (n1 * gains_ref[0:1, :]).astype(bf16).T
         vec_all[here + (slice(0, 1), slice(None))] += jnp.sum(gn * n1, axis=0, keepdims=True)
         g1 = gn * gains_ref[0:1, :]
         gx_ref[rows, :] = gx_ref[rows, :] + r * (
             g1 - n1 * jnp.mean(g1 * n1, axis=-1, keepdims=True)
         )
 
+    agenda.now += 0.1
     agenda.loop(length // block, ROWS, input_grad)
-    for t in range(2):
-        span = slice(t * cols, (t + 1) * cols)
-        for n, ref in enumerate((q_ref, k_ref, v_ref)):
-            agenda.catch_up(agenda.now)
-            d = mm(nt[...], ref[:, span]).astype(bf16)
-            dw[:, :, :, t, :, n * cols : (n + 1) * cols] = d.reshape(
-                dw.shape[:3] + (rows_per, cols)
-            )
-            agenda.now += WEIGHT
     low[...] = gx_ref[other, :].astype(bf16)
     keep = pltpu.make_async_copy(gx_ref.at[own], gx_end.at[x_at, 0], moved.at[0])
     keep.start()
@@ -1210,7 +1227,7 @@
         scratch_shapes=[
             pltpu.SemaphoreType.DMA((draft.used,)),
             pltpu.SemaphoreType.DMA((draft.used,)),
-            pltpu.SemaphoreType.DMA((6,)),
+            pltpu.SemaphoreType.DMA((3 * SETS,)),
             pltpu.SemaphoreType.REGULAR((draft.credits,)),
             pltpu.SemaphoreType.DMA((8,)),
             pltpu.VMEM((half, depth), bf16),

time: 358 us -> 343 us (0.958)
  Pallas kernels: 332 us -> 317 us
    pallas_call x1, Pallas kernels: 155 us -> 139 us  [forward(): pl.pallas_call(functools.partial(forward_kernel, fsdp=fsdp, wide=wide, he...]
where the time goes in v6:
time: 343 us; the launch traced here: 340 us
  Pallas kernels  317 us (92%)
  local copies, waits for them, and re-layouts  16.6 us (5%)
  other arithmetic  4 us (1%)
    pallas_call x1, Pallas kernels, forward(): pl.pallas_call(functools.partial(forward_kernel, fsdp=fsdp, wide=wide, he...  139 us
    pallas_call x1, Pallas kernels, backward(): pl.pallas_call(functools.partial(backward_kernel, fsdp=fsdp, wide=wide, h...  108 us
    pallas_call x1, Pallas kernels, middle(): pl.pallas_call(functools.partial(middle_kernel, fsdp=fsdp), out_shape=[ja...  70.3 us
    unnamed x48, local copies, waits for them, and re-layouts  7.58 us

profile of v6, /device:TPU:0, one launch (start us, length us, event | category | flops | bytes accessed | tf_op | source)
XLA Modules:
  0.0 339.9 jit_solution(5609561820073407597)
XLA Ops:
  0.6 0.0 copy-start
  0.7 0.0 copy-start.13
  0.7 0.0 copy-start.21
  0.7 0.0 copy-start.20
  0.7 0.0 copy-start.19
  0.7 0.0 copy-start.3
  0.7 0.8 constant_dynamic-slice_fusion.1
  1.5 0.8 fusion.4
  2.3 0.0 copy-start.11
  2.3 0.6 copy-done.11
  2.9 0.0 copy-done.13
  2.9 0.0 copy-start.4
  2.9 0.6 fusion.16.refs_10_
  3.6 0.0 copy-start.9
  3.6 1.0 copy.48.refs_9_
  4.6 0.0 copy-done
  4.6 0.6 constant_dynamic-slice_fusion.2
  5.2 0.1 pad.14.clone
  5.3 0.0 copy-done.9
  5.3 0.0 copy-done.21
  5.3 0.0 copy-done.20
  5.3 0.0 copy-done.19
  5.3 0.1 maximum_maximum_fusion
  5.4 0.1 tile.10
  5.5 0.6 broadcast_select_fusion.refs_4_
  6.1 0.0 copy-done.3
  6.1 0.4 fusion.26
  6.5 0.8 copy_bitcast_fusion.1
  7.3 0.0 copy-done.4
  7.3 0.4 fusion.25
  7.7 0.7 copy_bitcast_fusion
  8.4 0.7 fusion.10.refs_11_
  9.1 0.0 copy-done.15
  9.1 0.0 copy-done.18
  9.1 0.6 pad.4.refs_5_
  9.7 139.0 %forward.1 = (bf16[4,2,2,2,48,1536]{5,4,3,2,1,0:T(8,128)(2,1)}, f32[8,768]{1,0:T(8,128)}, bf16[1024,768]{1,0:T(8,128)(2,1)}, bf16[1024,768]{1,0:T(8,128)(2,1)}, ...) custom-call(bf16[48,384]{1,0:T(8,128)(2,1)} %refs_0_.1, ...), custom_call_target="tpu_custom_call" | custom-call | flops 165000003584 | bytes 1024 | tf_op jit(solution)/shard_map/forward/pallas_call | solution.py:639
  148.7 0.0 copy-done.12
  148.8 0.0 copy-done.14
  148.8 0.0 copy-done.10
  148.8 1.0 copy.49.refs_3_
  149.8 70.3 %middle.1 = (bf16[1024,768]{1,0:T(8,128)(2,1)}, f32[1024,768]{1,0:T(8,128)}, bf16[1024,768]{1,0:T(8,128)(2,1)}, bf16[4,2,2,2,48,384]{5,4,3,2,1,0:T(8,128)(2,1)},...) custom-call(bf16[1024,768]{1,0:T(8,128)(2,1)} %get-tuple-element.50., ...), custom_call_target="tpu_custom_call" | custom-call | flops 65999998976 | bytes 1024 | tf_op jit(solution)/shard_map/middle/pallas_call | solution.py:931
  220.2 0.0 copy-done.16
  220.2 0.8 fusion.11.refs_3_
  221.0 108.1 %backward.1 = (f32[48,1536]{1,0:T(8,128)}, f32[8,768]{1,0:T(8,128)}, bf16[2,1,512,768]{3,2,1,0:T(8,128)(2,1)}, f32[2,1,512,768]{3,2,1,0:T(8,128)}, f32[48,1536]{1,0:T(8,128)}, /*index=5*/f32[48,1536]{1,0:T(8,128)}) custom-call(bf16[1024,768]{1,0:T(8,128)(2,1)} %get-tuple-element.48.refs_0_, f32[8,768]{1,0:T(8,128)} %get-tuple-element.49.refs_7_.refs_1_, ...), custom_call_target="tpu_custom_call" | custom-call | flops 165000003584 | bytes 1024 | tf_op jit(solution)/shard_map/backward/pallas_call | solution.py:1216
  329.1 0.0 copy-start.6
  329.1 0.0 copy-start.8
  329.1 0.0 copy-done.7
  329.1 0.0 copy-start.5
  329.2 1.1 pad_maximum_fusion.1
  330.3 1.3 copy.51
  331.5 0.0 copy-done.6
  331.5 0.0 copy-done.8
  331.6 1.3 copy.50
  332.9 0.0 copy-done.5
  332.9 0.7 fusion.24
  333.6 0.0 copy-done.17
  333.6 0.1 constant_dynamic-slice_fusion
  333.7 0.5 slice_bitcast_fusion.1
  334.2 0.6 slice_bitcast_fusion
  334.7 0.6 dynamic-slice_reduce_fusion
  335.4 2.7 copy.62
  338.0 0.0 copy-done.2
  338.0 1.7 copy.63
  339.7 0.0 copy-done.1
  (20 shorter events, 0.1 us)
Async XLA Ops:
  0.6 3.9 %copy-start = (s32[2,1]{0,1:T(1,128)S(1)}, s32[2,1]{0,1:T(1,128)}, u32[]{:S(2)}) copy-start(s32[2,1]{0,1:T(1,128)} %param.17) | copy-start | bytes 28
  0.7 2.3 copy-start.13
  0.7 4.6 %copy-start.21 = (f32[24]{0:T(128)S(1)}, f32[24]{0:T(128)}, u32[]{:S(2)}) copy-start(f32[24]{0:T(128)} %param.18) | copy-start | bytes 292
  0.7 4.6 %copy-start.20 = (f32[24]{0:T(128)S(1)}, f32[24]{0:T(128)}, u32[]{:S(2)}) copy-start(f32[24]{0:T(128)} %param.24) | copy-start | bytes 292
  0.7 4.6 %copy-start.19 = (f32[24,2]{0,1:T(2,128)S(1)}, f32[24,2]{0,1:T(2,128)}, u32[]{:S(2)}) copy-start(f32[24,2]{0,1:T(2,128)} %param.25) | copy-start | bytes 580
  0.7 5.4 %copy-start.3 = (bf16[48,2,1536]{2,1,0:T(2,128)(2,1)S(1)}, bf16[48,2,1536]{2,1,0:T(2,128)(2,1)}, u32[]{:S(2)}) copy-start(bf16[48,2,1536]{2,1,0:T(2,128)(2,1)} %param.26) | copy-start | bytes 884740
  2.3 0.6 copy-start.11
  2.9 4.3 %copy-start.4 = (bf16[48,2,1536]{2,1,0:T(2,128)(2,1)S(1)}, bf16[48,2,1536]{2,1,0:T(2,128)(2,1)}, u32[]{:S(2)}) copy-start(bf16[48,2,1536]{2,1,0:T(2,128)(2,1)} %param.27) | copy-start | bytes 884740
  3.6 1.7 copy-start.9
  6.1 3.0 copy-start.18
  8.4 0.7 copy-start.15
  9.7 139.0 %copy-start.12 = (s32[1024,2]{0,1:T(2,128)S(1)}, s32[1024,2]{0,1:T(2,128)}, u32[]{:S(2)}) copy-start(s32[1024,2]{0,1:T(2,128)} %copy-done.11) | copy-start | bytes 24580
  9.7 139.0 %copy-start.14 = (s32[2,1,1024,1]{2,3,1,0:T(1,128)S(1)}, s32[2,1,1024,1]{2,3,1,0:T(1,128)}, u32[]{:S(2)}) copy-start(s32[2,1,1024,1]{2,3,1,0:T(1,128)} %param.16) | copy-start | bytes 24580
  9.7 139.1 %copy-start.10 = (s32[1024,1]{0,1:T(1,128)S(1)}, s32[1024,1]{0,1:T(1,128)}, u32[]{:S(2)}) copy-start(s32[1024,1]{0,1:T(1,128)} %copy-done.9) | copy-start | bytes 12292
  149.8 70.3 %copy-start.16 = (s32[512]{0:T(512)S(1)}, s32[512]{0:T(512)}, u32[]{:S(2)}) copy-start(s32[512]{0:T(512)} %copy-done.15) | copy-start | bytes 6148
  221.0 108.1 %copy-start.7 = (f32[48,1536]{1,0:T(8,128)S(1)}, f32[48,1536]{1,0:T(8,128)}, u32[]{:S(2)}) copy-start(f32[48,1536]{1,0:T(8,128)} %get-tuple-element.82) | copy-start | bytes 884740
  329.1 2.4 copy-start.6
  329.1 2.4 copy-start.8
  329.1 3.7 %copy-start.5 = (f32[48,1536]{1,0:T(8,128)S(1)}, f32[48,1536]{1,0:T(8,128)}, u32[]{:S(2)}) copy-start(f32[48,1536]{1,0:T(8,128)} %get-tuple-element.79) | copy-start | bytes 884740
  330.3 3.3 copy-start.17
  332.9 5.2 %copy-start.2 = (f32[2,1,512,768]{3,2,1,0:T(8,128)S(1)}, f32[2,1,512,768]{3,2,1,0:T(8,128)}, u32[]{:S(2)}) copy-start(f32[2,1,512,768]{3,2,1,0:T(8,128)} %get-tuple-element.147) | copy-start | bytes 9437188
  335.4 4.3 %copy-start.1 = (s32[2,1]{0,1:T(1,128)S(1)}, s32[2,1]{0,1:T(1,128)}, u32[]{:S(2)}) copy-start(s32[2,1]{0,1:T(1,128)} %param.17) | copy-start | bytes 28

commit v7 on v6

--- a/solution.py
+++ b/solution.py
@@ -163,7 +163,7 @@
                 phase[2]()
 
 
-link_rate = {"z": 87e3, "y": 87e3, "x": 87e3, "c": 300e3}
+link_rate = {"z": 87e3, "y": 87e3, "x": 87e3, "c": 450e3}
 
 
 def schedule(chains, room, link_delay, want_ends=False):

time: 343 us -> 339 us (0.988)
  Pallas kernels: 317 us -> 313 us
where the time goes in v7:
time: 339 us; the launch traced here: 335 us
  Pallas kernels  313 us (92%)
  local copies, waits for them, and re-layouts  16.6 us (5%)
  other arithmetic  4 us (1%)
    pallas_call x1, Pallas kernels, forward(): pl.pallas_call(functools.partial(forward_kernel, fsdp=fsdp, wide=wide, he...  138 us
    pallas_call x1, Pallas kernels, backward(): pl.pallas_call(functools.partial(backward_kernel, fsdp=fsdp, wide=wide, h...  106 us
    pallas_call x1, Pallas kernels, middle(): pl.pallas_call(functools.partial(middle_kernel, fsdp=fsdp), out_shape=[ja...  68.2 us
    unnamed x48, local copies, waits for them, and re-layouts  7.58 us

profile of v7, /device:TPU:0, one launch (start us, length us, event | category | flops | bytes accessed | tf_op | source)
XLA Modules:
  0.0 335.5 jit_solution(18000328973077487647)
XLA Ops:
  0.6 0.0 copy-start
  0.7 0.0 copy-start.13
  0.7 0.0 copy-start.21
  0.7 0.0 copy-start.20
  0.7 0.0 copy-start.19
  0.7 0.0 copy-start.3
  0.7 0.8 constant_dynamic-slice_fusion.1
  1.5 0.8 fusion.4
  2.3 0.0 copy-start.11
  2.3 0.6 copy-done.11
  2.9 0.0 copy-done.13
  2.9 0.0 copy-start.4
  2.9 0.6 fusion.16.refs_10_
  3.6 0.0 copy-start.9
  3.6 1.0 copy.48.refs_9_
  4.6 0.0 copy-done
  4.6 0.6 constant_dynamic-slice_fusion.2
  5.2 0.1 pad.14.clone
  5.3 0.0 copy-done.9
  5.3 0.0 copy-done.21
  5.3 0.0 copy-done.20
  5.3 0.0 copy-done.19
  5.3 0.1 maximum_maximum_fusion
  5.4 0.1 tile.10
  5.5 0.6 broadcast_select_fusion.refs_4_
  6.1 0.0 copy-done.3
  6.1 0.4 fusion.26
  6.5 0.8 copy_bitcast_fusion.1
  7.3 0.0 copy-done.4
  7.3 0.4 fusion.25
  7.7 0.7 copy_bitcast_fusion
  8.4 0.7 fusion.10.refs_11_
  9.1 0.0 copy-done.15
  9.1 0.0 copy-done.18
  9.1 0.6 pad.4.refs_5_
  9.7 138.4 %forward.1 = (bf16[4,2,2,2,48,1536]{5,4,3,2,1,0:T(8,128)(2,1)}, f32[8,768]{1,0:T(8,128)}, bf16[1024,768]{1,0:T(8,128)(2,1)}, bf16[1024,768]{1,0:T(8,128)(2,1)}, ...) custom-call(bf16[48,384]{1,0:T(8,128)(2,1)} %refs_0_.1, ...), custom_call_target="tpu_custom_call" | custom-call | flops 165000003584 | bytes 1024 | tf_op jit(solution)/shard_map/forward/pallas_call | solution.py:639
  148.1 0.0 copy-done.12
  148.1 0.0 copy-done.14
  148.2 0.0 copy-done.10
  148.2 1.0 copy.49.refs_3_
  149.2 68.2 %middle.1 = (bf16[1024,768]{1,0:T(8,128)(2,1)}, f32[1024,768]{1,0:T(8,128)}, bf16[1024,768]{1,0:T(8,128)(2,1)}, bf16[4,2,2,2,48,384]{5,4,3,2,1,0:T(8,128)(2,1)},...) custom-call(bf16[1024,768]{1,0:T(8,128)(2,1)} %get-tuple-element.50., ...), custom_call_target="tpu_custom_call" | custom-call | flops 65999998976 | bytes 1024 | tf_op jit(solution)/shard_map/middle/pallas_call | solution.py:931
  217.4 0.0 copy-done.16
  217.4 0.8 fusion.11.refs_3_
  218.2 106.4 %backward.1 = (f32[48,1536]{1,0:T(8,128)}, f32[8,768]{1,0:T(8,128)}, bf16[2,1,512,768]{3,2,1,0:T(8,128)(2,1)}, f32[2,1,512,768]{3,2,1,0:T(8,128)}, f32[48,1536]{1,0:T(8,128)}, /*index=5*/f32[48,1536]{1,0:T(8,128)}) custom-call(bf16[1024,768]{1,0:T(8,128)(2,1)} %get-tuple-element.48.refs_0_, f32[8,768]{1,0:T(8,128)} %get-tuple-element.49.refs_7_.refs_1_, ...), custom_call_target="tpu_custom_call" | custom-call | flops 165000003584 | bytes 1024 | tf_op jit(solution)/shard_map/backward/pallas_call | solution.py:1216
  324.7 0.0 copy-start.6
  324.7 0.0 copy-start.8
  324.7 0.0 copy-done.7
  324.7 0.0 copy-start.5
  324.7 1.1 pad_maximum_fusion.1
  325.9 1.3 copy.51
  327.1 0.0 copy-done.6
  327.1 0.0 copy-done.8
  327.2 1.3 copy.50
  328.5 0.0 copy-done.5
  328.5 0.7 fusion.24
  329.2 0.0 copy-done.17
  329.2 0.1 constant_dynamic-slice_fusion
  329.2 0.5 slice_bitcast_fusion.1
  329.8 0.6 slice_bitcast_fusion
  330.3 0.6 dynamic-slice_reduce_fusion
  330.9 2.7 copy.62
  333.6 0.0 copy-done.2
  333.6 1.7 copy.63
  335.3 0.0 copy-done.1
  (20 shorter events, 0.1 us)
Async XLA Ops:
  0.6 3.9 %copy-start = (s32[2,1]{0,1:T(1,128)S(1)}, s32[2,1]{0,1:T(1,128)}, u32[]{:S(2)}) copy-start(s32[2,1]{0,1:T(1,128)} %param.17) | copy-start | bytes 28
  0.7 2.3 copy-start.13
  0.7 4.6 %copy-start.21 = (f32[24]{0:T(128)S(1)}, f32[24]{0:T(128)}, u32[]{:S(2)}) copy-start(f32[24]{0:T(128)} %param.18) | copy-start | bytes 292
  0.7 4.6 %copy-start.20 = (f32[24]{0:T(128)S(1)}, f32[24]{0:T(128)}, u32[]{:S(2)}) copy-start(f32[24]{0:T(128)} %param.24) | copy-start | bytes 292
  0.7 4.6 %copy-start.19 = (f32[24,2]{0,1:T(2,128)S(1)}, f32[24,2]{0,1:T(2,128)}, u32[]{:S(2)}) copy-start(f32[24,2]{0,1:T(2,128)} %param.25) | copy-start | bytes 580
  0.7 5.4 %copy-start.3 = (bf16[48,2,1536]{2,1,0:T(2,128)(2,1)S(1)}, bf16[48,2,1536]{2,1,0:T(2,128)(2,1)}, u32[]{:S(2)}) copy-start(bf16[48,2,1536]{2,1,0:T(2,128)(2,1)} %param.26) | copy-start | bytes 884740
  2.3 0.6 copy-start.11
  2.9 4.3 %copy-start.4 = (bf16[48,2,1536]{2,1,0:T(2,128)(2,1)S(1)}, bf16[48,2,1536]{2,1,0:T(2,128)(2,1)}, u32[]{:S(2)}) copy-start(bf16[48,2,1536]{2,1,0:T(2,128)(2,1)} %param.27) | copy-start | bytes 884740
  3.6 1.7 copy-start.9
  6.1 3.0 copy-start.18
  8.4 0.7 copy-start.15
  9.7 138.4 %copy-start.12 = (s32[1024,2]{0,1:T(2,128)S(1)}, s32[1024,2]{0,1:T(2,128)}, u32[]{:S(2)}) copy-start(s32[1024,2]{0,1:T(2,128)} %copy-done.11) | copy-start | bytes 24580
  9.7 138.4 %copy-start.14 = (s32[2,1,1024,1]{2,3,1,0:T(1,128)S(1)}, s32[2,1,1024,1]{2,3,1,0:T(1,128)}, u32[]{:S(2)}) copy-start(s32[2,1,1024,1]{2,3,1,0:T(1,128)} %param.16) | copy-start | bytes 24580
  9.7 138.4 %copy-start.10 = (s32[1024,1]{0,1:T(1,128)S(1)}, s32[1024,1]{0,1:T(1,128)}, u32[]{:S(2)}) copy-start(s32[1024,1]{0,1:T(1,128)} %copy-done.9) | copy-start | bytes 12292
  149.2 68.2 %copy-start.16 = (s32[512]{0:T(512)S(1)}, s32[512]{0:T(512)}, u32[]{:S(2)}) copy-start(s32[512]{0:T(512)} %copy-done.15) | copy-start | bytes 6148
  218.2 106.5 %copy-start.7 = (f32[48,1536]{1,0:T(8,128)S(1)}, f32[48,1536]{1,0:T(8,128)}, u32[]{:S(2)}) copy-start(f32[48,1536]{1,0:T(8,128)} %get-tuple-element.82) | copy-start | bytes 884740
  324.7 2.4 copy-start.6
  324.7 2.4 copy-start.8
  324.7 3.7 %copy-start.5 = (f32[48,1536]{1,0:T(8,128)S(1)}, f32[48,1536]{1,0:T(8,128)}, u32[]{:S(2)}) copy-start(f32[48,1536]{1,0:T(8,128)} %get-tuple-element.79) | copy-start | bytes 884740
  325.9 3.3 copy-start.17
  328.5 5.2 %copy-start.2 = (f32[2,1,512,768]{3,2,1,0:T(8,128)S(1)}, f32[2,1,512,768]{3,2,1,0:T(8,128)}, u32[]{:S(2)}) copy-start(f32[2,1,512,768]{3,2,1,0:T(8,128)} %get-tuple-element.147) | copy-start | bytes 9437188
  330.9 4.3 %copy-start.1 = (s32[2,1]{0,1:T(1,128)S(1)}, s32[2,1]{0,1:T(1,128)}, u32[]{:S(2)}) copy-start(s32[2,1]{0,1:T(1,128)} %param.17) | copy-start | bytes 28

commit v8 on v7

--- a/solution.py
+++ b/solution.py
@@ -1050,7 +1050,7 @@
         wire, (vec_all, out, out_end, low, low_in, *jobs), local, rows_per, width, len(jobs), half,
         depth, late,
     )
-    agenda = Agenda(schedule(chains, 6, 3.0))
+    agenda = Agenda(schedule(chains, 6, 5.0))
     agenda.catch_up(0.0)
 
     tiles = length // TILE

time: 339 us -> 338 us (level)
  no operation moved by 1% of the time
where the time goes in v8:
time: 338 us; the launch traced here: 335 us
  Pallas kernels  313 us (93%)
  local copies, waits for them, and re-layouts  16.6 us (5%)
  other arithmetic  4 us (1%)
    pallas_call x1, Pallas kernels, forward(): pl.pallas_call(functools.partial(forward_kernel, fsdp=fsdp, wide=wide, he...  138 us
    pallas_call x1, Pallas kernels, backward(): pl.pallas_call(functools.partial(backward_kernel, fsdp=fsdp, wide=wide, h...  106 us
    pallas_call x1, Pallas kernels, middle(): pl.pallas_call(functools.partial(middle_kernel, fsdp=fsdp), out_shape=[ja...  68.2 us
    unnamed x48, local copies, waits for them, and re-layouts  7.58 us

profile of v8, /device:TPU:0, one launch (start us, length us, event | category | flops | bytes accessed | tf_op | source)
XLA Modules:
  0.0 335.2 jit_solution(15692712740923494383)
XLA Ops:
  0.6 0.0 copy-start
  0.7 0.0 copy-start.13
  0.7 0.0 copy-start.21
  0.7 0.0 copy-start.20
  0.7 0.0 copy-start.19
  0.7 0.0 copy-start.3
  0.7 0.8 constant_dynamic-slice_fusion.1
  1.5 0.8 fusion.4
  2.3 0.0 copy-start.11
  2.3 0.6 copy-done.11
  2.9 0.0 copy-done.13
  2.9 0.0 copy-start.4
  2.9 0.6 fusion.16.refs_10_
  3.6 0.0 copy-start.9
  3.6 1.0 copy.48.refs_9_
  4.6 0.0 copy-done
  4.6 0.6 constant_dynamic-slice_fusion.2
  5.2 0.1 pad.14.clone
  5.3 0.0 copy-done.9
  5.3 0.0 copy-done.21
  5.3 0.0 copy-done.20
  5.3 0.0 copy-done.19
  5.3 0.1 maximum_maximum_fusion
  5.4 0.1 tile.10
  5.5 0.6 broadcast_select_fusion.refs_4_
  6.1 0.0 copy-done.3
  6.1 0.4 fusion.26
  6.5 0.8 copy_bitcast_fusion.1
  7.3 0.0 copy-done.4
  7.3 0.4 fusion.25
  7.7 0.7 copy_bitcast_fusion
  8.4 0.7 fusion.10.refs_11_
  9.1 0.0 copy-done.15
  9.1 0.0 copy-done.18
  9.1 0.6 pad.4.refs_5_
  9.7 138.4 %forward.1 = (bf16[4,2,2,2,48,1536]{5,4,3,2,1,0:T(8,128)(2,1)}, f32[8,768]{1,0:T(8,128)}, bf16[1024,768]{1,0:T(8,128)(2,1)}, bf16[1024,768]{1,0:T(8,128)(2,1)}, ...) custom-call(bf16[48,384]{1,0:T(8,128)(2,1)} %refs_0_.1, ...), custom_call_target="tpu_custom_call" | custom-call | flops 165000003584 | bytes 1024 | tf_op jit(solution)/shard_map/forward/pallas_call | solution.py:639
  148.1 0.0 copy-done.12
  148.1 0.0 copy-done.14
  148.2 0.0 copy-done.10
  148.2 1.0 copy.49.refs_3_
  149.2 68.2 %middle.1 = (bf16[1024,768]{1,0:T(8,128)(2,1)}, f32[1024,768]{1,0:T(8,128)}, bf16[1024,768]{1,0:T(8,128)(2,1)}, bf16[4,2,2,2,48,384]{5,4,3,2,1,0:T(8,128)(2,1)},...) custom-call(bf16[1024,768]{1,0:T(8,128)(2,1)} %get-tuple-element.50., ...), custom_call_target="tpu_custom_call" | custom-call | flops 65999998976 | bytes 1024 | tf_op jit(solution)/shard_map/middle/pallas_call | solution.py:931
  217.4 0.0 copy-done.16
  217.4 0.8 fusion.11.refs_3_
  218.2 106.1 %backward.1 = (f32[48,1536]{1,0:T(8,128)}, f32[8,768]{1,0:T(8,128)}, bf16[2,1,512,768]{3,2,1,0:T(8,128)(2,1)}, f32[2,1,512,768]{3,2,1,0:T(8,128)}, f32[48,1536]{1,0:T(8,128)}, /*index=5*/f32[48,1536]{1,0:T(8,128)}) custom-call(bf16[1024,768]{1,0:T(8,128)(2,1)} %get-tuple-element.48.refs_0_, f32[8,768]{1,0:T(8,128)} %get-tuple-element.49.refs_7_.refs_1_, ...), custom_call_target="tpu_custom_call" | custom-call | flops 165000003584 | bytes 1024 | tf_op jit(solution)/shard_map/backward/pallas_call | solution.py:1216
  324.4 0.0 copy-start.6
  324.4 0.0 copy-start.8
  324.4 0.0 copy-done.7
  324.4 0.0 copy-start.5
  324.4 1.1 pad_maximum_fusion.1
  325.5 1.3 copy.51
  326.8 0.0 copy-done.6
  326.8 0.0 copy-done.8
  326.9 1.3 copy.50
  328.1 0.0 copy-done.5
  328.1 0.7 fusion.24
  328.9 0.0 copy-done.17
  328.9 0.1 constant_dynamic-slice_fusion
  328.9 0.5 slice_bitcast_fusion.1
  329.5 0.6 slice_bitcast_fusion
  330.0 0.6 dynamic-slice_reduce_fusion
  330.6 2.7 copy.62
  333.3 0.0 copy-done.2
  333.3 1.7 copy.63
  335.0 0.0 copy-done.1
  (20 shorter events, 0.1 us)
Async XLA Ops:
  0.6 3.9 %copy-start = (s32[2,1]{0,1:T(1,128)S(1)}, s32[2,1]{0,1:T(1,128)}, u32[]{:S(2)}) copy-start(s32[2,1]{0,1:T(1,128)} %param.17) | copy-start | bytes 28
  0.7 2.3 copy-start.13
  0.7 4.6 %copy-start.21 = (f32[24]{0:T(128)S(1)}, f32[24]{0:T(128)}, u32[]{:S(2)}) copy-start(f32[24]{0:T(128)} %param.18) | copy-start | bytes 292
  0.7 4.6 %copy-start.20 = (f32[24]{0:T(128)S(1)}, f32[24]{0:T(128)}, u32[]{:S(2)}) copy-start(f32[24]{0:T(128)} %param.24) | copy-start | bytes 292
  0.7 4.6 %copy-start.19 = (f32[24,2]{0,1:T(2,128)S(1)}, f32[24,2]{0,1:T(2,128)}, u32[]{:S(2)}) copy-start(f32[24,2]{0,1:T(2,128)} %param.25) | copy-start | bytes 580
  0.7 5.4 %copy-start.3 = (bf16[48,2,1536]{2,1,0:T(2,128)(2,1)S(1)}, bf16[48,2,1536]{2,1,0:T(2,128)(2,1)}, u32[]{:S(2)}) copy-start(bf16[48,2,1536]{2,1,0:T(2,128)(2,1)} %param.26) | copy-start | bytes 884740
  2.3 0.6 copy-start.11
  2.9 4.3 %copy-start.4 = (bf16[48,2,1536]{2,1,0:T(2,128)(2,1)S(1)}, bf16[48,2,1536]{2,1,0:T(2,128)(2,1)}, u32[]{:S(2)}) copy-start(bf16[48,2,1536]{2,1,0:T(2,128)(2,1)} %param.27) | copy-start | bytes 884740
  3.6 1.7 copy-start.9
  6.1 3.0 copy-start.18
  8.4 0.7 copy-start.15
  9.7 138.4 %copy-start.12 = (s32[1024,2]{0,1:T(2,128)S(1)}, s32[1024,2]{0,1:T(2,128)}, u32[]{:S(2)}) copy-start(s32[1024,2]{0,1:T(2,128)} %copy-done.11) | copy-start | bytes 24580
  9.7 138.4 %copy-start.14 = (s32[2,1,1024,1]{2,3,1,0:T(1,128)S(1)}, s32[2,1,1024,1]{2,3,1,0:T(1,128)}, u32[]{:S(2)}) copy-start(s32[2,1,1024,1]{2,3,1,0:T(1,128)} %param.16) | copy-start | bytes 24580
  9.7 138.4 %copy-start.10 = (s32[1024,1]{0,1:T(1,128)S(1)}, s32[1024,1]{0,1:T(1,128)}, u32[]{:S(2)}) copy-start(s32[1024,1]{0,1:T(1,128)} %copy-done.9) | copy-start | bytes 12292
  149.2 68.2 %copy-start.16 = (s32[512]{0:T(512)S(1)}, s32[512]{0:T(512)}, u32[]{:S(2)}) copy-start(s32[512]{0:T(512)} %copy-done.15) | copy-start | bytes 6148
  218.2 106.2 %copy-start.7 = (f32[48,1536]{1,0:T(8,128)S(1)}, f32[48,1536]{1,0:T(8,128)}, u32[]{:S(2)}) copy-start(f32[48,1536]{1,0:T(8,128)} %get-tuple-element.82) | copy-start | bytes 884740
  324.4 2.4 copy-start.6
  324.4 2.4 copy-start.8
  324.4 3.7 %copy-start.5 = (f32[48,1536]{1,0:T(8,128)S(1)}, f32[48,1536]{1,0:T(8,128)}, u32[]{:S(2)}) copy-start(f32[48,1536]{1,0:T(8,128)} %get-tuple-element.79) | copy-start | bytes 884740
  325.5 3.3 copy-start.17
  328.1 5.2 %copy-start.2 = (f32[2,1,512,768]{3,2,1,0:T(8,128)S(1)}, f32[2,1,512,768]{3,2,1,0:T(8,128)}, u32[]{:S(2)}) copy-start(f32[2,1,512,768]{3,2,1,0:T(8,128)} %get-tuple-element.147) | copy-start | bytes 9437188
  330.6 4.3 %copy-start.1 = (s32[2,1]{0,1:T(1,128)S(1)}, s32[2,1]{0,1:T(1,128)}, u32[]{:S(2)}) copy-start(s32[2,1]{0,1:T(1,128)} %param.17) | copy-start | bytes 28
